TPU v7x, 32 devices: a whole 2x2x4 slice. The times are simulated.
32 devices in a mesh: gz: 4 (over y, x), gy: 8 (over z, core).
Axes of the slice: x: 2, y: 2, z: 4, core: 2. Of those that a mesh axis runs over, the one named last changes fastest.
Arguments:
- source: bfloat16 [12, 24, 128, 128], P('gz', 'gy'), may hold values from -6 to 6
- target: bfloat16 [12, 24, 128, 128], P('gz', 'gy'), may hold values from -6 to 6
- hidden: bfloat16 [12, 24, 96, 128], P('gz', 'gy'), may hold values from -1 to 1
- motion: float32 [12, 24, 3, 128], P('gz', 'gy'), may hold values from -6 to 6
- w_corr: bfloat16 [96, 343], replicated, may hold values from -0.3125 to 0.3125
- w_motion: float32 [96, 3], replicated, may hold values from -3.5 to 3.5
- bias_encoder: float32 [96], replicated, may hold values from -3 to 3
- w_update: bfloat16 [27, 18432], replicated, may hold values from -0.078125 to 0.078125
- bias_update: float32 [96], replicated, may hold values from -4 to 4
- w_reset: bfloat16 [27, 18432], replicated, may hold values from -0.078125 to 0.078125
- bias_reset: float32 [96], replicated, may hold values from -4 to 4
- w_cand: bfloat16 [27, 18432], replicated, may hold values from -0.078125 to 0.078125
- bias_cand: float32 [96], replicated, may hold values from -3 to 3
- w_head: bfloat16 [27, 3, 96], replicated, may hold values from -0.125 to 0.125
- bias_head: float32 [3], replicated, may hold values from -3 to 3
Outputs:
- state_out: bfloat16 [12, 24, 96, 128], P('gz', 'gy')
- motion_out: float32 [12, 24, 3, 128], P('gz', 'gy')
All inputs are finite; a program needn't handle non-finite values.
Results may differ from a plain program's by a relative error of at most 0.0046.
Values may be sent and summed in bfloat16 or wider, within the bound.
No kernel may reach another device: no remote copies, remote signals or barrier semaphores. Data moves between devices by JAX's collectives and lax.ppermute only.
A program may use at most 64 MiB of HBM per device.

v0:
```python
import functools

import jax
import jax.numpy as jnp
from jax import lax
from jax.experimental import pallas as pl
from jax.experimental.pallas import tpu as pltpu
from jax.sharding import PartitionSpec as P

F32 = jnp.float32
BF16 = jnp.bfloat16
LANES = 128
MIB = 1024 * 1024


def around(block, axis, step):
    count = lax.axis_size(axis)
    return lax.ppermute(block, axis, [(i, (i + step) % count) for i in range(count)])


def planes_around(first, last):
    return around(last, "gz", 1), around(first, "gz", -1)


def rows_around(to_mate, to_other):
    count = lax.axis_size("gy")
    mate = lax.ppermute(to_mate, "gy", [(i, i ^ 1) for i in range(count)])
    other = lax.ppermute(to_other, "gy", [(i, ((i + 1) ^ 1) - 1) for i in range(1, count - 1)])
    return mate, other


def edges(block, width):
    rows = block.shape[1]
    if rows == width:
        return block, block
    odd = lax.axis_index("gy") % 2
    to_mate = lax.dynamic_slice_in_dim(block, (rows - width) * (1 - odd), width, axis=1)
    return to_mate, lax.dynamic_slice_in_dim(block, (rows - width) * odd, width, axis=1)


def inside():
    z, y = lax.axis_index("gz"), lax.axis_index("gy")
    odd = y % 2
    end = jnp.where(odd == 1, lax.axis_size("gy") - 1, 0)
    return jnp.stack([z > 0, z < lax.axis_size("gz") - 1, y != end, odd == 1]).astype(jnp.int32)


def vmem(count):
    return [pl.BlockSpec(memory_space=pltpu.VMEM)] * count


def call(body, out_shape, scratch, args, name, mib, place=None, from_hbm=(), kept=True):
    struct = lambda o: isinstance(o, jax.ShapeDtypeStruct)
    in_specs = vmem(len(args))
    for n, given in enumerate(from_hbm):
        in_specs[n] = pl.BlockSpec(memory_space=given)
    args = [pltpu.with_memory_space_constraint(a, pltpu.HBM if n < len(from_hbm) else pltpu.VMEM) for n, a in enumerate(args)]
    if place is not None:
        args = [place] + args
        in_specs = [pl.BlockSpec(memory_space=pltpu.SMEM)] + in_specs
    return pl.pallas_call(
        body,
        out_shape=jax.tree.map(lambda o: pltpu.VMEM(o.shape, o.dtype) if kept and struct(o) else o, out_shape),
        in_specs=in_specs,
        out_specs=jax.tree.map(lambda _: pl.BlockSpec(memory_space=pltpu.VMEM), out_shape),
        scratch_shapes=scratch,
        compiler_params=pltpu.CompilerParams(vmem_limit_bytes=mib * MIB),
        cost_estimate=pl.CostEstimate(flops=1000, bytes_accessed=1000, transcendentals=0),
        name=name,
    )(*args)


def lay_out(width, weight, first_out, last_out, flat, wide):
    pieces = width * 2 * width // LANES
    half = width // 2
    lane = lax.broadcasted_iota(jnp.int32, (half, LANES), 1)

    def turn(value, by):
        return pltpu.roll(value, by, 1)

    def packed(parts):
        made = []
        for first in range(0, 9, 4):
            group = parts[first : first + 4]
            if len(group) == 1:
                made.append(jnp.where(lane < 96, group[0], 0.0))
                continue
            one, two = turn(group[1], 96), turn(group[2], 64)
            made.append(jnp.where(lane < 96, group[0], one))
            made.append(jnp.where(lane < 64, one, two))
            made.append(jnp.where(lane < 32, two, turn(group[3], 32)))
        return made

    def spread(j, carry):
        got = weight[:, pl.ds(pl.multiple_of(j * LANES, LANES), LANES)].astype(F32)
        for first in range(0, 27, 8):
            size = min(8, 27 - first)
            flat[pl.ds(j + first * pieces, size, stride=pieces), :] = got[first : first + size]
        return carry

    lax.fori_loop(0, pieces, spread, 0, unroll=4)

    for c in range(3):
        rows = [[], [], [], []]
        for ab in range(9):
            first, mid, last = [flat[pl.ds((ab * 3 + c) * pieces + k, half, stride=3), :] for k in range(3)]
            rows[0].append(first)
            rows[1].append(turn(jnp.where(lane < 64, last, mid), 64))
            rows[2].append(turn(jnp.where(lane >= 96, first, mid), 32))
            rows[3].append(turn(last, 96))
        for part in range(4):
            for k, chunk in enumerate(packed(rows[part])):
                wide[part // 2, k, pl.ds(c * width + part % 2, half, stride=2), :] = chunk
    for part, out in enumerate((first_out, last_out)):
        for chunk in range(7):
            out[:, chunk * LANES : (chunk + 1) * LANES] = wide[part, chunk].astype(BF16)


def lay_out_scratch(width):
    return [pltpu.VMEM((27 * width * 2 * width // LANES, LANES), F32), pltpu.VMEM((2, 7, 3 * width, LANES), F32)]


def update_body(weight, first_out, last_out, flat, wide):
    lay_out(first_out.shape[0] // 3, weight, first_out, last_out, flat, wide)


def cand_body(weight, head, first_out, last_out, head_out, flat, wide, eights):
    width = head.shape[2]
    lay_out(width, weight, first_out, last_out, flat, wide)
    eights[...] = jnp.zeros_like(eights)
    for o in range(head.shape[0]):
        eights[pl.ds(o, 27, stride=8), :width] = head[o].astype(F32)
    head_out[...] = eights[:, :width].astype(BF16)


def corr_part(held, source, tt, s_flat, corr, wc):
    planes_out, rows_out, channels, _ = source.shape
    wide = rows_out * LANES
    scale = channels ** (-0.5)
    for z in range(planes_out):
        for y in range(rows_out):
            s_flat[z, :, y * LANES : (y + 1) * LANES] = source[z, y]
    sub = lax.broadcasted_iota(jnp.int32, (8, LANES), 0)
    cell = lax.broadcasted_iota(jnp.int32, (8, LANES), 1)
    block_of = (cell + 4 - sub + 8) // 8 - 1
    turn = (3 - lax.broadcasted_iota(jnp.int32, (1, 8, LANES), 2)) & 7
    turn = jnp.concatenate([turn] * rows_out, axis=2)

    results = []
    for z in range(planes_out):
        filled = set()
        for j in range(rows_out + 6):
            ys = [y for y in range(rows_out) if 0 <= j - y <= 6]
            lo, hi = ys[0] * LANES, (ys[-1] + 1) * LANES
            for first, last in held(j):
                first, last = max(z, first), min(z + 7, last)
                if first >= last:
                    continue
                lhs = tt[j, first:last].reshape((last - first) * LANES, channels)
                prod = jnp.dot(lhs, s_flat[z, :, lo:hi], preferred_element_type=F32)
                for plane in range(first, last):
                    for n, y in enumerate(ys):
                        got = jnp.zeros((8, LANES), F32)
                        for k in range(LANES // 8):
                            at = (plane - first) * LANES + 8 * k
                            piece = prod[at : at + 8, n * LANES : (n + 1) * LANES]
                            got = jnp.where(block_of == k, piece, got)
                        corr[(plane - z) * 7 + j - y, :, y * LANES : (y + 1) * LANES] = got
                        filled.add(((plane - z) * 7 + j - y, y))
        for pair in range(49):
            for y in range(rows_out):
                if (pair, y) not in filled:
                    corr[pair, :, y * LANES : (y + 1) * LANES] = jnp.zeros((8, LANES), F32)
        got = corr[...]
        for bit in (1, 2, 4):
            got = jnp.where((turn & bit) != 0, pltpu.roll(got, bit, 1), got)
        got = (got * scale).reshape(49 * 8, wide).astype(BF16)
        results.append(jnp.dot(wc[...], got, preferred_element_type=F32))
    return results


def put_block(tt, block, ok, row, plane):
    def store(value):
        for p in range(block.shape[0]):
            for y in range(block.shape[1]):
                tt[row + y, plane + p] = value(p, y)

    if ok is None:
        store(lambda p, y: block[p, y].T)
        return

    @pl.when(ok)
    def _():
        store(lambda p, y: block[p, y].T)

    @pl.when(jnp.logical_not(ok))
    def _():
        store(lambda p, y: jnp.zeros(tt.shape[2:], BF16))


def column(row):
    return jnp.broadcast_to(row, (LANES, row.shape[1])).T


def own_body(
    w_reset, w_update, source, own, w_corr, hidden,
    out, wc, h_first, h_last, re_old, re_new, update_here, tt, s_flat, corr, reset_here, flat, wide, arrived
):
    copies = [
        pltpu.make_async_copy(w_reset, reset_here, arrived.at[0]),
        pltpu.make_async_copy(w_update, update_here, arrived.at[1]),
    ]
    for copy in copies:
        copy.start()
    planes, rows = source.shape[:2]
    h_first[...] = hidden[:2]
    h_last[...] = hidden[planes - 2 :]
    at = lax.broadcasted_iota(jnp.int32, (w_corr.shape[1], 49 * 8), 0)
    to = lax.broadcasted_iota(jnp.int32, (w_corr.shape[1], 49 * 8), 1)
    pick = ((to & 7) < 7) & (at == (to >> 3) * 7 + (to & 7))
    wc[...] = jnp.dot(w_corr[...], jnp.where(pick, 1.0, 0.0).astype(BF16), preferred_element_type=F32).astype(BF16)
    put_block(tt, own, None, 3, 3)
    held = lambda j: [(3, 3 + planes)] if 3 <= j < 3 + rows else []
    for z, got in enumerate(corr_part(held, source, tt, s_flat, corr, wc)):
        out[z] = got
    copies[0].wait()
    lay_out(hidden.shape[2], reset_here, re_old, re_new, flat, wide)
    copies[1].wait()


def corr_face_body(place, source, before, low, high, mate, other, wc, out, tt, s_flat, corr):
    planes, rows = source.shape[:2]
    odd = place[3]
    put_block(tt, low, place[0] == 1, 3, 0)
    put_block(tt, high, place[1] == 1, 3, 3 + planes)
    put_block(tt, mate, None, (3 + rows) * (1 - odd), 3)
    put_block(tt, other, place[2] == 1, (3 + rows) * odd, 3)

    def held(j):
        return [(3, 3 + planes)] if j < 3 or j >= 3 + rows else [(0, 3), (3 + planes, 6 + planes)]

    for z, got in enumerate(corr_part(held, source, tt, s_flat, corr, wc)):
        out[z] = before[z] + got


def corr_corner_body(
    place, source, motion, w_motion, bias, before, low_mate, low_other, high_mate, high_other, wc,
    enc, enc_first, enc_last, tt, s_flat, corr
):
    planes, rows = source.shape[:2]
    odd = place[3]
    mate_at, other_at = (3 + rows) * (1 - odd), (3 + rows) * odd
    put_block(tt, low_mate, place[0] == 1, mate_at, 0)
    put_block(tt, low_other, place[0] + place[2] == 2, other_at, 0)
    put_block(tt, high_mate, place[1] == 1, mate_at, 3 + planes)
    put_block(tt, high_other, place[1] + place[2] == 2, other_at, 3 + planes)
    held = lambda j: [(0, 3), (3 + planes, 6 + planes)] if j < 3 or j >= 3 + rows else []
    shift = column(bias[...])
    moves = [column(w_motion[k : k + 1, :]) for k in range(w_motion.shape[0])]
    for z, got in enumerate(corr_part(held, source, tt, s_flat, corr, wc)):
        for y in range(rows):
            at = slice(y * LANES, (y + 1) * LANES)
            total = got[:, at] + before[z, :, at]
            for k, move in enumerate(moves):
                total = total + move * motion[z, y, k : k + 1, :]
            value = jnp.maximum(total + shift, 0.0).astype(BF16)
            enc[z, y] = value
            if z < 2:
                enc_first[z, y] = value
            if z >= planes - 2:
                enc_last[z - planes + 2, y] = value


def pack_body(place, own, low, high, to_mate, to_other):
    width = to_mate.shape[1]
    planes, rows = own.shape[:2]
    odd = place[3]
    for y in range(width):
        mate_at, other_at = (rows - width) * (1 - odd) + y, (rows - width) * odd + y
        first = 0
        for block in (low, own, high):
            to_mate[first : first + block.shape[0], y] = block[:, mate_at]
            to_other[first : first + block.shape[0], y] = block[:, other_at]
            first += block.shape[0]


def rows_of(place, low, own, high, width, name, from_hbm=()):
    planes = low.shape[0] + own.shape[0] + high.shape[0]
    out = jax.ShapeDtypeStruct((planes, width) + own.shape[2:], own.dtype)
    return call(pack_body, (out, out), [], (own, low, high), name, 6, place, from_hbm)


def taps(field, z, row, rows):
    wide = rows * LANES
    got = []
    for a in range(3):
        for b in range(3):
            got.append(field[z + a, :, (row + b) * LANES : (row + b) * LANES + wide])
    return got + [jnp.zeros((32, wide), BF16)]


def conv(weight, rhs, rows):
    three = jnp.dot(weight, jnp.concatenate(rhs, axis=0), preferred_element_type=F32)
    width = three.shape[0] // 3
    cell = lax.broadcasted_iota(jnp.int32, (width, LANES), 1)
    out = []
    for y in range(rows):
        at = slice(y * LANES, (y + 1) * LANES)
        before = jnp.where(cell == 0, 0.0, pltpu.roll(three[:width, at], 1, 1))
        after = jnp.where(cell == LANES - 1, 0.0, pltpu.roll(three[2 * width :, at], LANES - 1, 1))
        out.append(three[width : 2 * width, at] + before + after)
    return out


def fill(place, field, own, z0, z1, mate, other):
    planes, rows, width = own.shape[:3]
    odd = place[3]

    def store(plane, y, value):
        at = y * LANES if isinstance(y, int) else pl.multiple_of(y * LANES, LANES)
        field[plane, :, pl.ds(at, LANES)] = value

    def store_if(ok, plane, y, value):
        @pl.when(ok)
        def _():
            store(plane, y, value())

        @pl.when(jnp.logical_not(ok))
        def _():
            store(plane, y, jnp.zeros((width, LANES), BF16))

    for plane in range(planes + 4):
        in_z = None
        if plane < 2:
            in_z = place[0]
        elif plane >= planes + 2:
            in_z = place[1]
        for y in range(rows):
            if plane < 2:
                store_if(in_z == 1, plane, y + 2, lambda: z0[plane, y])
            elif plane >= planes + 2:
                store_if(in_z == 1, plane, y + 2, lambda: z1[plane - planes - 2, y])
            else:
                store(plane, y + 2, own[plane - 2, y])
        for y in range(2):
            mate_at, other_at = y + (rows + 2) * (1 - odd), y + (rows + 2) * odd
            if in_z is None:
                store(plane, mate_at, mate[plane, y])
                store_if(place[2] == 1, plane, other_at, lambda: other[plane, y])
            else:
                store_if(in_z == 1, plane, mate_at, lambda: mate[plane, y])
                store_if(in_z + place[2] == 2, plane, other_at, lambda: other[plane, y])


def old_body(place, hidden, b_up, b_re, hz0, hz1, h_mate, h_other, a_up, a_re, update_out, reset_out, near_out, field):
    planes, rows = hidden.shape[:2]
    fill(place, field, hidden, hz0, hz1, h_mate, h_other)
    up_shift, re_shift = column(b_up[...]), column(b_re[...])

    def reset_plane(z, carry):
        near_out[z] = field[z + 1, :, LANES : (rows + 3) * LANES]
        for y, got in enumerate(conv(a_re[...], taps(field, z, 0, rows + 2), rows + 2)):
            reset_out[z, y] = got + re_shift
        return carry

    lax.fori_loop(0, planes + 2, reset_plane, 0)

    def update_plane(z, carry):
        for y, got in enumerate(conv(a_up[...], taps(field, z + 1, 1, rows), rows)):
            update_out[z, y] = got + up_shift
        return carry

    lax.fori_loop(0, planes, update_plane, 0)


def gru_body(
    place, hidden, b_ca, near, update_old, reset_old, enc, ez0, ez1, e_mate, e_other, a_up, a_re, a_ca_old, a_ca_new,
    head, state_out, part_low, part_out, part_high, field, gated, state
):
    planes, rows = hidden.shape[:2]
    fill(place, field, enc, ez0, ez1, e_mate, e_other)
    ca_shift = column(b_ca[...])

    def reset_plane(z, carry):
        for y, got in enumerate(conv(a_re[...], taps(field, z, 0, rows + 2), rows + 2)):
            at = slice(y * LANES, (y + 1) * LANES)
            gate = jax.nn.sigmoid(got + reset_old[z, y])
            gated[z, :, at] = (gate * near[z, :, at].astype(F32)).astype(BF16)
        return carry

    lax.fori_loop(0, planes + 2, reset_plane, 0)

    def state_plane(z, carry):
        new_taps = taps(field, z + 1, 1, rows)
        update = conv(a_up[...], new_taps, rows)
        both = jnp.concatenate([a_ca_old[...], a_ca_new[...]], axis=1)
        cand = conv(both, taps(gated, z, 0, rows) + new_taps, rows)
        for y in range(rows):
            gate = jax.nn.sigmoid(update[y] + update_old[z, y])
            new = jnp.tanh(cand[y] + ca_shift)
            old = hidden[z, y].astype(F32)
            got = ((1.0 - gate) * old + gate * new).astype(BF16)
            state_out[z, y] = got
            state[z, :, y * LANES : (y + 1) * LANES] = got
        return carry

    lax.fori_loop(0, planes, state_plane, 0)

    cell = lax.broadcasted_iota(jnp.int32, (8, LANES), 1)
    sums = {}
    for z in range(planes):
        prod = jnp.dot(head[...], state[z], preferred_element_type=F32)
        for y in range(rows):
            for a in range(3):
                for b in range(3):
                    key = (z + 2 - a, y + 2 - b)
                    for c in range(3):
                        t = a * 9 + b * 3 + c
                        piece = prod[t * 8 : t * 8 + 8, y * LANES : (y + 1) * LANES]
                        slot = sums.setdefault(key, [None] * 3)
                        slot[c] = piece if slot[c] is None else slot[c] + piece
    for (z, y), (before, same, after) in sums.items():
        before = jnp.where(cell == 0, 0.0, pltpu.roll(before, 1, 1))
        after = jnp.where(cell == LANES - 1, 0.0, pltpu.roll(after, LANES - 1, 1))
        total = same + before + after
        if z == 0:
            part_low[0, y] = total
        elif z == planes + 1:
            part_high[0, y] = total
        else:
            part_out[z - 1, y] = total


def mix_body(place, part, low, high, mine, to_mate, to_other):
    planes, rows = mine.shape[:2]
    odd = place[3]
    mate_at, other_at = (rows + 1) * (1 - odd), (rows + 1) * odd

    def added(z, at):
        total = part[z, at]
        if z == 0:
            total = total + jnp.where(place[0] == 1, low[0, at], 0.0)
        if z == planes - 1:
            total = total + jnp.where(place[1] == 1, high[0, at], 0.0)
        return total

    for z in range(planes):
        for y in range(rows):
            mine[z, y] = added(z, y + 1)
        to_mate[z, 0] = added(z, mate_at)
        to_other[z, 0] = added(z, other_at)


def last_body(place, motion, bias, mine, mate, other, out):
    planes, rows, outs = out.shape[:3]
    odd = place[3]
    shift = column(bias[...])
    for z in range(planes):
        for y in range(rows):
            out[z, y] = motion[z, y] + mine[z, y, :outs] + shift
        mate_at, other_at = (rows - 1) * (1 - odd), (rows - 1) * odd
        out[z, mate_at] = out[z, mate_at] + mate[z, 0, :outs]

        @pl.when(place[2] == 1)
        def _():
            out[z, other_at] = out[z, other_at] + other[z, 0, :outs]


def on_device(
    source, target, hidden, motion, w_corr, w_motion, bias_encoder, w_update, bias_update,
    w_reset, bias_reset, w_cand, bias_cand, w_head, bias_head
):
    planes, rows, channels, cells = source.shape
    width = hidden.shape[2]
    wide = rows * LANES
    place = inside()

    t_low, t_high = planes_around(target[:3], target[-3:])
    t_mate, t_other = rows_around(*edges(target, 3))

    scratch = [
        pltpu.VMEM((rows + 6, planes + 6, LANES, channels), BF16),
        pltpu.VMEM((planes, channels, wide), BF16),
        pltpu.VMEM((49, 8, wide), F32),
    ]
    sums = jax.ShapeDtypeStruct((planes, width, wide), F32)
    two = jax.ShapeDtypeStruct((2, rows, width, cells), BF16)
    laid = pltpu.HBM((3 * width, 7 * LANES), BF16)
    own, wc, h_first, h_last, re_old, re_new, update_here = call(
        own_body,
        (sums, jax.ShapeDtypeStruct((width, 49 * 8), BF16), two, two, laid, laid)
        + (jax.ShapeDtypeStruct(w_update.shape, BF16),),
        scratch + [pltpu.VMEM(w_reset.shape, BF16)] + lay_out_scratch(width) + [pltpu.SemaphoreType.DMA((2,))],
        (w_reset, w_update, source, target, w_corr, hidden),
        "own",
        20,
        from_hbm=(pltpu.HBM,) * 2 + (pltpu.VMEM,) * 4,
    )
    t_low, own = lax.optimization_barrier((t_low, own))
    t_low_mate, t_low_other = rows_around(*edges(t_low, 3))
    update_here, t_low = lax.optimization_barrier((update_here, t_low))
    up_old, up_new = call(
        update_body, (laid, laid), lay_out_scratch(width), (update_here,), "lay_out_update", 12
    )
    t_high, up_new = lax.optimization_barrier((t_high, up_new))
    t_high_mate, t_high_other = rows_around(*edges(t_high, 3))
    h_first, h_last, t_low, t_high = lax.optimization_barrier((h_first, h_last, t_low, t_high))
    h_low, h_high = planes_around(h_first, h_last)
    face = call(
        corr_face_body, sums, scratch, (source, own, t_low, t_high, t_mate, t_other, wc), "face", 12, place,
        from_hbm=(pltpu.VMEM,),
    )
    enc, enc_first, enc_last = call(
        corr_corner_body,
        (jax.ShapeDtypeStruct((planes, rows, width, cells), BF16), two, two),
        scratch,
        (source, motion, w_motion.T, bias_encoder[None, :])
        + (face, t_low_mate, t_low_other, t_high_mate, t_high_other, wc),
        "corner",
        12,
        place,
        from_hbm=(pltpu.VMEM,) * 4,
    )
    e_low, e_high = planes_around(enc_first, enc_last)
    taps_head, enc = lax.optimization_barrier((jnp.transpose(w_head, (1, 0, 2)), enc))
    ca_old, ca_new, head = call(
        cand_body,
        (laid, laid, pltpu.HBM((27 * 8, width), BF16)),
        lay_out_scratch(width) + [pltpu.VMEM((27 * 8, LANES), F32)],
        (w_cand, taps_head),
        "lay_out_cand",
        12,
        from_hbm=(pltpu.VMEM,) * 2,
    )
    e_low, ca_new = lax.optimization_barrier((e_low, ca_new))
    h_low, h_high, enc = lax.optimization_barrier((h_low, h_high, enc))
    h_mate, h_other = rows_around(*rows_of(place, h_low, hidden, h_high, 2, "pack_hidden", (pltpu.VMEM,)))
    field = pltpu.VMEM((planes + 4, width, (rows + 4) * LANES), BF16)
    update_old, reset_old, near = call(
        old_body,
        (
            jax.ShapeDtypeStruct((planes, rows, width, cells), F32),
            jax.ShapeDtypeStruct((planes + 2, rows + 2, width, cells), F32),
            jax.ShapeDtypeStruct((planes + 2, width, (rows + 2) * LANES), BF16),
        ),
        [field],
        (hidden, bias_update[None, :], bias_reset[None, :], h_low, h_high, h_mate, h_other, up_old, re_old),
        "old",
        12,
        place,
        from_hbm=(pltpu.VMEM,) * 3,
    )
    e_mate, e_other = rows_around(*rows_of(place, e_low, enc, e_high, 2, "pack_encoded"))

    ring = lambda n: jax.ShapeDtypeStruct((n, rows + 2, 8, cells), F32)
    state_out, part_low, part, part_high = call(
        gru_body,
        (jax.ShapeDtypeStruct((planes, rows, width, cells), BF16), ring(1), ring(planes), ring(1)),
        [
            field,
            pltpu.VMEM((planes + 2, width, (rows + 2) * LANES), BF16),
            pltpu.VMEM((planes, width, wide), BF16),
        ],
        (hidden, bias_cand[None, :], near, update_old, reset_old, enc, e_low, e_high, e_mate, e_other)
        + (up_new, re_new, ca_old, ca_new, head),
        "gru",
        14,
        place,
        from_hbm=(pltpu.VMEM,) * 2,
        kept=False,
    )
    low, high = planes_around(part_low, part_high)
    row = jax.ShapeDtypeStruct((planes, 1, 8, cells), F32)
    mine, to_mate, to_other = call(
        mix_body,
        (jax.ShapeDtypeStruct((planes, rows, 8, cells), F32), row, row),
        [],
        (part, low, high),
        "mix",
        4,
        place,
    )
    mate, other = rows_around(to_mate, to_other)
    motion_out = call(
        last_body,
        jax.ShapeDtypeStruct(motion.shape, F32),
        [],
        (motion, bias_head[None, :], mine, mate, other),
        "last",
        4,
        place,
        from_hbm=(pltpu.VMEM,) * 2,
        kept=False,
    )
    return state_out, motion_out


def solution(mesh):
    split = P("gz", "gy", None, None)
    return jax.shard_map(
        on_device,
        mesh=mesh,
        in_specs=(split,) * 4 + (P(),) * 11,
        out_specs=(split, split),
        check_vma=False,
    )
```

profile of v0, /device:TPU:11, one launch (start us, length us, event | category | flops | bytes accessed | tf_op | source)
XLA Modules:
  0.0 77.8 jit_solution(16289129783576830113)
XLA Ops:
  0.6 1.3 %collective-permute-start = (bf16[3,3,128,128]{3,2,1,0:T(8,128)(2,1)}, bf16[3,3,128,128]{3,2,1,0:T(8,128)(2,1)S(1)}, u32[]{:S(2)}, u32[]{:S(2)}) collective-permute-start(bf16[3,3,128,128]{3,2,1,0:T(8,128)(2,1)} %own.4), channel_id=1, source_target_pairs={{0,8},{8,16},{16,24},{24,0},{1,9},{9,17},{17,25},{25,1},{2,10},{10... | collective-permute-start | bytes 884744 | tf_op jit(solution)/shard_map/ppermute | solution.py:18
  1.9 0.3 collective-permute-start.1
  2.1 4.3 %collective-permute-start.5 = (bf16[3,3,128,128]{3,2,1,0:T(8,128)(2,1)}, bf16[3,3,128,128]{3,2,1,0:T(8,128)(2,1)S(1)}, u32[]{:S(2)}, u32[]{:S(2)}) collective-permute-start(bf16[3,3,128,128]{3,2,1,0:T(8,128)(2,1)} %own.4), channel_id=1, source_target_pairs={{1,2},{2,1},{3,4},{4,3},{5,6},{6,5},{9,10},{10,9},{11,12},{12,11},... | collective-permute-start | bytes 884744 | tf_op jit(solution)/shard_map/ppermute | solution.py:28
  6.5 0.1 collective-permute-start.4
  6.5 5.8 %own.3 = (f32[3,96,384]{2,1,0:T(8,128)S(1)}, bf16[96,392]{1,0:T(8,128)(2,1)S(1)}, bf16[2,3,96,128]{3,2,1,0:T(8,128)(2,1)S(1)}, bf16[2,3,96,128]{3,2,1,0:T(8,128)...) custom-call(bf16[27,18432]{1,0:T(8,128)(2,1)} %w_reset.1, ...), custom_call_target="tpu_custom_call" | custom-call | flops 1000 | bytes 1000 | tf_op jit(solution)/shard_map/own/pallas_call | solution.py:61
  12.4 0.0 collective-permute-done.low
  12.4 3.6 %collective-permute-start.7 = (bf16[3,3,128,128]{3,2,1,0:T(8,128)(2,1)S(1)}, bf16[3,3,128,128]{3,2,1,0:T(8,128)(2,1)S(1)}, u32[]{:S(2)}, u32[]{:S(2)}) collective-permute-start(bf16[3,3,128,128]{3,2,1,0:T(8,128)(2,1)S(1)} %collective-permute-done.low), channel_id=1, source_target_pairs={{1,2},{2,1},{3,4},{4,3},{5,6},{6,5},{9,10},{10,9},{11,12},{12,11},... | collective-permute-start | bytes 884744 | tf_op jit(solution)/shard_map/ppermute | solution.py:28
  16.0 0.1 collective-permute-start.6
  16.1 3.1 %lay_out_update.1 = (bf16[288,896]{1,0:T(8,128)(2,1)}, bf16[288,896]{1,0:T(8,128)(2,1)}) custom-call(bf16[27,18432]{1,0:T(8,128)(2,1)S(1)} %get-tuple-element.54.weight), custom_call_target="tpu_custom_call" | custom-call | flops 1000 | bytes 1000 | tf_op jit(solution)/shard_map/lay_out_update/pallas_call | solution.py:61
  19.2 0.0 collective-permute-done.1.high
  19.2 2.1 %collective-permute-start.9 = (bf16[3,3,128,128]{3,2,1,0:T(8,128)(2,1)S(1)}, bf16[3,3,128,128]{3,2,1,0:T(8,128)(2,1)S(1)}, u32[]{:S(2)}, u32[]{:S(2)}) collective-permute-start(bf16[3,3,128,128]{3,2,1,0:T(8,128)(2,1)S(1)} %collective-permute-done.1.high), channel_id=1, source_target_pairs={{1,2},{2,1},{3,4},{4,3},{5,6},{6,5},{9,10},{10,9},{11,12},{12,11},... | collective-permute-start | bytes 884744 | tf_op jit(solution)/shard_map/ppermute | solution.py:28
  21.3 0.0 collective-permute-done.5.other
  21.3 0.4 collective-permute-start.8
  21.7 0.1 add_convert_fusion.place
  21.8 0.0 collective-permute-done.4.mate
  21.8 2.1 %collective-permute-start.2 = (bf16[2,3,96,128]{3,2,1,0:T(8,128)(2,1)S(1)}, bf16[2,3,96,128]{3,2,1,0:T(8,128)(2,1)S(1)}, u32[]{:S(2)}, u32[]{:S(2)}) collective-permute-start(bf16[2,3,96,128]{3,2,1,0:T(8,128)(2,1)S(1)} %get-tuple-element.57), channel_id=1, source_target_pairs={{0,8},{8,16},{16,24},{24,0},{1,9},{9,17},{17,25},{25,1},{2,10},{10... | collective-permute-start | bytes 442376 | tf_op jit(solution)/shard_map/ppermute | solution.py:18
  23.9 0.0 collective-permute-done.7.low_other
  23.9 0.0 collective-permute-start.3
  23.9 4.1 %face.1.before = f32[3,96,384]{2,1,0:T(8,128)S(1)} custom-call(s32[4]{0:T(128)S(1)} %add_convert_fusion.place, bf16[3,3,128,128]{3,2,1,0:T(8,128)(2,1)} %source.5, f32[3,96,384]{2,1,0:T(8,128)S(1)} %get-tuple-element.59.before, bf16[3,3,128,128]{3,2,1,0:T(8,128)(2,1)S(1)} %collective-permute-done.low, ...), custom_call_target="tpu_custom_call" | custom-call | flops 1000 | bytes 1000 | tf_op jit(solution)/shard_map/face/pallas_call | solution.py:61
  28.0 0.0 collective-permute-done.6.low_mate
  28.0 0.0 collective-permute-done.9.high_other
  28.0 0.0 collective-permute-done.8.high_mate
  28.0 3.6 %corner.1 = (bf16[3,3,96,128]{3,2,1,0:T(8,128)(2,1)S(1)}, bf16[2,3,96,128]{3,2,1,0:T(8,128)(2,1)S(1)}, bf16[2,3,96,128]{3,2,1,0:T(8,128)(2,1)S(1)}) custom-call(s32[4]{0:T(128)S(1)} %add_convert_fusion.place, bf16[3,3,128,128]{3,2,1,0:T(8,128)(2,1)} %source.5, f32[3,3,3,128]{3,2,1,0:T(4,128)} %motion.3, f32[3,96]{1,0:T(4,128)} %bitcast.12, ...), custom_call_target="tpu_custom_call" | custom-call | flops 1000 | bytes 1000 | tf_op jit(solution)/shard_map/corner/pallas_call | solution.py:61
  31.6 0.0 copy-start.2
  31.6 0.0 copy-start.3
  31.6 2.4 %collective-permute-start.12 = (bf16[2,3,96,128]{3,2,1,0:T(8,128)(2,1)S(1)}, bf16[2,3,96,128]{3,2,1,0:T(8,128)(2,1)S(1)}, u32[]{:S(2)}, u32[]{:S(2)}) collective-permute-start(bf16[2,3,96,128]{3,2,1,0:T(8,128)(2,1)S(1)} %get-tuple-element.75), channel_id=1, source_target_pairs={{0,8},{8,16},{16,24},{24,0},{1,9},{9,17},{17,25},{25,1},{2,10},{10... | collective-permute-start | bytes 442376 | tf_op jit(solution)/shard_map/ppermute | solution.py:18
  34.0 0.0 collective-permute-start.13
  34.0 0.0 collective-permute-done.2.low.hz0
  34.0 0.0 collective-permute-done.3.high.hz1
  34.0 1.0 %pack_hidden.1 = (bf16[7,2,96,128]{3,2,1,0:T(8,128)(2,1)S(1)}, bf16[7,2,96,128]{3,2,1,0:T(8,128)(2,1)S(1)}) custom-call(s32[4]{0:T(128)S(1)} %add_convert_fusion.place, bf16[3,3,96,128]{3,2,1,0:T(8,128)(2,1)} %hidden.5, bf16[2,3,96,128]{3,2,1,0:T(8,128)(2,1)S(1)} %collective-permute-done.2.low.hz0, bf16[2,3,96,128]{3,2,1,0:T(8,128)(2,1)S(1)} %collective-permute-done.3.high.hz1), custom_call_target="tpu_custom_call" | custom-call | flops 1000 | bytes 1000 | tf_op jit(solution)/shard_map/pack_hidden/pallas_call | solution.py:61
  35.1 1.1 %collective-permute-start.10 = (bf16[7,2,96,128]{3,2,1,0:T(8,128)(2,1)S(1)}, bf16[7,2,96,128]{3,2,1,0:T(8,128)(2,1)S(1)}, u32[]{:S(2)}, u32[]{:S(2)}) collective-permute-start(bf16[7,2,96,128]{3,2,1,0:T(8,128)(2,1)S(1)} %get-tuple-element.67), channel_id=1, source_target_pairs={{0,1},{1,0},{2,3},{3,2},{4,5},{5,4},{6,7},{7,6},{8,9},{9,8},{10,11... | collective-permute-start | bytes 1032200 | tf_op jit(solution)/shard_map/ppermute | solution.py:27
  36.1 3.0 %collective-permute-start.11 = (bf16[7,2,96,128]{3,2,1,0:T(8,128)(2,1)S(1)}, bf16[7,2,96,128]{3,2,1,0:T(8,128)(2,1)S(1)}, u32[]{:S(2)}, u32[]{:S(2)}) collective-permute-start(bf16[7,2,96,128]{3,2,1,0:T(8,128)(2,1)S(1)} %get-tuple-element.68), channel_id=1, source_target_pairs={{1,2},{2,1},{3,4},{4,3},{5,6},{6,5},{9,10},{10,9},{11,12},{12,11},... | collective-permute-start | bytes 1032200 | tf_op jit(solution)/shard_map/ppermute | solution.py:28
  39.1 4.3 %lay_out_cand.1 = (bf16[288,896]{1,0:T(8,128)(2,1)}, bf16[288,896]{1,0:T(8,128)(2,1)}, bf16[216,96]{1,0:T(8,128)(2,1)}) custom-call(bf16[27,18432]{1,0:T(8,128)(2,1)} %weight.1, bf16[3,27,96]{2,1,0:T(8,128)(2,1)} %bitcast.11), custom_call_target="tpu_custom_call" | custom-call | flops 1000 | bytes 1000 | tf_op jit(solution)/shard_map/lay_out_cand/pallas_call | solution.py:61
  43.4 0.0 collective-permute-done.12.low.ez0
  43.4 0.0 collective-permute-done.13.high.ez1
  43.4 0.6 pack_encoded.1
  44.0 0.0 copy-start
  44.0 0.0 copy-start.1
  44.0 0.0 copy-start.4
  44.0 0.0 copy-start.5
  44.0 0.0 copy-start.6
  44.1 0.8 collective-permute-start.14
  44.8 2.0 %collective-permute-start.15 = (bf16[7,2,96,128]{3,2,1,0:T(8,128)(2,1)S(1)}, bf16[7,2,96,128]{3,2,1,0:T(8,128)(2,1)S(1)}, u32[]{:S(2)}, u32[]{:S(2)}) collective-permute-start(bf16[7,2,96,128]{3,2,1,0:T(8,128)(2,1)S(1)} %get-tuple-element.81), channel_id=1, source_target_pairs={{1,2},{2,1},{3,4},{4,3},{5,6},{6,5},{9,10},{10,9},{11,12},{12,11},... | collective-permute-start | bytes 1032200 | tf_op jit(solution)/shard_map/ppermute | solution.py:28
  46.9 0.0 collective-permute-done.10.h_mate
  46.9 0.0 collective-permute-done.11.h_other
  46.9 6.8 %old.1 = (f32[3,3,96,128]{3,2,1,0:T(8,128)S(1)}, f32[5,5,96,128]{3,2,1,0:T(8,128)S(1)}, bf16[5,96,640]{2,1,0:T(8,128)(2,1)S(1)}) custom-call(s32[4]{0:T(128)S(1)} %add_convert_fusion.place, bf16[3,3,96,128]{3,2,1,0:T(8,128)(2,1)} %hidden.5, f32[1,96]{1,0:T(1,128)} %bitcast.14, f32[1,96]{1,0:T(1,128)} %bitcast.15, ...), custom_call_target="tpu_custom_call" | custom-call | flops 1000 | bytes 1000 | tf_op jit(solution)/shard_map/old/pallas_call | solution.py:61
  53.7 0.0 collective-permute-done.14.e_mate
  53.7 0.0 collective-permute-done.15.e_other
  53.8 0.0 copy-done
  53.8 0.0 copy-done.1
  53.8 0.0 copy-done.4
  53.8 0.0 copy-done.5
  53.8 0.0 copy-done.6
  53.8 9.3 %gru.1 = (bf16[3,3,96,128]{3,2,1,0:T(8,128)(2,1)}, f32[1,5,8,128]{3,2,1,0:T(8,128)S(1)}, f32[3,5,8,128]{3,2,1,0:T(8,128)S(1)}, f32[1,5,8,128]{3,2,1,0:T(8,128)S(1)}) custom-call(s32[4]{0:T(128)S(1)} %add_convert_fusion.place, bf16[3,3,96,128]{3,2,1,0:T(8,128)(2,1)} %hidden.5, f32[1,96]{1,0:T(1,128)} %bitcast.16, ...), custom_call_target="tpu_custom_call" | custom-call | flops 1000 | bytes 1000 | tf_op jit(solution)/shard_map/gru/pallas_call | solution.py:61
  63.1 2.6 %collective-permute-start.16 = (f32[1,5,8,128]{3,2,1,0:T(8,128)S(1)}, f32[1,5,8,128]{3,2,1,0:T(8,128)S(1)}, u32[]{:S(2)}, u32[]{:S(2)}) collective-permute-start(f32[1,5,8,128]{3,2,1,0:T(8,128)S(1)} %get-tuple-element.89), channel_id=1, source_target_pairs={{0,8},{8,16},{16,24},{24,0},{1,9},{9,17},{17,25},{25,1},{2,10},{10... | collective-permute-start | bytes 61448 | tf_op jit(solution)/shard_map/ppermute | solution.py:18
  65.7 0.0 collective-permute-start.17
  65.7 0.9 %collective-permute-done.16.low = f32[1,5,8,128]{3,2,1,0:T(8,128)S(1)} collective-permute-done((f32[1,5,8,128]{3,2,1,0:T(8,128)S(1)}, f32[1,5,8,128]{3,2,1,0:T(8,128)S(1)}, u32[]{:S(2)}, u32[]{:S(2)}) %collective-permute-start.16) | collective-permute-done | bytes 20512 | tf_op jit(solution)/shard_map/ppermute | solution.py:18
  66.6 2.6 %collective-permute-done.17.high = f32[1,5,8,128]{3,2,1,0:T(8,128)S(1)} collective-permute-done((f32[1,5,8,128]{3,2,1,0:T(8,128)S(1)}, f32[1,5,8,128]{3,2,1,0:T(8,128)S(1)}, u32[]{:S(2)}, u32[]{:S(2)}) %collective-permute-start.17) | collective-permute-done | bytes 20512 | tf_op jit(solution)/shard_map/ppermute | solution.py:18
  69.2 0.6 mix.1
  69.8 1.5 %collective-permute-start.18 = (f32[3,1,8,128]{3,2,1,0:T(8,128)S(1)}, f32[3,1,8,128]{3,2,1,0:T(8,128)S(1)}, u32[]{:S(2)}, u32[]{:S(2)}) collective-permute-start(f32[3,1,8,128]{3,2,1,0:T(8,128)S(1)} %get-tuple-element.92), channel_id=1, source_target_pairs={{0,1},{1,0},{2,3},{3,2},{4,5},{5,4},{6,7},{7,6},{8,9},{9,8},{10,11... | collective-permute-start | bytes 36872 | tf_op jit(solution)/shard_map/ppermute | solution.py:27
  71.3 3.5 %collective-permute-start.19 = (f32[3,1,8,128]{3,2,1,0:T(8,128)S(1)}, f32[3,1,8,128]{3,2,1,0:T(8,128)S(1)}, u32[]{:S(2)}, u32[]{:S(2)}) collective-permute-start(f32[3,1,8,128]{3,2,1,0:T(8,128)S(1)} %get-tuple-element.93), channel_id=1, source_target_pairs={{1,2},{2,1},{3,4},{4,3},{5,6},{6,5},{9,10},{10,9},{11,12},{12,11},... | collective-permute-start | bytes 36872 | tf_op jit(solution)/shard_map/ppermute | solution.py:28
  74.8 0.0 collective-permute-done.18.mate
  74.8 1.5 %collective-permute-done.19.other = f32[3,1,8,128]{3,2,1,0:T(8,128)S(1)} collective-permute-done((f32[3,1,8,128]{3,2,1,0:T(8,128)S(1)}, f32[3,1,8,128]{3,2,1,0:T(8,128)S(1)}, u32[]{:S(2)}, u32[]{:S(2)}) %collective-permute-start.19) | collective-permute-done | bytes 12320 | tf_op jit(solution)/shard_map/ppermute | solution.py:28
  76.3 1.4 %last.1 = f32[3,3,3,128]{3,2,1,0:T(4,128)} custom-call(s32[4]{0:T(128)S(1)} %add_convert_fusion.place, f32[3,3,3,128]{3,2,1,0:T(4,128)} %motion.3, f32[1,3]{1,0:T(1,128)} %bitcast.17, f32[3,3,8,128]{3,2,1,0:T(8,128)S(1)} %get-tuple-element.91.mine, f32[3,1,8,128]{3,2,1,0:T(8,128)S(1)} %collective-permute-done.18.mate, ...), custom_call_target="tpu_custom_call" | custom-call | flops 1000 | bytes 1000 | tf_op jit(solution)/shard_map/last/pallas_call | solution.py:61
  (2 shorter events, 0.0 us)
Async XLA Ops:
  0.6 11.8 %collective-permute-start = (bf16[3,3,128,128]{3,2,1,0:T(8,128)(2,1)}, bf16[3,3,128,128]{3,2,1,0:T(8,128)(2,1)S(1)}, u32[]{:S(2)}, u32[]{:S(2)}) collective-permute-start(bf16[3,3,128,128]{3,2,1,0:T(8,128)(2,1)} %own.4), channel_id=1, source_target_pairs={{0,8},{8,16},{16,24},{24,0},{1,9},{9,17},{17,25},{25,1},{2,10},{10... | collective-permute-start | bytes 884744 | tf_op jit(solution)/shard_map/ppermute | solution.py:18
  1.9 17.3 %collective-permute-start.1 = (bf16[3,3,128,128]{3,2,1,0:T(8,128)(2,1)}, bf16[3,3,128,128]{3,2,1,0:T(8,128)(2,1)S(1)}, u32[]{:S(2)}, u32[]{:S(2)}) collective-permute-start(bf16[3,3,128,128]{3,2,1,0:T(8,128)(2,1)} %own.4), channel_id=1, source_target_pairs={{0,24},{8,0},{16,8},{24,16},{1,25},{9,1},{17,9},{25,17},{2,26},{10... | collective-permute-start | bytes 884744 | tf_op jit(solution)/shard_map/ppermute | solution.py:18
  2.1 19.1 %collective-permute-start.5 = (bf16[3,3,128,128]{3,2,1,0:T(8,128)(2,1)}, bf16[3,3,128,128]{3,2,1,0:T(8,128)(2,1)S(1)}, u32[]{:S(2)}, u32[]{:S(2)}) collective-permute-start(bf16[3,3,128,128]{3,2,1,0:T(8,128)(2,1)} %own.4), channel_id=1, source_target_pairs={{1,2},{2,1},{3,4},{4,3},{5,6},{6,5},{9,10},{10,9},{11,12},{12,11},... | collective-permute-start | bytes 884744 | tf_op jit(solution)/shard_map/ppermute | solution.py:28
  6.5 15.3 %collective-permute-start.4 = (bf16[3,3,128,128]{3,2,1,0:T(8,128)(2,1)}, bf16[3,3,128,128]{3,2,1,0:T(8,128)(2,1)S(1)}, u32[]{:S(2)}, u32[]{:S(2)}) collective-permute-start(bf16[3,3,128,128]{3,2,1,0:T(8,128)(2,1)} %own.4), channel_id=1, source_target_pairs={{0,1},{1,0},{2,3},{3,2},{4,5},{5,4},{6,7},{7,6},{8,9},{9,8},{10,11... | collective-permute-start | bytes 884744 | tf_op jit(solution)/shard_map/ppermute | solution.py:27
  12.4 11.5 %collective-permute-start.7 = (bf16[3,3,128,128]{3,2,1,0:T(8,128)(2,1)S(1)}, bf16[3,3,128,128]{3,2,1,0:T(8,128)(2,1)S(1)}, u32[]{:S(2)}, u32[]{:S(2)}) collective-permute-start(bf16[3,3,128,128]{3,2,1,0:T(8,128)(2,1)S(1)} %collective-permute-done.low), channel_id=1, source_target_pairs={{1,2},{2,1},{3,4},{4,3},{5,6},{6,5},{9,10},{10,9},{11,12},{12,11},... | collective-permute-start | bytes 884744 | tf_op jit(solution)/shard_map/ppermute | solution.py:28
  16.0 12.0 %collective-permute-start.6 = (bf16[3,3,128,128]{3,2,1,0:T(8,128)(2,1)S(1)}, bf16[3,3,128,128]{3,2,1,0:T(8,128)(2,1)S(1)}, u32[]{:S(2)}, u32[]{:S(2)}) collective-permute-start(bf16[3,3,128,128]{3,2,1,0:T(8,128)(2,1)S(1)} %collective-permute-done.low), channel_id=1, source_target_pairs={{0,1},{1,0},{2,3},{3,2},{4,5},{5,4},{6,7},{7,6},{8,9},{9,8},{10,11... | collective-permute-start | bytes 884744 | tf_op jit(solution)/shard_map/ppermute | solution.py:27
  19.2 8.8 %collective-permute-start.9 = (bf16[3,3,128,128]{3,2,1,0:T(8,128)(2,1)S(1)}, bf16[3,3,128,128]{3,2,1,0:T(8,128)(2,1)S(1)}, u32[]{:S(2)}, u32[]{:S(2)}) collective-permute-start(bf16[3,3,128,128]{3,2,1,0:T(8,128)(2,1)S(1)} %collective-permute-done.1.high), channel_id=1, source_target_pairs={{1,2},{2,1},{3,4},{4,3},{5,6},{6,5},{9,10},{10,9},{11,12},{12,11},... | collective-permute-start | bytes 884744 | tf_op jit(solution)/shard_map/ppermute | solution.py:28
  21.3 6.7 %collective-permute-start.8 = (bf16[3,3,128,128]{3,2,1,0:T(8,128)(2,1)S(1)}, bf16[3,3,128,128]{3,2,1,0:T(8,128)(2,1)S(1)}, u32[]{:S(2)}, u32[]{:S(2)}) collective-permute-start(bf16[3,3,128,128]{3,2,1,0:T(8,128)(2,1)S(1)} %collective-permute-done.1.high), channel_id=1, source_target_pairs={{0,1},{1,0},{2,3},{3,2},{4,5},{5,4},{6,7},{7,6},{8,9},{9,8},{10,11... | collective-permute-start | bytes 884744 | tf_op jit(solution)/shard_map/ppermute | solution.py:27
  21.8 12.3 %collective-permute-start.2 = (bf16[2,3,96,128]{3,2,1,0:T(8,128)(2,1)S(1)}, bf16[2,3,96,128]{3,2,1,0:T(8,128)(2,1)S(1)}, u32[]{:S(2)}, u32[]{:S(2)}) collective-permute-start(bf16[2,3,96,128]{3,2,1,0:T(8,128)(2,1)S(1)} %get-tuple-element.57), channel_id=1, source_target_pairs={{0,8},{8,16},{16,24},{24,0},{1,9},{9,17},{17,25},{25,1},{2,10},{10... | collective-permute-start | bytes 442376 | tf_op jit(solution)/shard_map/ppermute | solution.py:18
  23.9 10.1 %collective-permute-start.3 = (bf16[2,3,96,128]{3,2,1,0:T(8,128)(2,1)S(1)}, bf16[2,3,96,128]{3,2,1,0:T(8,128)(2,1)S(1)}, u32[]{:S(2)}, u32[]{:S(2)}) collective-permute-start(bf16[2,3,96,128]{3,2,1,0:T(8,128)(2,1)S(1)} %get-tuple-element.58), channel_id=1, source_target_pairs={{0,24},{8,0},{16,8},{24,16},{1,25},{9,1},{17,9},{25,17},{2,26},{10... | collective-permute-start | bytes 442376 | tf_op jit(solution)/shard_map/ppermute | solution.py:18
  31.6 15.3 %copy-start.2 = (bf16[288,896]{1,0:T(8,128)(2,1)S(1)}, bf16[288,896]{1,0:T(8,128)(2,1)}, u32[]{:S(2)}) copy-start(bf16[288,896]{1,0:T(8,128)(2,1)} %get-tuple-element.70.a_re) | copy-start | bytes 1548292
  31.6 15.3 %copy-start.3 = (bf16[288,896]{1,0:T(8,128)(2,1)S(1)}, bf16[288,896]{1,0:T(8,128)(2,1)}, u32[]{:S(2)}) copy-start(bf16[288,896]{1,0:T(8,128)(2,1)} %get-tuple-element.69.a_up) | copy-start | bytes 1548292
  31.6 11.8 %collective-permute-start.12 = (bf16[2,3,96,128]{3,2,1,0:T(8,128)(2,1)S(1)}, bf16[2,3,96,128]{3,2,1,0:T(8,128)(2,1)S(1)}, u32[]{:S(2)}, u32[]{:S(2)}) collective-permute-start(bf16[2,3,96,128]{3,2,1,0:T(8,128)(2,1)S(1)} %get-tuple-element.75), channel_id=1, source_target_pairs={{0,8},{8,16},{16,24},{24,0},{1,9},{9,17},{17,25},{25,1},{2,10},{10... | collective-permute-start | bytes 442376 | tf_op jit(solution)/shard_map/ppermute | solution.py:18
  34.0 9.4 %collective-permute-start.13 = (bf16[2,3,96,128]{3,2,1,0:T(8,128)(2,1)S(1)}, bf16[2,3,96,128]{3,2,1,0:T(8,128)(2,1)S(1)}, u32[]{:S(2)}, u32[]{:S(2)}) collective-permute-start(bf16[2,3,96,128]{3,2,1,0:T(8,128)(2,1)S(1)} %get-tuple-element.79), channel_id=1, source_target_pairs={{0,24},{8,0},{16,8},{24,16},{1,25},{9,1},{17,9},{25,17},{2,26},{10... | collective-permute-start | bytes 442376 | tf_op jit(solution)/shard_map/ppermute | solution.py:18
  35.1 11.8 %collective-permute-start.10 = (bf16[7,2,96,128]{3,2,1,0:T(8,128)(2,1)S(1)}, bf16[7,2,96,128]{3,2,1,0:T(8,128)(2,1)S(1)}, u32[]{:S(2)}, u32[]{:S(2)}) collective-permute-start(bf16[7,2,96,128]{3,2,1,0:T(8,128)(2,1)S(1)} %get-tuple-element.67), channel_id=1, source_target_pairs={{0,1},{1,0},{2,3},{3,2},{4,5},{5,4},{6,7},{7,6},{8,9},{9,8},{10,11... | collective-permute-start | bytes 1032200 | tf_op jit(solution)/shard_map/ppermute | solution.py:27
  36.1 10.8 %collective-permute-start.11 = (bf16[7,2,96,128]{3,2,1,0:T(8,128)(2,1)S(1)}, bf16[7,2,96,128]{3,2,1,0:T(8,128)(2,1)S(1)}, u32[]{:S(2)}, u32[]{:S(2)}) collective-permute-start(bf16[7,2,96,128]{3,2,1,0:T(8,128)(2,1)S(1)} %get-tuple-element.68), channel_id=1, source_target_pairs={{1,2},{2,1},{3,4},{4,3},{5,6},{6,5},{9,10},{10,9},{11,12},{12,11},... | collective-permute-start | bytes 1032200 | tf_op jit(solution)/shard_map/ppermute | solution.py:28
  44.0 9.7 %copy-start = (bf16[288,896]{1,0:T(8,128)(2,1)S(1)}, bf16[288,896]{1,0:T(8,128)(2,1)}, u32[]{:S(2)}) copy-start(bf16[288,896]{1,0:T(8,128)(2,1)} %get-tuple-element.83.a_re) | copy-start | bytes 1548292
  44.0 9.7 %copy-start.1 = (bf16[288,896]{1,0:T(8,128)(2,1)S(1)}, bf16[288,896]{1,0:T(8,128)(2,1)}, u32[]{:S(2)}) copy-start(bf16[288,896]{1,0:T(8,128)(2,1)} %get-tuple-element.82.a_up) | copy-start | bytes 1548292
  44.0 9.7 %copy-start.4 = (bf16[288,896]{1,0:T(8,128)(2,1)S(1)}, bf16[288,896]{1,0:T(8,128)(2,1)}, u32[]{:S(2)}) copy-start(bf16[288,896]{1,0:T(8,128)(2,1)} %get-tuple-element.84.a_ca_old) | copy-start | bytes 1548292
  44.0 9.7 %copy-start.5 = (bf16[288,896]{1,0:T(8,128)(2,1)S(1)}, bf16[288,896]{1,0:T(8,128)(2,1)}, u32[]{:S(2)}) copy-start(bf16[288,896]{1,0:T(8,128)(2,1)} %get-tuple-element.85.a_ca_new) | copy-start | bytes 1548292
  44.0 9.7 %copy-start.6 = (bf16[216,96]{1,0:T(8,128)(2,1)S(1)}, bf16[216,96]{1,0:T(8,128)(2,1)}, u32[]{:S(2)}) copy-start(bf16[216,96]{1,0:T(8,128)(2,1)} %get-tuple-element.86.head) | copy-start | bytes 124420
  44.1 9.7 %collective-permute-start.14 = (bf16[7,2,96,128]{3,2,1,0:T(8,128)(2,1)S(1)}, bf16[7,2,96,128]{3,2,1,0:T(8,128)(2,1)S(1)}, u32[]{:S(2)}, u32[]{:S(2)}) collective-permute-start(bf16[7,2,96,128]{3,2,1,0:T(8,128)(2,1)S(1)} %get-tuple-element.80), channel_id=1, source_target_pairs={{0,1},{1,0},{2,3},{3,2},{4,5},{5,4},{6,7},{7,6},{8,9},{9,8},{10,11... | collective-permute-start | bytes 1032200 | tf_op jit(solution)/shard_map/ppermute | solution.py:27
  44.8 8.9 %collective-permute-start.15 = (bf16[7,2,96,128]{3,2,1,0:T(8,128)(2,1)S(1)}, bf16[7,2,96,128]{3,2,1,0:T(8,128)(2,1)S(1)}, u32[]{:S(2)}, u32[]{:S(2)}) collective-permute-start(bf16[7,2,96,128]{3,2,1,0:T(8,128)(2,1)S(1)} %get-tuple-element.81), channel_id=1, source_target_pairs={{1,2},{2,1},{3,4},{4,3},{5,6},{6,5},{9,10},{10,9},{11,12},{12,11},... | collective-permute-start | bytes 1032200 | tf_op jit(solution)/shard_map/ppermute | solution.py:28
  63.1 3.5 %collective-permute-start.16 = (f32[1,5,8,128]{3,2,1,0:T(8,128)S(1)}, f32[1,5,8,128]{3,2,1,0:T(8,128)S(1)}, u32[]{:S(2)}, u32[]{:S(2)}) collective-permute-start(f32[1,5,8,128]{3,2,1,0:T(8,128)S(1)} %get-tuple-element.89), channel_id=1, source_target_pairs={{0,8},{8,16},{16,24},{24,0},{1,9},{9,17},{17,25},{25,1},{2,10},{10... | collective-permute-start | bytes 61448 | tf_op jit(solution)/shard_map/ppermute | solution.py:18
  65.7 3.5 %collective-permute-start.17 = (f32[1,5,8,128]{3,2,1,0:T(8,128)S(1)}, f32[1,5,8,128]{3,2,1,0:T(8,128)S(1)}, u32[]{:S(2)}, u32[]{:S(2)}) collective-permute-start(f32[1,5,8,128]{3,2,1,0:T(8,128)S(1)} %get-tuple-element.90), channel_id=1, source_target_pairs={{0,24},{8,0},{16,8},{24,16},{1,25},{9,1},{17,9},{25,17},{2,26},{10... | collective-permute-start | bytes 61448 | tf_op jit(solution)/shard_map/ppermute | solution.py:18
  69.8 5.0 %collective-permute-start.18 = (f32[3,1,8,128]{3,2,1,0:T(8,128)S(1)}, f32[3,1,8,128]{3,2,1,0:T(8,128)S(1)}, u32[]{:S(2)}, u32[]{:S(2)}) collective-permute-start(f32[3,1,8,128]{3,2,1,0:T(8,128)S(1)} %get-tuple-element.92), channel_id=1, source_target_pairs={{0,1},{1,0},{2,3},{3,2},{4,5},{5,4},{6,7},{7,6},{8,9},{9,8},{10,11... | collective-permute-start | bytes 36872 | tf_op jit(solution)/shard_map/ppermute | solution.py:27
  71.3 5.0 %collective-permute-start.19 = (f32[3,1,8,128]{3,2,1,0:T(8,128)S(1)}, f32[3,1,8,128]{3,2,1,0:T(8,128)S(1)}, u32[]{:S(2)}, u32[]{:S(2)}) collective-permute-start(f32[3,1,8,128]{3,2,1,0:T(8,128)S(1)} %get-tuple-element.93), channel_id=1, source_target_pairs={{1,2},{2,1},{3,4},{4,3},{5,6},{6,5},{9,10},{10,9},{11,12},{12,11},... | collective-permute-start | bytes 36872 | tf_op jit(solution)/shard_map/ppermute | solution.py:28
where the time goes:
time: 78.6 us; the launch traced here: 77.8 us
  Pallas kernels  40.6 us (52%)
  starting transfers between devices  31.1 us (40%)
  waiting for transfers between devices  5.08 us (6%)
  between operations  0.95 us (1%)
    pallas_call x11, Pallas kernels, call(): pl.pallas_call(body, out_shape=jax.tree.map(lambda o: pltpu.VMEM(o.shape,...  40.6 us
    ppermute x6, starting transfers between devices, rows_around(): lax.ppermute(to_other, 'gy', [(i, (i + 1 ^ 1) - 1) for i in range(1, coun...  18.5 us
    ppermute x8, starting transfers between devices, around(): lax.ppermute(block, axis, [(i, (i + step) % count) for i in range(count)])  8.7 us
    ppermute x6, starting transfers between devices, rows_around(): mate = lax.ppermute(to_mate, 'gy', [(i, i ^ 1) for i in range(count)])  3.9 us
    ppermute x8, waiting for transfers between devices, around(): lax.ppermute(block, axis, [(i, (i + step) % count) for i in range(count)])  3.54 us
  transfers between devices with their start and end apart: 20, of which 3 were waited for; matrix products, arithmetic and copies ran while one was open for 0% of the time, Pallas kernels for 38%

commit v1 on v0

--- a/solution.py
+++ b/solution.py
@@ -72,6 +72,7 @@
 
 def lay_out(width, weight, first_out, last_out, flat, wide):
     pieces = width * 2 * width // LANES
+    pitch = pieces + 1
     half = width // 2
     lane = lax.broadcasted_iota(jnp.int32, (half, LANES), 1)
 
@@ -95,15 +96,15 @@
         got = weight[:, pl.ds(pl.multiple_of(j * LANES, LANES), LANES)].astype(F32)
         for first in range(0, 27, 8):
             size = min(8, 27 - first)
-            flat[pl.ds(j + first * pieces, size, stride=pieces), :] = got[first : first + size]
+            flat[pl.ds(j + first * pitch, size, stride=pitch), :] = got[first : first + size]
         return carry
 
-    lax.fori_loop(0, pieces, spread, 0, unroll=4)
+    lax.fori_loop(0, pieces, spread, 0, unroll=8)
 
     for c in range(3):
         rows = [[], [], [], []]
         for ab in range(9):
-            first, mid, last = [flat[pl.ds((ab * 3 + c) * pieces + k, half, stride=3), :] for k in range(3)]
+            first, mid, last = [flat[pl.ds((ab * 3 + c) * pitch + k, half, stride=3), :] for k in range(3)]
             rows[0].append(first)
             rows[1].append(turn(jnp.where(lane < 64, last, mid), 64))
             rows[2].append(turn(jnp.where(lane >= 96, first, mid), 32))
@@ -117,7 +118,8 @@
 
 
 def lay_out_scratch(width):
-    return [pltpu.VMEM((27 * width * 2 * width // LANES, LANES), F32), pltpu.VMEM((2, 7, 3 * width, LANES), F32)]
+    pitch = width * 2 * width // LANES + 1
+    return [pltpu.VMEM((27 * pitch, LANES), F32), pltpu.VMEM((2, 7, 3 * width, LANES), F32)]
 
 
 def update_body(weight, first_out, last_out, flat, wide):
@@ -133,22 +135,36 @@
     head_out[...] = eights[:, :width].astype(BF16)
 
 
-def corr_part(held, source, tt, s_flat, corr, wc):
-    planes_out, rows_out, channels, _ = source.shape
-    wide = rows_out * LANES
-    scale = channels ** (-0.5)
-    for z in range(planes_out):
-        for y in range(rows_out):
-            s_flat[z, :, y * LANES : (y + 1) * LANES] = source[z, y]
+def held_rows(part, planes, rows):
+    def held(j):
+        if 3 <= j < 3 + rows:
+            return {"own": [(3, 3 + planes)], "face": [(0, 3), (3 + planes, 6 + planes)], "corner": []}[part]
+        return {"own": [], "face": [(3, 3 + planes)], "corner": [(0, 3), (3 + planes, 6 + planes)]}[part]
+
+    return held
+
+
+def slots_of(part, planes, rows):
+    slots = {}
+    held = held_rows(part, planes, rows)
+    for z in range(planes):
+        for j in range(rows + 6):
+            for first, last in held(j):
+                for plane in range(max(z, first), min(z + 7, last)):
+                    for y in range(rows):
+                        if 0 <= j - y <= 6:
+                            slots[z, y, (plane - z) * 7 + j - y] = len(slots)
+    return slots
+
+
+def corr_part(part, planes_out, rows_out, tt, s_flat, pairs):
+    channels = s_flat.shape[1]
     sub = lax.broadcasted_iota(jnp.int32, (8, LANES), 0)
     cell = lax.broadcasted_iota(jnp.int32, (8, LANES), 1)
     block_of = (cell + 4 - sub + 8) // 8 - 1
-    turn = (3 - lax.broadcasted_iota(jnp.int32, (1, 8, LANES), 2)) & 7
-    turn = jnp.concatenate([turn] * rows_out, axis=2)
-
-    results = []
+    held, slots = held_rows(part, planes_out, rows_out), slots_of(part, planes_out, rows_out)
+
     for z in range(planes_out):
-        filled = set()
         for j in range(rows_out + 6):
             ys = [y for y in range(rows_out) if 0 <= j - y <= 6]
             lo, hi = ys[0] * LANES, (ys[-1] + 1) * LANES
@@ -165,13 +181,26 @@
                             at = (plane - first) * LANES + 8 * k
                             piece = prod[at : at + 8, n * LANES : (n + 1) * LANES]
                             got = jnp.where(block_of == k, piece, got)
-                        corr[(plane - z) * 7 + j - y, :, y * LANES : (y + 1) * LANES] = got
-                        filled.add(((plane - z) * 7 + j - y, y))
+                        pairs[slots[z, y, (plane - z) * 7 + j - y]] = got
+
+
+def encode(planes, rows, scale, parts, wc):
+    wide = rows * LANES
+    found = {}
+    for part, pairs in parts.items():
+        found.update({key: (pairs, slot) for key, slot in slots_of(part, planes, rows).items()})
+    turn = (3 - lax.broadcasted_iota(jnp.int32, (1, 8, LANES), 2)) & 7
+    turn = jnp.concatenate([turn] * rows, axis=2)
+    results = []
+    for z in range(planes):
+        made = []
         for pair in range(49):
-            for y in range(rows_out):
-                if (pair, y) not in filled:
-                    corr[pair, :, y * LANES : (y + 1) * LANES] = jnp.zeros((8, LANES), F32)
-        got = corr[...]
+            row = []
+            for y in range(rows):
+                pairs, slot = found[z, y, pair]
+                row.append(pairs[slot])
+            made.append(jnp.concatenate(row, axis=1)[None])
+        got = jnp.concatenate(made, axis=0)
         for bit in (1, 2, 4):
             got = jnp.where((turn & bit) != 0, pltpu.roll(got, bit, 1), got)
         got = (got * scale).reshape(49 * 8, wide).astype(BF16)
@@ -203,8 +232,9 @@
 
 
 def own_body(
-    w_reset, w_update, source, own, w_corr, hidden,
-    out, wc, h_first, h_last, re_old, re_new, update_here, tt, s_flat, corr, reset_here, flat, wide, arrived
+    w_reset, w_update, source, own, w_corr, hidden, motion, w_motion, bias_encoder, bias_update, bias_reset, bias_cand, bias_head,
+    pairs, wc, h_first, h_last, s_flat, hidden_here, motion_here, begun, small, re_old, re_new, update_here,
+    tt, reset_here, flat, wide, arrived
 ):
     copies = [
         pltpu.make_async_copy(w_reset, reset_here, arrived.at[0]),
@@ -215,52 +245,61 @@
     planes, rows = source.shape[:2]
     h_first[...] = hidden[:2]
     h_last[...] = hidden[planes - 2 :]
+    hidden_here[...] = hidden[...]
+    motion_here[...] = motion[...]
+    width, outs = hidden.shape[2], motion.shape[2]
+    for n, row in enumerate((bias_encoder, bias_update, bias_reset, bias_cand)):
+        small[n : n + 1, :width] = row[...]
+    for n in range(w_motion.shape[0]):
+        small[4 + n : 5 + n, :width] = w_motion[n : n + 1, :]
+    shift = column(bias_head[...])
+    for z in range(planes):
+        for y in range(rows):
+            s_flat[z, :, y * LANES : (y + 1) * LANES] = source[z, y]
+            begun[z, y] = jnp.zeros(begun.shape[2:], F32)
+            begun[z, y, :outs] = motion[z, y] + shift
     at = lax.broadcasted_iota(jnp.int32, (w_corr.shape[1], 49 * 8), 0)
     to = lax.broadcasted_iota(jnp.int32, (w_corr.shape[1], 49 * 8), 1)
     pick = ((to & 7) < 7) & (at == (to >> 3) * 7 + (to & 7))
     wc[...] = jnp.dot(w_corr[...], jnp.where(pick, 1.0, 0.0).astype(BF16), preferred_element_type=F32).astype(BF16)
     put_block(tt, own, None, 3, 3)
-    held = lambda j: [(3, 3 + planes)] if 3 <= j < 3 + rows else []
-    for z, got in enumerate(corr_part(held, source, tt, s_flat, corr, wc)):
-        out[z] = got
+    corr_part("own", planes, rows, tt, s_flat, pairs)
     copies[0].wait()
-    lay_out(hidden.shape[2], reset_here, re_old, re_new, flat, wide)
+    lay_out(width, reset_here, re_old, re_new, flat, wide)
     copies[1].wait()
 
 
-def corr_face_body(place, source, before, low, high, mate, other, wc, out, tt, s_flat, corr):
-    planes, rows = source.shape[:2]
+def corr_face_body(place, s_flat, low, high, mate, other, pairs, tt):
+    planes, rows = s_flat.shape[0], s_flat.shape[2] // LANES
     odd = place[3]
     put_block(tt, low, place[0] == 1, 3, 0)
     put_block(tt, high, place[1] == 1, 3, 3 + planes)
     put_block(tt, mate, None, (3 + rows) * (1 - odd), 3)
     put_block(tt, other, place[2] == 1, (3 + rows) * odd, 3)
 
-    def held(j):
-        return [(3, 3 + planes)] if j < 3 or j >= 3 + rows else [(0, 3), (3 + planes, 6 + planes)]
-
-    for z, got in enumerate(corr_part(held, source, tt, s_flat, corr, wc)):
-        out[z] = before[z] + got
+    corr_part("face", planes, rows, tt, s_flat, pairs)
 
 
 def corr_corner_body(
-    place, source, motion, w_motion, bias, before, low_mate, low_other, high_mate, high_other, wc,
-    enc, enc_first, enc_last, tt, s_flat, corr
+    place, s_flat, motion, small, own_pairs, face_pairs, low_mate, low_other, high_mate, high_other, wc,
+    enc, enc_first, enc_last, tt, pairs
 ):
-    planes, rows = source.shape[:2]
+    planes, rows, outs = motion.shape[:3]
+    width = enc.shape[2]
     odd = place[3]
     mate_at, other_at = (3 + rows) * (1 - odd), (3 + rows) * odd
     put_block(tt, low_mate, place[0] == 1, mate_at, 0)
     put_block(tt, low_other, place[0] + place[2] == 2, other_at, 0)
     put_block(tt, high_mate, place[1] == 1, mate_at, 3 + planes)
     put_block(tt, high_other, place[1] + place[2] == 2, other_at, 3 + planes)
-    held = lambda j: [(0, 3), (3 + planes, 6 + planes)] if j < 3 or j >= 3 + rows else []
-    shift = column(bias[...])
-    moves = [column(w_motion[k : k + 1, :]) for k in range(w_motion.shape[0])]
-    for z, got in enumerate(corr_part(held, source, tt, s_flat, corr, wc)):
+    shift = column(small[0:1, :width])
+    moves = [column(small[4 + k : 5 + k, :width]) for k in range(outs)]
+    corr_part("corner", planes, rows, tt, s_flat, pairs)
+    scale = s_flat.shape[1] ** (-0.5)
+    parts = {"own": own_pairs, "face": face_pairs, "corner": pairs}
+    for z, got in enumerate(encode(planes, rows, scale, parts, wc)):
         for y in range(rows):
-            at = slice(y * LANES, (y + 1) * LANES)
-            total = got[:, at] + before[z, :, at]
+            total = got[:, y * LANES : (y + 1) * LANES]
             for k, move in enumerate(moves):
                 total = total + move * motion[z, y, k : k + 1, :]
             value = jnp.maximum(total + shift, 0.0).astype(BF16)
@@ -352,10 +391,11 @@
                 store_if(in_z + place[2] == 2, plane, other_at, lambda: other[plane, y])
 
 
-def old_body(place, hidden, b_up, b_re, hz0, hz1, h_mate, h_other, a_up, a_re, update_out, reset_out, near_out, field):
+def old_body(place, hidden, small, hz0, hz1, h_mate, h_other, a_up, a_re, update_out, reset_out, near_out, field):
     planes, rows = hidden.shape[:2]
     fill(place, field, hidden, hz0, hz1, h_mate, h_other)
-    up_shift, re_shift = column(b_up[...]), column(b_re[...])
+    width = hidden.shape[2]
+    up_shift, re_shift = column(small[1:2, :width]), column(small[2:3, :width])
 
     def reset_plane(z, carry):
         near_out[z] = field[z + 1, :, LANES : (rows + 3) * LANES]
@@ -363,23 +403,23 @@
             reset_out[z, y] = got + re_shift
         return carry
 
-    lax.fori_loop(0, planes + 2, reset_plane, 0)
+    lax.fori_loop(0, planes + 2, reset_plane, 0, unroll=True)
 
     def update_plane(z, carry):
         for y, got in enumerate(conv(a_up[...], taps(field, z + 1, 1, rows), rows)):
             update_out[z, y] = got + up_shift
         return carry
 
-    lax.fori_loop(0, planes, update_plane, 0)
+    lax.fori_loop(0, planes, update_plane, 0, unroll=True)
 
 
 def gru_body(
-    place, hidden, b_ca, near, update_old, reset_old, enc, ez0, ez1, e_mate, e_other, a_up, a_re, a_ca_old, a_ca_new,
+    place, begun, small, near, update_old, reset_old, enc, ez0, ez1, e_mate, e_other, a_up, a_re, a_ca_old, a_ca_new,
     head, state_out, part_low, part_out, part_high, field, gated, state
 ):
-    planes, rows = hidden.shape[:2]
+    planes, rows, width = enc.shape[:3]
     fill(place, field, enc, ez0, ez1, e_mate, e_other)
-    ca_shift = column(b_ca[...])
+    ca_shift = column(small[3:4, :width])
 
     def reset_plane(z, carry):
         for y, got in enumerate(conv(a_re[...], taps(field, z, 0, rows + 2), rows + 2)):
@@ -388,7 +428,7 @@
             gated[z, :, at] = (gate * near[z, :, at].astype(F32)).astype(BF16)
         return carry
 
-    lax.fori_loop(0, planes + 2, reset_plane, 0)
+    lax.fori_loop(0, planes + 2, reset_plane, 0, unroll=True)
 
     def state_plane(z, carry):
         new_taps = taps(field, z + 1, 1, rows)
@@ -398,13 +438,13 @@
         for y in range(rows):
             gate = jax.nn.sigmoid(update[y] + update_old[z, y])
             new = jnp.tanh(cand[y] + ca_shift)
-            old = hidden[z, y].astype(F32)
+            old = near[z + 1, :, (y + 1) * LANES : (y + 2) * LANES].astype(F32)
             got = ((1.0 - gate) * old + gate * new).astype(BF16)
             state_out[z, y] = got
             state[z, :, y * LANES : (y + 1) * LANES] = got
         return carry
 
-    lax.fori_loop(0, planes, state_plane, 0)
+    lax.fori_loop(0, planes, state_plane, 0, unroll=True)
 
     cell = lax.broadcasted_iota(jnp.int32, (8, LANES), 1)
     sums = {}
@@ -427,6 +467,8 @@
             part_low[0, y] = total
         elif z == planes + 1:
             part_high[0, y] = total
+        elif 0 < y <= rows:
+            part_out[z - 1, y] = total + begun[z - 1, y - 1]
         else:
             part_out[z - 1, y] = total
 
@@ -451,13 +493,12 @@
         to_other[z, 0] = added(z, other_at)
 
 
-def last_body(place, motion, bias, mine, mate, other, out):
+def last_body(place, mine, mate, other, out):
     planes, rows, outs = out.shape[:3]
     odd = place[3]
-    shift = column(bias[...])
     for z in range(planes):
         for y in range(rows):
-            out[z, y] = motion[z, y] + mine[z, y, :outs] + shift
+            out[z, y] = mine[z, y, :outs]
         mate_at, other_at = (rows - 1) * (1 - odd), (rows - 1) * odd
         out[z, mate_at] = out[z, mate_at] + mate[z, 0, :outs]
 
@@ -478,48 +519,47 @@
     t_low, t_high = planes_around(target[:3], target[-3:])
     t_mate, t_other = rows_around(*edges(target, 3))
 
-    scratch = [
-        pltpu.VMEM((rows + 6, planes + 6, LANES, channels), BF16),
-        pltpu.VMEM((planes, channels, wide), BF16),
-        pltpu.VMEM((49, 8, wide), F32),
-    ]
-    sums = jax.ShapeDtypeStruct((planes, width, wide), F32)
-    two = jax.ShapeDtypeStruct((2, rows, width, cells), BF16)
+    target_rows = pltpu.VMEM((rows + 6, planes + 6, LANES, channels), BF16)
+    made = jax.ShapeDtypeStruct
+    pairs = {part: made((len(slots_of(part, planes, rows)), 8, cells), F32) for part in ("own", "face", "corner")}
+    two = made((2, rows, width, cells), BF16)
+    eight = made((planes, rows, 8, cells), F32)
     laid = pltpu.HBM((3 * width, 7 * LANES), BF16)
-    own, wc, h_first, h_last, re_old, re_new, update_here = call(
+    biases = [b[None, :] for b in (bias_encoder, bias_update, bias_reset, bias_cand, bias_head)]
+    own, wc, h_first, h_last, s_flat, hidden_here, motion_here, begun, small, re_old, re_new, update_here = call(
         own_body,
-        (sums, jax.ShapeDtypeStruct((width, 49 * 8), BF16), two, two, laid, laid)
-        + (jax.ShapeDtypeStruct(w_update.shape, BF16),),
-        scratch + [pltpu.VMEM(w_reset.shape, BF16)] + lay_out_scratch(width) + [pltpu.SemaphoreType.DMA((2,))],
-        (w_reset, w_update, source, target, w_corr, hidden),
+        (pairs["own"], made((width, 49 * 8), BF16), two, two, made((planes, channels, wide), BF16))
+        + (made(hidden.shape, BF16), made(motion.shape, F32), eight, made((8, LANES), F32), laid, laid)
+        + (made(w_update.shape, BF16),),
+        [target_rows, pltpu.VMEM(w_reset.shape, BF16)] + lay_out_scratch(width) + [pltpu.SemaphoreType.DMA((2,))],
+        [w_reset, w_update, source, target, w_corr, hidden, motion, w_motion.T] + biases,
         "own",
-        20,
-        from_hbm=(pltpu.HBM,) * 2 + (pltpu.VMEM,) * 4,
+        14,
+        from_hbm=(pltpu.HBM,) * 2 + (pltpu.VMEM,) * 11,
     )
     t_low, own = lax.optimization_barrier((t_low, own))
     t_low_mate, t_low_other = rows_around(*edges(t_low, 3))
     update_here, t_low = lax.optimization_barrier((update_here, t_low))
     up_old, up_new = call(
-        update_body, (laid, laid), lay_out_scratch(width), (update_here,), "lay_out_update", 12
+        update_body, (laid, laid), lay_out_scratch(width), (update_here,), "lay_out_update", 8
     )
     t_high, up_new = lax.optimization_barrier((t_high, up_new))
     t_high_mate, t_high_other = rows_around(*edges(t_high, 3))
     h_first, h_last, t_low, t_high = lax.optimization_barrier((h_first, h_last, t_low, t_high))
     h_low, h_high = planes_around(h_first, h_last)
     face = call(
-        corr_face_body, sums, scratch, (source, own, t_low, t_high, t_mate, t_other, wc), "face", 12, place,
-        from_hbm=(pltpu.VMEM,),
-    )
+        corr_face_body, pairs["face"], [target_rows], (s_flat, t_low, t_high, t_mate, t_other), "face", 9, place
+    )
+
     enc, enc_first, enc_last = call(
         corr_corner_body,
-        (jax.ShapeDtypeStruct((planes, rows, width, cells), BF16), two, two),
-        scratch,
-        (source, motion, w_motion.T, bias_encoder[None, :])
-        + (face, t_low_mate, t_low_other, t_high_mate, t_high_other, wc),
+        (made(hidden.shape, BF16), two, two),
+        [target_rows] + [pltpu.VMEM(pairs["corner"].shape, F32)],
+        (s_flat, motion_here, small)
+        + (own, face, t_low_mate, t_low_other, t_high_mate, t_high_other, wc),
         "corner",
-        12,
+        10,
         place,
-        from_hbm=(pltpu.VMEM,) * 4,
     )
     e_low, e_high = planes_around(enc_first, enc_last)
     taps_head, enc = lax.optimization_barrier((jnp.transpose(w_head, (1, 0, 2)), enc))
@@ -529,12 +569,12 @@
         lay_out_scratch(width) + [pltpu.VMEM((27 * 8, LANES), F32)],
         (w_cand, taps_head),
         "lay_out_cand",
-        12,
+        8,
         from_hbm=(pltpu.VMEM,) * 2,
     )
     e_low, ca_new = lax.optimization_barrier((e_low, ca_new))
     h_low, h_high, enc = lax.optimization_barrier((h_low, h_high, enc))
-    h_mate, h_other = rows_around(*rows_of(place, h_low, hidden, h_high, 2, "pack_hidden", (pltpu.VMEM,)))
+    h_mate, h_other = rows_around(*rows_of(place, h_low, hidden_here, h_high, 2, "pack_hidden"))
     field = pltpu.VMEM((planes + 4, width, (rows + 4) * LANES), BF16)
     update_old, reset_old, near = call(
         old_body,
@@ -544,11 +584,10 @@
             jax.ShapeDtypeStruct((planes + 2, width, (rows + 2) * LANES), BF16),
         ),
         [field],
-        (hidden, bias_update[None, :], bias_reset[None, :], h_low, h_high, h_mate, h_other, up_old, re_old),
+        (hidden_here, small, h_low, h_high, h_mate, h_other, up_old, re_old),
         "old",
-        12,
+        10,
         place,
-        from_hbm=(pltpu.VMEM,) * 3,
     )
     e_mate, e_other = rows_around(*rows_of(place, e_low, enc, e_high, 2, "pack_encoded"))
 
@@ -561,12 +600,11 @@
             pltpu.VMEM((planes + 2, width, (rows + 2) * LANES), BF16),
             pltpu.VMEM((planes, width, wide), BF16),
         ],
-        (hidden, bias_cand[None, :], near, update_old, reset_old, enc, e_low, e_high, e_mate, e_other)
+        (begun, small, near, update_old, reset_old, enc, e_low, e_high, e_mate, e_other)
         + (up_new, re_new, ca_old, ca_new, head),
         "gru",
-        14,
+        12,
         place,
-        from_hbm=(pltpu.VMEM,) * 2,
         kept=False,
     )
     low, high = planes_around(part_low, part_high)
@@ -585,11 +623,10 @@
         last_body,
         jax.ShapeDtypeStruct(motion.shape, F32),
         [],
-        (motion, bias_head[None, :], mine, mate, other),
+        (mine, mate, other),
         "last",
         4,
         place,
-        from_hbm=(pltpu.VMEM,) * 2,
         kept=False,
     )
     return state_out, motion_out

time: 78.6 us -> 70.7 us (0.90)
  Pallas kernels: 40.6 us -> 31.5 us
  waiting for transfers between devices: 5.08 us -> 7.42 us
    pallas_call x11, Pallas kernels: 40.6 us -> 31.5 us  [call(): pl.pallas_call(body, out_shape=jax.tree.map(lambda o: pltpu.VMEM(o.shape,...]
    ppermute x6, waiting for transfers between devices: 1.52 us -> 3.86 us  [rows_around(): lax.ppermute(to_other, 'gy', [(i, (i + 1 ^ 1) - 1) for i in range(1, coun...]
  transfers between devices with their start and end apart: 20 -> 20, of which waited for: 3 -> 5; matrix products, arithmetic and copies ran while one was open for 0% -> 0% of each run, Pallas kernels for 38% -> 33%
where the time goes in v1:
time: 70.7 us; the launch traced here: 70.3 us
  Pallas kernels  31.5 us (45%)
  starting transfers between devices  30.4 us (43%)
  waiting for transfers between devices  7.42 us (10%)
  between operations  0.96 us (1%)
    pallas_call x11, Pallas kernels, call(): pl.pallas_call(body, out_shape=jax.tree.map(lambda o: pltpu.VMEM(o.shape,...  31.5 us
    ppermute x6, starting transfers between devices, rows_around(): lax.ppermute(to_other, 'gy', [(i, (i + 1 ^ 1) - 1) for i in range(1, coun...  18.1 us
    ppermute x8, starting transfers between devices, around(): lax.ppermute(block, axis, [(i, (i + step) % count) for i in range(count)])  8.46 us
    ppermute x6, waiting for transfers between devices, rows_around(): lax.ppermute(to_other, 'gy', [(i, (i + 1 ^ 1) - 1) for i in range(1, coun...  3.86 us
    ppermute x6, starting transfers between devices, rows_around(): mate = lax.ppermute(to_mate, 'gy', [(i, i ^ 1) for i in range(count)])  3.81 us
    ppermute x8, waiting for transfers between devices, around(): lax.ppermute(block, axis, [(i, (i + step) % count) for i in range(count)])  3.54 us
  transfers between devices with their start and end apart: 20, of which 5 were waited for; matrix products, arithmetic and copies ran while one was open for 0% of the time, Pallas kernels for 33%

profile of v1, /device:TPU:11, one launch (start us, length us, event | category | flops | bytes accessed | tf_op | source)
XLA Modules:
  0.0 70.3 jit_solution(14761986037479685689)
XLA Ops:
  0.6 1.3 %collective-permute-start = (bf16[3,3,128,128]{3,2,1,0:T(8,128)(2,1)}, bf16[3,3,128,128]{3,2,1,0:T(8,128)(2,1)S(1)}, u32[]{:S(2)}, u32[]{:S(2)}) collective-permute-start(bf16[3,3,128,128]{3,2,1,0:T(8,128)(2,1)} %own.3), channel_id=1, source_target_pairs={{0,8},{8,16},{16,24},{24,0},{1,9},{9,17},{17,25},{25,1},{2,10},{10... | collective-permute-start | bytes 884744 | tf_op jit(solution)/shard_map/ppermute | solution.py:18
  1.9 0.3 collective-permute-start.1
  2.2 1.2 %collective-permute-start.4 = (bf16[3,3,128,128]{3,2,1,0:T(8,128)(2,1)}, bf16[3,3,128,128]{3,2,1,0:T(8,128)(2,1)S(1)}, u32[]{:S(2)}, u32[]{:S(2)}) collective-permute-start(bf16[3,3,128,128]{3,2,1,0:T(8,128)(2,1)} %own.3), channel_id=1, source_target_pairs={{0,1},{1,0},{2,3},{3,2},{4,5},{5,4},{6,7},{7,6},{8,9},{9,8},{10,11... | collective-permute-start | bytes 884744 | tf_op jit(solution)/shard_map/ppermute | solution.py:27
  3.4 3.1 %collective-permute-start.5 = (bf16[3,3,128,128]{3,2,1,0:T(8,128)(2,1)}, bf16[3,3,128,128]{3,2,1,0:T(8,128)(2,1)S(1)}, u32[]{:S(2)}, u32[]{:S(2)}) collective-permute-start(bf16[3,3,128,128]{3,2,1,0:T(8,128)(2,1)} %own.3), channel_id=1, source_target_pairs={{1,2},{2,1},{3,4},{4,3},{5,6},{6,5},{9,10},{10,9},{11,12},{12,11},... | collective-permute-start | bytes 884744 | tf_op jit(solution)/shard_map/ppermute | solution.py:28
  6.5 5.2 %own.2 = (f32[81,8,128]{2,1,0:T(8,128)S(1)}, bf16[96,392]{1,0:T(8,128)(2,1)S(1)}, bf16[2,3,96,128]{3,2,1,0:T(8,128)(2,1)S(1)}, bf16[2,3,96,128]{3,2,1,0:T(8,128)...) custom-call(bf16[27,18432]{1,0:T(8,128)(2,1)} %w_reset.1, ...), custom_call_target="tpu_custom_call" | custom-call | flops 1000 | bytes 1000 | tf_op jit(solution)/shard_map/own/pallas_call | solution.py:61
  11.7 0.0 copy-start.7
  11.7 0.0 collective-permute-done.low
  11.7 0.1 collective-permute-start.6
  11.8 3.6 %collective-permute-start.7 = (bf16[3,3,128,128]{3,2,1,0:T(8,128)(2,1)S(1)}, bf16[3,3,128,128]{3,2,1,0:T(8,128)(2,1)S(1)}, u32[]{:S(2)}, u32[]{:S(2)}) collective-permute-start(bf16[3,3,128,128]{3,2,1,0:T(8,128)(2,1)S(1)} %collective-permute-done.low), channel_id=1, source_target_pairs={{1,2},{2,1},{3,4},{4,3},{5,6},{6,5},{9,10},{10,9},{11,12},{12,11},... | collective-permute-start | bytes 884744 | tf_op jit(solution)/shard_map/ppermute | solution.py:28
  15.3 2.4 %lay_out_update.1 = (bf16[288,896]{1,0:T(8,128)(2,1)}, bf16[288,896]{1,0:T(8,128)(2,1)}) custom-call(bf16[27,18432]{1,0:T(8,128)(2,1)S(1)} %get-tuple-element.62.weight), custom_call_target="tpu_custom_call" | custom-call | flops 1000 | bytes 1000 | tf_op jit(solution)/shard_map/lay_out_update/pallas_call | solution.py:61
  17.7 0.0 collective-permute-done.1.high
  17.7 0.0 collective-permute-start.8
  17.7 0.0 collective-permute-done.4.mate
  17.8 0.0 copy-done.7
  17.8 2.9 %collective-permute-start.9 = (bf16[3,3,128,128]{3,2,1,0:T(8,128)(2,1)S(1)}, bf16[3,3,128,128]{3,2,1,0:T(8,128)(2,1)S(1)}, u32[]{:S(2)}, u32[]{:S(2)}) collective-permute-start(bf16[3,3,128,128]{3,2,1,0:T(8,128)(2,1)S(1)} %collective-permute-done.1.high), channel_id=1, source_target_pairs={{1,2},{2,1},{3,4},{4,3},{5,6},{6,5},{9,10},{10,9},{11,12},{12,11},... | collective-permute-start | bytes 884744 | tf_op jit(solution)/shard_map/ppermute | solution.py:28
  20.7 0.0 collective-permute-done.5.other
  20.7 2.0 %collective-permute-start.2 = (bf16[2,3,96,128]{3,2,1,0:T(8,128)(2,1)}, bf16[2,3,96,128]{3,2,1,0:T(8,128)(2,1)S(1)}, u32[]{:S(2)}, u32[]{:S(2)}) collective-permute-start(bf16[2,3,96,128]{3,2,1,0:T(8,128)(2,1)} %copy-done.7), channel_id=1, source_target_pairs={{0,8},{8,16},{16,24},{24,0},{1,9},{9,17},{17,25},{25,1},{2,10},{10... | collective-permute-start | bytes 442376 | tf_op jit(solution)/shard_map/ppermute | solution.py:18
  22.8 0.0 collective-permute-done.6.low_mate
  22.8 0.0 collective-permute-start.3
  22.8 0.1 add_convert_fusion.place
  22.8 3.1 %face.1.face_pairs = f32[216,8,128]{2,1,0:T(8,128)S(1)} custom-call(s32[4]{0:T(128)S(1)} %add_convert_fusion.place, bf16[3,128,384]{2,1,0:T(8,128)(2,1)S(1)} %get-tuple-element.67.s_flat, bf16[3,3,128,128]{3,2,1,0:T(8,128)(2,1)S(1)} %collective-permute-done.low, bf16[3,3,128,128]{3,2,1,0:T(8,128)(2,1)S(1)} %collective-permute-done.1.high, ...), custom_call_target="tpu_custom_call" | custom-call | flops 1000 | bytes 1000 | tf_op jit(solution)/shard_map/face/pallas_call | solution.py:61
  25.9 0.0 collective-permute-done.7.low_other
  25.9 0.0 collective-permute-done.8.high_mate
  25.9 0.2 collective-permute-done.9.high_other
  26.1 2.9 %corner.1 = (bf16[3,3,96,128]{3,2,1,0:T(8,128)(2,1)S(1)}, bf16[2,3,96,128]{3,2,1,0:T(8,128)(2,1)S(1)}, bf16[2,3,96,128]{3,2,1,0:T(8,128)(2,1)S(1)}) custom-call(s32[4]{0:T(128)S(1)} %add_convert_fusion.place, bf16[3,128,384]{2,1,0:T(8,128)(2,1)S(1)} %get-tuple-element.67.s_flat, f32[3,3,3,128]{3,2,1,0:T(4,128)S(1)} %get-tuple-element.68.motion, ...), custom_call_target="tpu_custom_call" | custom-call | flops 1000 | bytes 1000 | tf_op jit(solution)/shard_map/corner/pallas_call | solution.py:61
  29.0 0.0 copy-start.2
  29.0 0.0 copy-start.3
  29.0 2.3 %collective-permute-start.12 = (bf16[2,3,96,128]{3,2,1,0:T(8,128)(2,1)S(1)}, bf16[2,3,96,128]{3,2,1,0:T(8,128)(2,1)S(1)}, u32[]{:S(2)}, u32[]{:S(2)}) collective-permute-start(bf16[2,3,96,128]{3,2,1,0:T(8,128)(2,1)S(1)} %get-tuple-element.85), channel_id=1, source_target_pairs={{0,8},{8,16},{16,24},{24,0},{1,9},{9,17},{17,25},{25,1},{2,10},{10... | collective-permute-start | bytes 442376 | tf_op jit(solution)/shard_map/ppermute | solution.py:18
  31.3 0.0 collective-permute-start.13
  31.3 0.0 collective-permute-done.2.low.hz0
  31.3 0.0 collective-permute-done.3.high.hz1
  31.3 0.6 pack_hidden.1
  31.9 0.6 collective-permute-start.10
  32.4 3.1 %collective-permute-start.11 = (bf16[7,2,96,128]{3,2,1,0:T(8,128)(2,1)S(1)}, bf16[7,2,96,128]{3,2,1,0:T(8,128)(2,1)S(1)}, u32[]{:S(2)}, u32[]{:S(2)}) collective-permute-start(bf16[7,2,96,128]{3,2,1,0:T(8,128)(2,1)S(1)} %get-tuple-element.78), channel_id=1, source_target_pairs={{1,2},{2,1},{3,4},{4,3},{5,6},{6,5},{9,10},{10,9},{11,12},{12,11},... | collective-permute-start | bytes 1032200 | tf_op jit(solution)/shard_map/ppermute | solution.py:28
  35.6 3.7 %lay_out_cand.1 = (bf16[288,896]{1,0:T(8,128)(2,1)}, bf16[288,896]{1,0:T(8,128)(2,1)}, bf16[216,96]{1,0:T(8,128)(2,1)}) custom-call(bf16[27,18432]{1,0:T(8,128)(2,1)} %weight.1, bf16[3,27,96]{2,1,0:T(8,128)(2,1)} %bitcast.11), custom_call_target="tpu_custom_call" | custom-call | flops 1000 | bytes 1000 | tf_op jit(solution)/shard_map/lay_out_cand/pallas_call | solution.py:61
  39.3 0.0 collective-permute-done.12.low.ez0
  39.3 0.0 collective-permute-done.13.high.ez1
  39.3 0.6 pack_encoded.1
  39.9 0.0 copy-start
  39.9 0.0 copy-start.1
  39.9 0.0 copy-start.4
  39.9 0.0 copy-start.5
  39.9 0.0 copy-start.6
  39.9 0.1 collective-permute-start.14
  40.0 2.9 %collective-permute-start.15 = (bf16[7,2,96,128]{3,2,1,0:T(8,128)(2,1)S(1)}, bf16[7,2,96,128]{3,2,1,0:T(8,128)(2,1)S(1)}, u32[]{:S(2)}, u32[]{:S(2)}) collective-permute-start(bf16[7,2,96,128]{3,2,1,0:T(8,128)(2,1)S(1)} %get-tuple-element.91), channel_id=1, source_target_pairs={{1,2},{2,1},{3,4},{4,3},{5,6},{6,5},{9,10},{10,9},{11,12},{12,11},... | collective-permute-start | bytes 1032200 | tf_op jit(solution)/shard_map/ppermute | solution.py:28
  42.9 0.0 collective-permute-done.10.h_mate
  42.9 0.0 collective-permute-done.11.h_other
  43.0 0.0 copy-done.2
  43.0 4.5 %old.1 = (f32[3,3,96,128]{3,2,1,0:T(8,128)S(1)}, f32[5,5,96,128]{3,2,1,0:T(8,128)S(1)}, bf16[5,96,640]{2,1,0:T(8,128)(2,1)S(1)}) custom-call(s32[4]{0:T(128)S(1)} %add_convert_fusion.place, bf16[3,3,96,128]{3,2,1,0:T(8,128)(2,1)S(1)} %get-tuple-element.55.own.hidden, f32[8,128]{1,0:T(8,128)S(1)} %get-tuple-element.54.small, ...), custom_call_target="tpu_custom_call" | custom-call | flops 1000 | bytes 1000 | tf_op jit(solution)/shard_map/old/pallas_call | solution.py:61
  47.5 0.0 collective-permute-done.14.e_mate
  47.5 1.2 %collective-permute-done.15.e_other = bf16[7,2,96,128]{3,2,1,0:T(8,128)(2,1)S(1)} collective-permute-done((bf16[7,2,96,128]{3,2,1,0:T(8,128)(2,1)S(1)}, bf16[7,2,96,128]{3,2,1,0:T(8,128)(2,1)S(1)}, u32[]{:S(2)}, u32[]{:S(2)}) %collective-permute-start.15) | collective-permute-done | bytes 344096 | tf_op jit(solution)/shard_map/ppermute | solution.py:28
  48.7 0.0 copy-done
  48.7 0.0 copy-done.4
  48.7 6.9 %gru.1 = (bf16[3,3,96,128]{3,2,1,0:T(8,128)(2,1)}, f32[1,5,8,128]{3,2,1,0:T(8,128)S(1)}, f32[3,5,8,128]{3,2,1,0:T(8,128)S(1)}, f32[1,5,8,128]{3,2,1,0:T(8,128)S(1)}) custom-call(s32[4]{0:T(128)S(1)} %add_convert_fusion.place, f32[3,3,8,128]{3,2,1,0:T(8,128)S(1)} %get-tuple-element.53.begun, f32[8,128]{1,0:T(8,128)S(1)} %get-tuple-element.54.small, ...), custom_call_target="tpu_custom_call" | custom-call | flops 1000 | bytes 1000 | tf_op jit(solution)/shard_map/gru/pallas_call | solution.py:61
  55.6 2.6 %collective-permute-start.16 = (f32[1,5,8,128]{3,2,1,0:T(8,128)S(1)}, f32[1,5,8,128]{3,2,1,0:T(8,128)S(1)}, u32[]{:S(2)}, u32[]{:S(2)}) collective-permute-start(f32[1,5,8,128]{3,2,1,0:T(8,128)S(1)} %get-tuple-element.99), channel_id=1, source_target_pairs={{0,8},{8,16},{16,24},{24,0},{1,9},{9,17},{17,25},{25,1},{2,10},{10... | collective-permute-start | bytes 61448 | tf_op jit(solution)/shard_map/ppermute | solution.py:18
  58.2 0.0 collective-permute-start.17
  58.2 0.9 %collective-permute-done.16.low = f32[1,5,8,128]{3,2,1,0:T(8,128)S(1)} collective-permute-done((f32[1,5,8,128]{3,2,1,0:T(8,128)S(1)}, f32[1,5,8,128]{3,2,1,0:T(8,128)S(1)}, u32[]{:S(2)}, u32[]{:S(2)}) %collective-permute-start.16) | collective-permute-done | bytes 20512 | tf_op jit(solution)/shard_map/ppermute | solution.py:18
  59.1 2.6 %collective-permute-done.17.high = f32[1,5,8,128]{3,2,1,0:T(8,128)S(1)} collective-permute-done((f32[1,5,8,128]{3,2,1,0:T(8,128)S(1)}, f32[1,5,8,128]{3,2,1,0:T(8,128)S(1)}, u32[]{:S(2)}, u32[]{:S(2)}) %collective-permute-start.17) | collective-permute-done | bytes 20512 | tf_op jit(solution)/shard_map/ppermute | solution.py:18
  61.8 0.6 mix.1
  62.3 1.8 %collective-permute-start.18 = (f32[3,1,8,128]{3,2,1,0:T(8,128)S(1)}, f32[3,1,8,128]{3,2,1,0:T(8,128)S(1)}, u32[]{:S(2)}, u32[]{:S(2)}) collective-permute-start(f32[3,1,8,128]{3,2,1,0:T(8,128)S(1)} %get-tuple-element.102), channel_id=1, source_target_pairs={{0,1},{1,0},{2,3},{3,2},{4,5},{5,4},{6,7},{7,6},{8,9},{9,8},{10,11... | collective-permute-start | bytes 36872 | tf_op jit(solution)/shard_map/ppermute | solution.py:27
  64.2 2.5 %collective-permute-start.19 = (f32[3,1,8,128]{3,2,1,0:T(8,128)S(1)}, f32[3,1,8,128]{3,2,1,0:T(8,128)S(1)}, u32[]{:S(2)}, u32[]{:S(2)}) collective-permute-start(f32[3,1,8,128]{3,2,1,0:T(8,128)S(1)} %get-tuple-element.103), channel_id=1, source_target_pairs={{1,2},{2,1},{3,4},{4,3},{5,6},{6,5},{9,10},{10,9},{11,12},{12,11},... | collective-permute-start | bytes 36872 | tf_op jit(solution)/shard_map/ppermute | solution.py:28
  66.6 0.0 collective-permute-done.18.mate
  66.6 2.5 %collective-permute-done.19.other = f32[3,1,8,128]{3,2,1,0:T(8,128)S(1)} collective-permute-done((f32[3,1,8,128]{3,2,1,0:T(8,128)S(1)}, f32[3,1,8,128]{3,2,1,0:T(8,128)S(1)}, u32[]{:S(2)}, u32[]{:S(2)}) %collective-permute-start.19) | collective-permute-done | bytes 12320 | tf_op jit(solution)/shard_map/ppermute | solution.py:28
  69.2 1.2 %last.1 = f32[3,3,3,128]{3,2,1,0:T(4,128)} custom-call(s32[4]{0:T(128)S(1)} %add_convert_fusion.place, f32[3,3,8,128]{3,2,1,0:T(8,128)S(1)} %get-tuple-element.101.mine, f32[3,1,8,128]{3,2,1,0:T(8,128)S(1)} %collective-permute-done.18.mate, f32[3,1,8,128]{3,2,1,0:T(8,128)S(1)} %collective-permute-done.19.other), custom_call_target="tpu_custom_call" | custom-call | flops 1000 | bytes 1000 | tf_op jit(solution)/shard_map/last/pallas_call | solution.py:61
  (4 shorter events, 0.0 us)
Async XLA Ops:
  0.6 11.0 %collective-permute-start = (bf16[3,3,128,128]{3,2,1,0:T(8,128)(2,1)}, bf16[3,3,128,128]{3,2,1,0:T(8,128)(2,1)S(1)}, u32[]{:S(2)}, u32[]{:S(2)}) collective-permute-start(bf16[3,3,128,128]{3,2,1,0:T(8,128)(2,1)} %own.3), channel_id=1, source_target_pairs={{0,8},{8,16},{16,24},{24,0},{1,9},{9,17},{17,25},{25,1},{2,10},{10... | collective-permute-start | bytes 884744 | tf_op jit(solution)/shard_map/ppermute | solution.py:18
  1.9 15.8 %collective-permute-start.1 = (bf16[3,3,128,128]{3,2,1,0:T(8,128)(2,1)}, bf16[3,3,128,128]{3,2,1,0:T(8,128)(2,1)S(1)}, u32[]{:S(2)}, u32[]{:S(2)}) collective-permute-start(bf16[3,3,128,128]{3,2,1,0:T(8,128)(2,1)} %own.3), channel_id=1, source_target_pairs={{0,24},{8,0},{16,8},{24,16},{1,25},{9,1},{17,9},{25,17},{2,26},{10... | collective-permute-start | bytes 884744 | tf_op jit(solution)/shard_map/ppermute | solution.py:18
  2.2 15.6 %collective-permute-start.4 = (bf16[3,3,128,128]{3,2,1,0:T(8,128)(2,1)}, bf16[3,3,128,128]{3,2,1,0:T(8,128)(2,1)S(1)}, u32[]{:S(2)}, u32[]{:S(2)}) collective-permute-start(bf16[3,3,128,128]{3,2,1,0:T(8,128)(2,1)} %own.3), channel_id=1, source_target_pairs={{0,1},{1,0},{2,3},{3,2},{4,5},{5,4},{6,7},{7,6},{8,9},{9,8},{10,11... | collective-permute-start | bytes 884744 | tf_op jit(solution)/shard_map/ppermute | solution.py:27
  3.4 17.3 %collective-permute-start.5 = (bf16[3,3,128,128]{3,2,1,0:T(8,128)(2,1)}, bf16[3,3,128,128]{3,2,1,0:T(8,128)(2,1)S(1)}, u32[]{:S(2)}, u32[]{:S(2)}) collective-permute-start(bf16[3,3,128,128]{3,2,1,0:T(8,128)(2,1)} %own.3), channel_id=1, source_target_pairs={{1,2},{2,1},{3,4},{4,3},{5,6},{6,5},{9,10},{10,9},{11,12},{12,11},... | collective-permute-start | bytes 884744 | tf_op jit(solution)/shard_map/ppermute | solution.py:28
  11.7 6.1 %copy-start.7 = (bf16[2,3,96,128]{3,2,1,0:T(8,128)(2,1)}, bf16[2,3,96,128]{3,2,1,0:T(8,128)(2,1)S(1)}, u32[]{:S(2)}) copy-start(bf16[2,3,96,128]{3,2,1,0:T(8,128)(2,1)S(1)} %get-tuple-element.65) | copy-start | bytes 442372
  11.7 11.1 %collective-permute-start.6 = (bf16[3,3,128,128]{3,2,1,0:T(8,128)(2,1)S(1)}, bf16[3,3,128,128]{3,2,1,0:T(8,128)(2,1)S(1)}, u32[]{:S(2)}, u32[]{:S(2)}) collective-permute-start(bf16[3,3,128,128]{3,2,1,0:T(8,128)(2,1)S(1)} %collective-permute-done.low), channel_id=1, source_target_pairs={{0,1},{1,0},{2,3},{3,2},{4,5},{5,4},{6,7},{7,6},{8,9},{9,8},{10,11... | collective-permute-start | bytes 884744 | tf_op jit(solution)/shard_map/ppermute | solution.py:27
  11.8 14.2 %collective-permute-start.7 = (bf16[3,3,128,128]{3,2,1,0:T(8,128)(2,1)S(1)}, bf16[3,3,128,128]{3,2,1,0:T(8,128)(2,1)S(1)}, u32[]{:S(2)}, u32[]{:S(2)}) collective-permute-start(bf16[3,3,128,128]{3,2,1,0:T(8,128)(2,1)S(1)} %collective-permute-done.low), channel_id=1, source_target_pairs={{1,2},{2,1},{3,4},{4,3},{5,6},{6,5},{9,10},{10,9},{11,12},{12,11},... | collective-permute-start | bytes 884744 | tf_op jit(solution)/shard_map/ppermute | solution.py:28
  17.7 8.2 %collective-permute-start.8 = (bf16[3,3,128,128]{3,2,1,0:T(8,128)(2,1)S(1)}, bf16[3,3,128,128]{3,2,1,0:T(8,128)(2,1)S(1)}, u32[]{:S(2)}, u32[]{:S(2)}) collective-permute-start(bf16[3,3,128,128]{3,2,1,0:T(8,128)(2,1)S(1)} %collective-permute-done.1.high), channel_id=1, source_target_pairs={{0,1},{1,0},{2,3},{3,2},{4,5},{5,4},{6,7},{7,6},{8,9},{9,8},{10,11... | collective-permute-start | bytes 884744 | tf_op jit(solution)/shard_map/ppermute | solution.py:27
  17.8 8.3 %collective-permute-start.9 = (bf16[3,3,128,128]{3,2,1,0:T(8,128)(2,1)S(1)}, bf16[3,3,128,128]{3,2,1,0:T(8,128)(2,1)S(1)}, u32[]{:S(2)}, u32[]{:S(2)}) collective-permute-start(bf16[3,3,128,128]{3,2,1,0:T(8,128)(2,1)S(1)} %collective-permute-done.1.high), channel_id=1, source_target_pairs={{1,2},{2,1},{3,4},{4,3},{5,6},{6,5},{9,10},{10,9},{11,12},{12,11},... | collective-permute-start | bytes 884744 | tf_op jit(solution)/shard_map/ppermute | solution.py:28
  20.7 10.5 %collective-permute-start.2 = (bf16[2,3,96,128]{3,2,1,0:T(8,128)(2,1)}, bf16[2,3,96,128]{3,2,1,0:T(8,128)(2,1)S(1)}, u32[]{:S(2)}, u32[]{:S(2)}) collective-permute-start(bf16[2,3,96,128]{3,2,1,0:T(8,128)(2,1)} %copy-done.7), channel_id=1, source_target_pairs={{0,8},{8,16},{16,24},{24,0},{1,9},{9,17},{17,25},{25,1},{2,10},{10... | collective-permute-start | bytes 442376 | tf_op jit(solution)/shard_map/ppermute | solution.py:18
  22.8 8.5 %collective-permute-start.3 = (bf16[2,3,96,128]{3,2,1,0:T(8,128)(2,1)S(1)}, bf16[2,3,96,128]{3,2,1,0:T(8,128)(2,1)S(1)}, u32[]{:S(2)}, u32[]{:S(2)}) collective-permute-start(bf16[2,3,96,128]{3,2,1,0:T(8,128)(2,1)S(1)} %get-tuple-element.66), channel_id=1, source_target_pairs={{0,24},{8,0},{16,8},{24,16},{1,25},{9,1},{17,9},{25,17},{2,26},{10... | collective-permute-start | bytes 442376 | tf_op jit(solution)/shard_map/ppermute | solution.py:18
  29.0 14.0 %copy-start.2 = (bf16[288,896]{1,0:T(8,128)(2,1)S(1)}, bf16[288,896]{1,0:T(8,128)(2,1)}, u32[]{:S(2)}) copy-start(bf16[288,896]{1,0:T(8,128)(2,1)} %get-tuple-element.80.a_re) | copy-start | bytes 1548292
  29.0 14.0 %copy-start.3 = (bf16[288,896]{1,0:T(8,128)(2,1)S(1)}, bf16[288,896]{1,0:T(8,128)(2,1)}, u32[]{:S(2)}) copy-start(bf16[288,896]{1,0:T(8,128)(2,1)} %get-tuple-element.79.a_up) | copy-start | bytes 1548292
  29.0 10.3 %collective-permute-start.12 = (bf16[2,3,96,128]{3,2,1,0:T(8,128)(2,1)S(1)}, bf16[2,3,96,128]{3,2,1,0:T(8,128)(2,1)S(1)}, u32[]{:S(2)}, u32[]{:S(2)}) collective-permute-start(bf16[2,3,96,128]{3,2,1,0:T(8,128)(2,1)S(1)} %get-tuple-element.85), channel_id=1, source_target_pairs={{0,8},{8,16},{16,24},{24,0},{1,9},{9,17},{17,25},{25,1},{2,10},{10... | collective-permute-start | bytes 442376 | tf_op jit(solution)/shard_map/ppermute | solution.py:18
  31.3 8.0 %collective-permute-start.13 = (bf16[2,3,96,128]{3,2,1,0:T(8,128)(2,1)S(1)}, bf16[2,3,96,128]{3,2,1,0:T(8,128)(2,1)S(1)}, u32[]{:S(2)}, u32[]{:S(2)}) collective-permute-start(bf16[2,3,96,128]{3,2,1,0:T(8,128)(2,1)S(1)} %get-tuple-element.89), channel_id=1, source_target_pairs={{0,24},{8,0},{16,8},{24,16},{1,25},{9,1},{17,9},{25,17},{2,26},{10... | collective-permute-start | bytes 442376 | tf_op jit(solution)/shard_map/ppermute | solution.py:18
  31.9 11.1 %collective-permute-start.10 = (bf16[7,2,96,128]{3,2,1,0:T(8,128)(2,1)S(1)}, bf16[7,2,96,128]{3,2,1,0:T(8,128)(2,1)S(1)}, u32[]{:S(2)}, u32[]{:S(2)}) collective-permute-start(bf16[7,2,96,128]{3,2,1,0:T(8,128)(2,1)S(1)} %get-tuple-element.77), channel_id=1, source_target_pairs={{0,1},{1,0},{2,3},{3,2},{4,5},{5,4},{6,7},{7,6},{8,9},{9,8},{10,11... | collective-permute-start | bytes 1032200 | tf_op jit(solution)/shard_map/ppermute | solution.py:27
  32.4 10.5 %collective-permute-start.11 = (bf16[7,2,96,128]{3,2,1,0:T(8,128)(2,1)S(1)}, bf16[7,2,96,128]{3,2,1,0:T(8,128)(2,1)S(1)}, u32[]{:S(2)}, u32[]{:S(2)}) collective-permute-start(bf16[7,2,96,128]{3,2,1,0:T(8,128)(2,1)S(1)} %get-tuple-element.78), channel_id=1, source_target_pairs={{1,2},{2,1},{3,4},{4,3},{5,6},{6,5},{9,10},{10,9},{11,12},{12,11},... | collective-permute-start | bytes 1032200 | tf_op jit(solution)/shard_map/ppermute | solution.py:28
  39.9 8.8 %copy-start = (bf16[288,896]{1,0:T(8,128)(2,1)S(1)}, bf16[288,896]{1,0:T(8,128)(2,1)}, u32[]{:S(2)}) copy-start(bf16[288,896]{1,0:T(8,128)(2,1)} %get-tuple-element.93.a_re) | copy-start | bytes 1548292
  39.9 8.8 %copy-start.1 = (bf16[288,896]{1,0:T(8,128)(2,1)S(1)}, bf16[288,896]{1,0:T(8,128)(2,1)}, u32[]{:S(2)}) copy-start(bf16[288,896]{1,0:T(8,128)(2,1)} %get-tuple-element.92.a_up) | copy-start | bytes 1548292
  39.9 8.8 %copy-start.4 = (bf16[288,896]{1,0:T(8,128)(2,1)S(1)}, bf16[288,896]{1,0:T(8,128)(2,1)}, u32[]{:S(2)}) copy-start(bf16[288,896]{1,0:T(8,128)(2,1)} %get-tuple-element.94.a_ca_old) | copy-start | bytes 1548292
  39.9 8.8 %copy-start.5 = (bf16[288,896]{1,0:T(8,128)(2,1)S(1)}, bf16[288,896]{1,0:T(8,128)(2,1)}, u32[]{:S(2)}) copy-start(bf16[288,896]{1,0:T(8,128)(2,1)} %get-tuple-element.95.a_ca_new) | copy-start | bytes 1548292
  39.9 8.8 %copy-start.6 = (bf16[216,96]{1,0:T(8,128)(2,1)S(1)}, bf16[216,96]{1,0:T(8,128)(2,1)}, u32[]{:S(2)}) copy-start(bf16[216,96]{1,0:T(8,128)(2,1)} %get-tuple-element.96.head) | copy-start | bytes 124420
  39.9 7.6 %collective-permute-start.14 = (bf16[7,2,96,128]{3,2,1,0:T(8,128)(2,1)S(1)}, bf16[7,2,96,128]{3,2,1,0:T(8,128)(2,1)S(1)}, u32[]{:S(2)}, u32[]{:S(2)}) collective-permute-start(bf16[7,2,96,128]{3,2,1,0:T(8,128)(2,1)S(1)} %get-tuple-element.90), channel_id=1, source_target_pairs={{0,1},{1,0},{2,3},{3,2},{4,5},{5,4},{6,7},{7,6},{8,9},{9,8},{10,11... | collective-permute-start | bytes 1032200 | tf_op jit(solution)/shard_map/ppermute | solution.py:27
  40.0 8.7 %collective-permute-start.15 = (bf16[7,2,96,128]{3,2,1,0:T(8,128)(2,1)S(1)}, bf16[7,2,96,128]{3,2,1,0:T(8,128)(2,1)S(1)}, u32[]{:S(2)}, u32[]{:S(2)}) collective-permute-start(bf16[7,2,96,128]{3,2,1,0:T(8,128)(2,1)S(1)} %get-tuple-element.91), channel_id=1, source_target_pairs={{1,2},{2,1},{3,4},{4,3},{5,6},{6,5},{9,10},{10,9},{11,12},{12,11},... | collective-permute-start | bytes 1032200 | tf_op jit(solution)/shard_map/ppermute | solution.py:28
  55.6 3.5 %collective-permute-start.16 = (f32[1,5,8,128]{3,2,1,0:T(8,128)S(1)}, f32[1,5,8,128]{3,2,1,0:T(8,128)S(1)}, u32[]{:S(2)}, u32[]{:S(2)}) collective-permute-start(f32[1,5,8,128]{3,2,1,0:T(8,128)S(1)} %get-tuple-element.99), channel_id=1, source_target_pairs={{0,8},{8,16},{16,24},{24,0},{1,9},{9,17},{17,25},{25,1},{2,10},{10... | collective-permute-start | bytes 61448 | tf_op jit(solution)/shard_map/ppermute | solution.py:18
  58.2 3.5 %collective-permute-start.17 = (f32[1,5,8,128]{3,2,1,0:T(8,128)S(1)}, f32[1,5,8,128]{3,2,1,0:T(8,128)S(1)}, u32[]{:S(2)}, u32[]{:S(2)}) collective-permute-start(f32[1,5,8,128]{3,2,1,0:T(8,128)S(1)} %get-tuple-element.100), channel_id=1, source_target_pairs={{0,24},{8,0},{16,8},{24,16},{1,25},{9,1},{17,9},{25,17},{2,26},{10... | collective-permute-start | bytes 61448 | tf_op jit(solution)/shard_map/ppermute | solution.py:18
  62.3 4.3 %collective-permute-start.18 = (f32[3,1,8,128]{3,2,1,0:T(8,128)S(1)}, f32[3,1,8,128]{3,2,1,0:T(8,128)S(1)}, u32[]{:S(2)}, u32[]{:S(2)}) collective-permute-start(f32[3,1,8,128]{3,2,1,0:T(8,128)S(1)} %get-tuple-element.102), channel_id=1, source_target_pairs={{0,1},{1,0},{2,3},{3,2},{4,5},{5,4},{6,7},{7,6},{8,9},{9,8},{10,11... | collective-permute-start | bytes 36872 | tf_op jit(solution)/shard_map/ppermute | solution.py:27
  64.2 5.0 %collective-permute-start.19 = (f32[3,1,8,128]{3,2,1,0:T(8,128)S(1)}, f32[3,1,8,128]{3,2,1,0:T(8,128)S(1)}, u32[]{:S(2)}, u32[]{:S(2)}) collective-permute-start(f32[3,1,8,128]{3,2,1,0:T(8,128)S(1)} %get-tuple-element.103), channel_id=1, source_target_pairs={{1,2},{2,1},{3,4},{4,3},{5,6},{6,5},{9,10},{10,9},{11,12},{12,11},... | collective-permute-start | bytes 36872 | tf_op jit(solution)/shard_map/ppermute | solution.py:28

commit v2 on v1

--- a/solution.py
+++ b/solution.py
@@ -22,11 +22,19 @@
     return around(last, "gz", 1), around(first, "gz", -1)
 
 
+def rows_of_mate(to_mate):
+    count = lax.axis_size("gy")
+    return lax.ppermute(to_mate, "gy", [(i, i ^ 1) for i in range(count)])
+
+
+def rows_of_other(to_other):
+    count = lax.axis_size("gy")
+    return lax.ppermute(to_other, "gy", [(i, ((i + 1) ^ 1) - 1) for i in range(1, count - 1)])
+
+
 def rows_around(to_mate, to_other):
-    count = lax.axis_size("gy")
-    mate = lax.ppermute(to_mate, "gy", [(i, i ^ 1) for i in range(count)])
-    other = lax.ppermute(to_other, "gy", [(i, ((i + 1) ^ 1) - 1) for i in range(1, count - 1)])
-    return mate, other
+    other = rows_of_other(to_other)
+    return rows_of_mate(to_mate), other
 
 
 def edges(block, width):
@@ -338,6 +346,10 @@
     return got + [jnp.zeros((32, wide), BF16)]
 
 
+def side_by_side(field, planes, row, rows):
+    return [jnp.concatenate(parts, axis=1) for parts in zip(*[taps(field, z, row, rows) for z in planes])]
+
+
 def conv(weight, rhs, rows):
     three = jnp.dot(weight, jnp.concatenate(rhs, axis=0), preferred_element_type=F32)
     width = three.shape[0] // 3
@@ -397,80 +409,101 @@
     width = hidden.shape[2]
     up_shift, re_shift = column(small[1:2, :width]), column(small[2:3, :width])
 
-    def reset_plane(z, carry):
+    for z in range(planes + 2):
         near_out[z] = field[z + 1, :, LANES : (rows + 3) * LANES]
-        for y, got in enumerate(conv(a_re[...], taps(field, z, 0, rows + 2), rows + 2)):
-            reset_out[z, y] = got + re_shift
-        return carry
-
-    lax.fori_loop(0, planes + 2, reset_plane, 0, unroll=True)
-
-    def update_plane(z, carry):
-        for y, got in enumerate(conv(a_up[...], taps(field, z + 1, 1, rows), rows)):
-            update_out[z, y] = got + up_shift
-        return carry
-
-    lax.fori_loop(0, planes, update_plane, 0, unroll=True)
-
-
-def gru_body(
-    place, begun, small, near, update_old, reset_old, enc, ez0, ez1, e_mate, e_other, a_up, a_re, a_ca_old, a_ca_new,
-    head, state_out, part_low, part_out, part_high, field, gated, state
-):
-    planes, rows, width = enc.shape[:3]
-    fill(place, field, enc, ez0, ez1, e_mate, e_other)
+    for n, got in enumerate(conv(a_re[...], side_by_side(field, range(planes + 2), 0, rows + 2), (planes + 2) * (rows + 2))):
+        reset_out[n // (rows + 2), n % (rows + 2)] = got + re_shift
+    for n, got in enumerate(conv(a_up[...], side_by_side(field, range(1, planes + 1), 1, rows), planes * rows)):
+        update_out[n // rows, n % rows] = got + up_shift
+
+
+def new_states(planes, rows, small, near, update_old, field, gated, a_up, a_ca_old, a_ca_new):
+    width = near.shape[1]
     ca_shift = column(small[3:4, :width])
-
-    def reset_plane(z, carry):
-        for y, got in enumerate(conv(a_re[...], taps(field, z, 0, rows + 2), rows + 2)):
-            at = slice(y * LANES, (y + 1) * LANES)
-            gate = jax.nn.sigmoid(got + reset_old[z, y])
-            gated[z, :, at] = (gate * near[z, :, at].astype(F32)).astype(BF16)
-        return carry
-
-    lax.fori_loop(0, planes + 2, reset_plane, 0, unroll=True)
-
-    def state_plane(z, carry):
-        new_taps = taps(field, z + 1, 1, rows)
-        update = conv(a_up[...], new_taps, rows)
-        both = jnp.concatenate([a_ca_old[...], a_ca_new[...]], axis=1)
-        cand = conv(both, taps(gated, z, 0, rows) + new_taps, rows)
-        for y in range(rows):
-            gate = jax.nn.sigmoid(update[y] + update_old[z, y])
-            new = jnp.tanh(cand[y] + ca_shift)
-            old = near[z + 1, :, (y + 1) * LANES : (y + 2) * LANES].astype(F32)
-            got = ((1.0 - gate) * old + gate * new).astype(BF16)
-            state_out[z, y] = got
-            state[z, :, y * LANES : (y + 1) * LANES] = got
-        return carry
-
-    lax.fori_loop(0, planes, state_plane, 0, unroll=True)
-
+    new_taps = side_by_side(field, [z + 1 for z in planes], 1, rows)
+    update = conv(a_up[...], new_taps, len(planes) * rows)
+    both = jnp.concatenate([a_ca_old[...], a_ca_new[...]], axis=1)
+    cand = conv(both, side_by_side(gated, planes, 0, rows) + new_taps, len(planes) * rows)
+    for n in range(len(planes) * rows):
+        z, y = planes[n // rows], n % rows
+        gate = jax.nn.sigmoid(update[n] + update_old[z, y])
+        new = jnp.tanh(cand[n] + ca_shift)
+        old = near[z + 1, :, (y + 1) * LANES : (y + 2) * LANES].astype(F32)
+        yield z, y, ((1.0 - gate) * old + gate * new).astype(BF16)
+
+
+def head_parts(head, state, planes, rows):
     cell = lax.broadcasted_iota(jnp.int32, (8, LANES), 1)
-    sums = {}
-    for z in range(planes):
-        prod = jnp.dot(head[...], state[z], preferred_element_type=F32)
+    sums, parts = {}, {}
+    for n, z in enumerate(planes):
+        prod = jnp.dot(head[...], state[n], preferred_element_type=F32)
         for y in range(rows):
             for a in range(3):
                 for b in range(3):
-                    key = (z + 2 - a, y + 2 - b)
                     for c in range(3):
                         t = a * 9 + b * 3 + c
                         piece = prod[t * 8 : t * 8 + 8, y * LANES : (y + 1) * LANES]
-                        slot = sums.setdefault(key, [None] * 3)
+                        slot = sums.setdefault((z + 2 - a, y + 2 - b), [None] * 3)
                         slot[c] = piece if slot[c] is None else slot[c] + piece
-    for (z, y), (before, same, after) in sums.items():
+    for key, (before, same, after) in sums.items():
         before = jnp.where(cell == 0, 0.0, pltpu.roll(before, 1, 1))
         after = jnp.where(cell == LANES - 1, 0.0, pltpu.roll(after, LANES - 1, 1))
-        total = same + before + after
-        if z == 0:
-            part_low[0, y] = total
-        elif z == planes + 1:
-            part_high[0, y] = total
-        elif 0 < y <= rows:
-            part_out[z - 1, y] = total + begun[z - 1, y - 1]
-        else:
-            part_out[z - 1, y] = total
+        parts[key] = same + before + after
+    return parts
+
+
+def outer_planes(planes):
+    return sorted({0, planes - 1})
+
+
+def gru_outer_body(
+    place, begun, small, near, update_old, reset_old, enc, ez0, ez1, e_mate, e_other, a_up, a_re, a_ca_old, a_ca_new, head,
+    part_low, part_out, part_high, field, gated, outer, state
+):
+    planes, rows = enc.shape[:2]
+    fill(place, field, enc, ez0, ez1, e_mate, e_other)
+    every = range(planes + 2)
+    for n, got in enumerate(conv(a_re[...], side_by_side(field, every, 0, rows + 2), (planes + 2) * (rows + 2))):
+        z, y = n // (rows + 2), n % (rows + 2)
+        at = slice(y * LANES, (y + 1) * LANES)
+        gate = jax.nn.sigmoid(got + reset_old[z, y])
+        gated[z, :, at] = (gate * near[z, :, at].astype(F32)).astype(BF16)
+
+    ends = outer_planes(planes)
+    for z, y, got in new_states(ends, rows, small, near, update_old, field, gated, a_up, a_ca_old, a_ca_new):
+        outer[ends.index(z), y] = got
+        state[ends.index(z), :, y * LANES : (y + 1) * LANES] = got
+
+    parts = head_parts(head, state, ends, rows)
+    for z in range(planes + 2):
+        for y in range(rows + 2):
+            total = parts.get((z, y))
+            if 0 < z <= planes and 0 < y <= rows:
+                total = begun[z - 1, y - 1] if total is None else total + begun[z - 1, y - 1]
+            if total is None:
+                total = jnp.zeros(part_out.shape[2:], F32)
+            if z == 0:
+                part_low[0, y] = total
+            elif z == planes + 1:
+                part_high[0, y] = total
+            else:
+                part_out[z - 1, y] = total
+
+
+def gru_inner_body(
+    small, near, update_old, field, gated, a_up, a_ca_old, a_ca_new, head, part, outer, state_out, part_out, state
+):
+    planes, rows = state_out.shape[:2]
+    ends = outer_planes(planes)
+    inner = [z for z in range(planes) if z not in ends]
+    for n, z in enumerate(ends):
+        state_out[z] = outer[n]
+    part_out[...] = part[...]
+    for z, y, got in new_states(inner, rows, small, near, update_old, field, gated, a_up, a_ca_old, a_ca_new):
+        state_out[z, y] = got
+        state[inner.index(z), :, y * LANES : (y + 1) * LANES] = got
+    for (z, y), total in head_parts(head, state, inner, rows).items():
+        part_out[z - 1, y] = part[z - 1, y] + total
 
 
 def mix_body(place, part, low, high, mine, to_mate, to_other):
@@ -491,20 +524,6 @@
             mine[z, y] = added(z, y + 1)
         to_mate[z, 0] = added(z, mate_at)
         to_other[z, 0] = added(z, other_at)
-
-
-def last_body(place, mine, mate, other, out):
-    planes, rows, outs = out.shape[:3]
-    odd = place[3]
-    for z in range(planes):
-        for y in range(rows):
-            out[z, y] = mine[z, y, :outs]
-        mate_at, other_at = (rows - 1) * (1 - odd), (rows - 1) * odd
-        out[z, mate_at] = out[z, mate_at] + mate[z, 0, :outs]
-
-        @pl.when(place[2] == 1)
-        def _():
-            out[z, other_at] = out[z, other_at] + other[z, 0, :outs]
 
 
 def on_device(
@@ -517,7 +536,8 @@
     place = inside()
 
     t_low, t_high = planes_around(target[:3], target[-3:])
-    t_mate, t_other = rows_around(*edges(target, 3))
+    to_mate, to_other = edges(target, 3)
+    t_other = rows_of_other(to_other)
 
     target_rows = pltpu.VMEM((rows + 6, planes + 6, LANES, channels), BF16)
     made = jax.ShapeDtypeStruct
@@ -537,7 +557,8 @@
         14,
         from_hbm=(pltpu.HBM,) * 2 + (pltpu.VMEM,) * 11,
     )
-    t_low, own = lax.optimization_barrier((t_low, own))
+    t_low, to_mate, own = lax.optimization_barrier((t_low, to_mate, own))
+    t_mate = rows_of_mate(to_mate)
     t_low_mate, t_low_other = rows_around(*edges(t_low, 3))
     update_here, t_low = lax.optimization_barrier((update_here, t_low))
     up_old, up_new = call(
@@ -592,22 +613,27 @@
     e_mate, e_other = rows_around(*rows_of(place, e_low, enc, e_high, 2, "pack_encoded"))
 
     ring = lambda n: jax.ShapeDtypeStruct((n, rows + 2, 8, cells), F32)
-    state_out, part_low, part, part_high = call(
-        gru_body,
-        (jax.ShapeDtypeStruct((planes, rows, width, cells), BF16), ring(1), ring(planes), ring(1)),
-        [
-            field,
-            pltpu.VMEM((planes + 2, width, (rows + 2) * LANES), BF16),
-            pltpu.VMEM((planes, width, wide), BF16),
-        ],
+    ends = len(outer_planes(planes))
+    part_low, part, part_high, e_field, gated, outer = call(
+        gru_outer_body,
+        (ring(1), ring(planes), ring(1), made(field.shape, BF16))
+        + (made((planes + 2, width, (rows + 2) * LANES), BF16), made((ends, rows, width, cells), BF16)),
+        [pltpu.VMEM((ends, width, wide), BF16)],
         (begun, small, near, update_old, reset_old, enc, e_low, e_high, e_mate, e_other)
         + (up_new, re_new, ca_old, ca_new, head),
-        "gru",
+        "gru_outer",
         12,
         place,
-        kept=False,
     )
     low, high = planes_around(part_low, part_high)
+    state_out, part = call(
+        gru_inner_body,
+        (pltpu.HBM(hidden.shape, BF16), ring(planes)),
+        [pltpu.VMEM((planes - ends, width, wide), BF16)],
+        (small, near, update_old, e_field, gated, up_new, ca_old, ca_new, head, part, outer),
+        "gru_inner",
+        12,
+    )
     row = jax.ShapeDtypeStruct((planes, 1, 8, cells), F32)
     mine, to_mate, to_other = call(
         mix_body,
@@ -619,16 +645,12 @@
         place,
     )
     mate, other = rows_around(to_mate, to_other)
-    motion_out = call(
-        last_body,
-        jax.ShapeDtypeStruct(motion.shape, F32),
-        [],
-        (mine, mate, other),
-        "last",
-        4,
-        place,
-        kept=False,
-    )
+    other = jnp.where(place[2] == 1, other, 0.0)
+    odd = place[3] == 1
+    below, above = jnp.where(odd, mate, other), jnp.where(odd, other, mate)
+    row = lax.broadcasted_iota(jnp.int32, mine.shape, 1)
+    total = mine + jnp.where(row == 0, below, 0.0) + jnp.where(row == rows - 1, above, 0.0)
+    motion_out = total[:, :, : motion.shape[2]]
     return state_out, motion_out
 
 

time: 70.7 us -> 68.6 us (0.970)
  waiting for transfers between devices: 7.42 us -> 3.43 us
  between operations: 0.96 us -> 2.27 us
  Pallas kernels: 31.5 us -> 30.2 us
    ppermute x8, waiting for transfers between devices: 3.54 us -> 0.92 us  [around(): lax.ppermute(block, axis, [(i, (i + step) % count) for i in range(count)])]
    ppermute x12, waiting for transfers between devices: 3.87 us -> 2.51 us  [the longest x6 2.49 us: rows_of_other(): lax.ppermute(to_other, 'gy', [(i, (i + 1 ^ 1) - 1) for i in range(1, coun...]
    pallas_call x11, Pallas kernels: 31.5 us -> 30.2 us  [call(): pl.pallas_call(body, out_shape=jax.tree.map(lambda o: pltpu.VMEM(o.shape,...]
  transfers between devices with their start and end apart: 20 -> 20, of which waited for: 5 -> 3; matrix products, arithmetic and copies ran while one was open for 0% -> 1% of each run, Pallas kernels for 33% -> 36%
where the time goes in v2:
time: 68.6 us; the launch traced here: 68.2 us
  starting transfers between devices  30.9 us (45%)
  Pallas kernels  30.2 us (44%)
  waiting for transfers between devices  3.43 us (5%)
  between operations  2.27 us (3%)
  other arithmetic  0.77 us (1%)
    pallas_call x11, Pallas kernels, call(): pl.pallas_call(body, out_shape=jax.tree.map(lambda o: pltpu.VMEM(o.shape,...  30.2 us
    ppermute x6, starting transfers between devices, rows_of_other(): lax.ppermute(to_other, 'gy', [(i, (i + 1 ^ 1) - 1) for i in range(1, coun...  19.5 us
    ppermute x8, starting transfers between devices, around(): lax.ppermute(block, axis, [(i, (i + step) % count) for i in range(count)])  8.4 us
    ppermute x6, starting transfers between devices, rows_of_mate(): return lax.ppermute(to_mate, 'gy', [(i, i ^ 1) for i in range(count)])  3.03 us
    ppermute x6, waiting for transfers between devices, rows_of_other(): lax.ppermute(to_other, 'gy', [(i, (i + 1 ^ 1) - 1) for i in range(1, coun...  2.49 us
  transfers between devices with their start and end apart: 20, of which 3 were waited for; matrix products, arithmetic and copies ran while one was open for 1% of the time, Pallas kernels for 36%

profile of v2, /device:TPU:11, one launch (start us, length us, event | category | flops | bytes accessed | tf_op | source)
XLA Modules:
  0.0 68.2 jit_solution(6760202376208262914)
XLA Ops:
  0.6 1.3 %collective-permute-start = (bf16[3,3,128,128]{3,2,1,0:T(8,128)(2,1)}, bf16[3,3,128,128]{3,2,1,0:T(8,128)(2,1)S(1)}, u32[]{:S(2)}, u32[]{:S(2)}) collective-permute-start(bf16[3,3,128,128]{3,2,1,0:T(8,128)(2,1)} %own.3), channel_id=1, source_target_pairs={{0,8},{8,16},{16,24},{24,0},{1,9},{9,17},{17,25},{25,1},{2,10},{10... | collective-permute-start | bytes 884744 | tf_op jit(solution)/shard_map/ppermute | solution.py:18
  1.9 0.3 collective-permute-start.1
  2.2 4.3 %collective-permute-start.5 = (bf16[3,3,128,128]{3,2,1,0:T(8,128)(2,1)}, bf16[3,3,128,128]{3,2,1,0:T(8,128)(2,1)S(1)}, u32[]{:S(2)}, u32[]{:S(2)}) collective-permute-start(bf16[3,3,128,128]{3,2,1,0:T(8,128)(2,1)} %own.3), channel_id=1, source_target_pairs={{1,2},{2,1},{3,4},{4,3},{5,6},{6,5},{9,10},{10,9},{11,12},{12,11},... | collective-permute-start | bytes 884744 | tf_op jit(solution)/shard_map/ppermute | solution.py:32
  6.5 5.1 %own.2 = (f32[81,8,128]{2,1,0:T(8,128)S(1)}, bf16[96,392]{1,0:T(8,128)(2,1)S(1)}, bf16[2,3,96,128]{3,2,1,0:T(8,128)(2,1)S(1)}, bf16[2,3,96,128]{3,2,1,0:T(8,128)...) custom-call(bf16[27,18432]{1,0:T(8,128)(2,1)} %w_reset.1, ...), custom_call_target="tpu_custom_call" | custom-call | flops 1000 | bytes 1000 | tf_op jit(solution)/shard_map/own/pallas_call | solution.py:69
  11.6 0.0 copy-start.7
  11.6 0.0 collective-permute-done.low
  11.6 0.1 collective-permute-start.4
  11.7 0.5 collective-permute-start.6
  12.2 3.2 %collective-permute-start.7 = (bf16[3,3,128,128]{3,2,1,0:T(8,128)(2,1)S(1)}, bf16[3,3,128,128]{3,2,1,0:T(8,128)(2,1)S(1)}, u32[]{:S(2)}, u32[]{:S(2)}) collective-permute-start(bf16[3,3,128,128]{3,2,1,0:T(8,128)(2,1)S(1)} %collective-permute-done.low), channel_id=1, source_target_pairs={{1,2},{2,1},{3,4},{4,3},{5,6},{6,5},{9,10},{10,9},{11,12},{12,11},... | collective-permute-start | bytes 884744 | tf_op jit(solution)/shard_map/ppermute | solution.py:32
  15.4 2.4 %lay_out_update.1 = (bf16[288,896]{1,0:T(8,128)(2,1)}, bf16[288,896]{1,0:T(8,128)(2,1)}) custom-call(bf16[27,18432]{1,0:T(8,128)(2,1)S(1)} %get-tuple-element.66.weight), custom_call_target="tpu_custom_call" | custom-call | flops 1000 | bytes 1000 | tf_op jit(solution)/shard_map/lay_out_update/pallas_call | solution.py:69
  17.8 0.0 collective-permute-done.1.high
  17.8 0.0 collective-permute-start.8
  17.8 0.0 collective-permute-done.5.other
  17.8 0.0 copy-done.7
  17.8 3.3 %collective-permute-start.9 = (bf16[3,3,128,128]{3,2,1,0:T(8,128)(2,1)S(1)}, bf16[3,3,128,128]{3,2,1,0:T(8,128)(2,1)S(1)}, u32[]{:S(2)}, u32[]{:S(2)}) collective-permute-start(bf16[3,3,128,128]{3,2,1,0:T(8,128)(2,1)S(1)} %collective-permute-done.1.high), channel_id=1, source_target_pairs={{1,2},{2,1},{3,4},{4,3},{5,6},{6,5},{9,10},{10,9},{11,12},{12,11},... | collective-permute-start | bytes 884744 | tf_op jit(solution)/shard_map/ppermute | solution.py:32
  21.1 0.0 collective-permute-done.4.mate
  21.1 2.2 %collective-permute-start.2 = (bf16[2,3,96,128]{3,2,1,0:T(8,128)(2,1)}, bf16[2,3,96,128]{3,2,1,0:T(8,128)(2,1)S(1)}, u32[]{:S(2)}, u32[]{:S(2)}) collective-permute-start(bf16[2,3,96,128]{3,2,1,0:T(8,128)(2,1)} %copy-done.7), channel_id=1, source_target_pairs={{0,8},{8,16},{16,24},{24,0},{1,9},{9,17},{17,25},{25,1},{2,10},{10... | collective-permute-start | bytes 442376 | tf_op jit(solution)/shard_map/ppermute | solution.py:18
  23.3 0.0 collective-permute-done.6.low_mate
  23.3 0.0 collective-permute-start.3
  23.3 0.1 add_convert_fusion.place
  23.4 3.1 %face.1.face_pairs = f32[216,8,128]{2,1,0:T(8,128)S(1)} custom-call(s32[4]{0:T(128)S(1)} %add_convert_fusion.place, bf16[3,128,384]{2,1,0:T(8,128)(2,1)S(1)} %get-tuple-element.71.s_flat, bf16[3,3,128,128]{3,2,1,0:T(8,128)(2,1)S(1)} %collective-permute-done.low, bf16[3,3,128,128]{3,2,1,0:T(8,128)(2,1)S(1)} %collective-permute-done.1.high, ...), custom_call_target="tpu_custom_call" | custom-call | flops 1000 | bytes 1000 | tf_op jit(solution)/shard_map/face/pallas_call | solution.py:69
  26.4 0.0 collective-permute-done.7.low_other
  26.5 0.0 collective-permute-done.8.high_mate
  26.5 0.0 collective-permute-done.9.high_other
  26.5 2.9 %corner.1 = (bf16[3,3,96,128]{3,2,1,0:T(8,128)(2,1)S(1)}, bf16[2,3,96,128]{3,2,1,0:T(8,128)(2,1)S(1)}, bf16[2,3,96,128]{3,2,1,0:T(8,128)(2,1)S(1)}) custom-call(s32[4]{0:T(128)S(1)} %add_convert_fusion.place, bf16[3,128,384]{2,1,0:T(8,128)(2,1)S(1)} %get-tuple-element.71.s_flat, f32[3,3,3,128]{3,2,1,0:T(4,128)S(1)} %get-tuple-element.72.motion, ...), custom_call_target="tpu_custom_call" | custom-call | flops 1000 | bytes 1000 | tf_op jit(solution)/shard_map/corner/pallas_call | solution.py:69
  29.4 0.0 copy-start.4
  29.4 0.0 copy-start.5
  29.4 2.4 %collective-permute-start.12 = (bf16[2,3,96,128]{3,2,1,0:T(8,128)(2,1)S(1)}, bf16[2,3,96,128]{3,2,1,0:T(8,128)(2,1)S(1)}, u32[]{:S(2)}, u32[]{:S(2)}) collective-permute-start(bf16[2,3,96,128]{3,2,1,0:T(8,128)(2,1)S(1)} %get-tuple-element.91), channel_id=1, source_target_pairs={{0,8},{8,16},{16,24},{24,0},{1,9},{9,17},{17,25},{25,1},{2,10},{10... | collective-permute-start | bytes 442376 | tf_op jit(solution)/shard_map/ppermute | solution.py:18
  31.8 0.0 collective-permute-start.13
  31.8 0.0 collective-permute-done.2.low.hz0
  31.8 0.0 collective-permute-done.3.high.hz1
  31.8 0.6 pack_hidden.1
  32.4 0.1 collective-permute-start.10
  32.5 3.1 %collective-permute-start.11 = (bf16[7,2,96,128]{3,2,1,0:T(8,128)(2,1)S(1)}, bf16[7,2,96,128]{3,2,1,0:T(8,128)(2,1)S(1)}, u32[]{:S(2)}, u32[]{:S(2)}) collective-permute-start(bf16[7,2,96,128]{3,2,1,0:T(8,128)(2,1)S(1)} %get-tuple-element.83), channel_id=1, source_target_pairs={{1,2},{2,1},{3,4},{4,3},{5,6},{6,5},{9,10},{10,9},{11,12},{12,11},... | collective-permute-start | bytes 1032200 | tf_op jit(solution)/shard_map/ppermute | solution.py:32
  35.6 3.7 %lay_out_cand.1 = (bf16[288,896]{1,0:T(8,128)(2,1)}, bf16[288,896]{1,0:T(8,128)(2,1)}, bf16[216,96]{1,0:T(8,128)(2,1)}) custom-call(bf16[27,18432]{1,0:T(8,128)(2,1)} %weight.1, bf16[3,27,96]{2,1,0:T(8,128)(2,1)} %bitcast.17), custom_call_target="tpu_custom_call" | custom-call | flops 1000 | bytes 1000 | tf_op jit(solution)/shard_map/lay_out_cand/pallas_call | solution.py:69
  39.3 0.0 collective-permute-done.12.low.ez0
  39.3 0.0 collective-permute-done.13.high.ez1
  39.3 0.6 pack_encoded.1
  39.9 0.0 copy-start
  39.9 0.0 copy-start.1
  39.9 0.0 copy-start.2
  40.0 0.0 copy-start.3
  40.0 0.0 copy-start.6
  40.0 0.5 collective-permute-start.14
  40.5 2.8 %collective-permute-start.15 = (bf16[7,2,96,128]{3,2,1,0:T(8,128)(2,1)S(1)}, bf16[7,2,96,128]{3,2,1,0:T(8,128)(2,1)S(1)}, u32[]{:S(2)}, u32[]{:S(2)}) collective-permute-start(bf16[7,2,96,128]{3,2,1,0:T(8,128)(2,1)S(1)} %get-tuple-element.97), channel_id=1, source_target_pairs={{1,2},{2,1},{3,4},{4,3},{5,6},{6,5},{9,10},{10,9},{11,12},{12,11},... | collective-permute-start | bytes 1032200 | tf_op jit(solution)/shard_map/ppermute | solution.py:32
  43.3 0.0 collective-permute-done.10.h_mate
  43.3 0.0 collective-permute-done.11.h_other
  43.3 0.0 copy-done.4
  43.4 4.2 %old.1 = (f32[3,3,96,128]{3,2,1,0:T(8,128)S(1)}, f32[5,5,96,128]{3,2,1,0:T(8,128)S(1)}, bf16[5,96,640]{2,1,0:T(8,128)(2,1)S(1)}) custom-call(s32[4]{0:T(128)S(1)} %add_convert_fusion.place, bf16[3,3,96,128]{3,2,1,0:T(8,128)(2,1)S(1)} %get-tuple-element.59.own.hidden, f32[8,128]{1,0:T(8,128)S(1)} %get-tuple-element.58.small, ...), custom_call_target="tpu_custom_call" | custom-call | flops 1000 | bytes 1000 | tf_op jit(solution)/shard_map/old/pallas_call | solution.py:69
  47.6 0.0 collective-permute-done.14.e_mate
  47.6 1.6 %collective-permute-done.15.e_other = bf16[7,2,96,128]{3,2,1,0:T(8,128)(2,1)S(1)} collective-permute-done((bf16[7,2,96,128]{3,2,1,0:T(8,128)(2,1)S(1)}, bf16[7,2,96,128]{3,2,1,0:T(8,128)(2,1)S(1)}, u32[]{:S(2)}, u32[]{:S(2)}) %collective-permute-start.15) | collective-permute-done | bytes 344096 | tf_op jit(solution)/shard_map/ppermute | solution.py:32
  49.2 5.1 %gru_outer.1 = (f32[1,5,8,128]{3,2,1,0:T(8,128)S(1)}, f32[3,5,8,128]{3,2,1,0:T(8,128)S(1)}, f32[1,5,8,128]{3,2,1,0:T(8,128)S(1)}, bf16[7,96,896]{2,1,0:T(8,128)(...) custom-call(s32[4]{0:T(128)S(1)} %add_convert_fusion.place, ...), custom_call_target="tpu_custom_call" | custom-call | flops 1000 | bytes 1000 | tf_op jit(solution)/shard_map/gru_outer/pallas_call | solution.py:69
  54.3 2.3 %collective-permute-start.16 = (f32[1,5,8,128]{3,2,1,0:T(8,128)S(1)}, f32[1,5,8,128]{3,2,1,0:T(8,128)S(1)}, u32[]{:S(2)}, u32[]{:S(2)}) collective-permute-start(f32[1,5,8,128]{3,2,1,0:T(8,128)S(1)} %get-tuple-element.109), channel_id=1, source_target_pairs={{0,8},{8,16},{16,24},{24,0},{1,9},{9,17},{17,25},{25,1},{2,10},{10... | collective-permute-start | bytes 61448 | tf_op jit(solution)/shard_map/ppermute | solution.py:18
  56.6 0.0 collective-permute-start.17
  56.6 0.6 fusion.1
  57.2 2.0 %gru_inner.1 = (bf16[3,3,96,128]{3,2,1,0:T(8,128)(2,1)}, f32[3,5,8,128]{3,2,1,0:T(8,128)S(1)}) custom-call(f32[8,128]{1,0:T(8,128)S(1)} %get-tuple-element.58.small, bf16[5,96,640]{2,1,0:T(8,128)(2,1)S(1)} %get-tuple-element.86.near, f32[3,3,96,128]{3,2,1,0:T(8,128)S(1)} %get-tuple-element.87.update_old, bf16[7,96,896]{2,1,0:T(8,128)(2,1)S(1)} %get-tuple-element.103.field, ...), custom_call_target="tpu_custom_call" | custom-call | flops 1000 | bytes 1000 | tf_op jit(solution)/shard_map/gru_inner/pallas_call | solution.py:69
  59.2 0.0 collective-permute-done.16.low
  59.2 0.9 %collective-permute-done.17.high = f32[1,5,8,128]{3,2,1,0:T(8,128)S(1)} collective-permute-done((f32[1,5,8,128]{3,2,1,0:T(8,128)S(1)}, f32[1,5,8,128]{3,2,1,0:T(8,128)S(1)}, u32[]{:S(2)}, u32[]{:S(2)}) %collective-permute-start.17) | collective-permute-done | bytes 20512 | tf_op jit(solution)/shard_map/ppermute | solution.py:18
  60.1 0.6 mix.1
  60.7 1.8 %collective-permute-start.18 = (f32[3,1,8,128]{3,2,1,0:T(8,128)S(1)}, f32[3,1,8,128]{3,2,1,0:T(8,128)S(1)}, u32[]{:S(2)}, u32[]{:S(2)}) collective-permute-start(f32[3,1,8,128]{3,2,1,0:T(8,128)S(1)} %get-tuple-element.112), channel_id=1, source_target_pairs={{0,1},{1,0},{2,3},{3,2},{4,5},{5,4},{6,7},{7,6},{8,9},{9,8},{10,11... | collective-permute-start | bytes 36872 | tf_op jit(solution)/shard_map/ppermute | solution.py:27
  62.5 2.8 %collective-permute-start.19 = (f32[3,1,8,128]{3,2,1,0:T(8,128)S(1)}, f32[3,1,8,128]{3,2,1,0:T(8,128)S(1)}, u32[]{:S(2)}, u32[]{:S(2)}) collective-permute-start(f32[3,1,8,128]{3,2,1,0:T(8,128)S(1)} %get-tuple-element.113), channel_id=1, source_target_pairs={{1,2},{2,1},{3,4},{4,3},{5,6},{6,5},{9,10},{10,9},{11,12},{12,11},... | collective-permute-start | bytes 36872 | tf_op jit(solution)/shard_map/ppermute | solution.py:32
  66.6 0.0 collective-permute-done.18
  66.6 0.9 %collective-permute-done.19 = f32[3,1,8,128]{3,2,1,0:T(8,128)S(1)} collective-permute-done((f32[3,1,8,128]{3,2,1,0:T(8,128)S(1)}, f32[3,1,8,128]{3,2,1,0:T(8,128)S(1)}, u32[]{:S(2)}, u32[]{:S(2)}) %collective-permute-start.19) | collective-permute-done | bytes 12320 | tf_op jit(solution)/shard_map/ppermute | solution.py:32
  67.5 0.7 %fusion = f32[3,3,3,128]{3,2,1,0:T(4,128)} fusion(f32[3,3,8,128]{3,2,1,0:T(8,128)S(1)} %get-tuple-element.111, f32[3,3,128]{2,1,0:T(4,128)S(1)} %slice.14, f32[3,3,128]{2,1,0:T(4,128)S(1)} %slice.12, pred[3]{0:T(512)(128)(4,1)S(1)} %get-tuple-element.118, pred[3]{0:T(512)(128)(4,1)S(1)} %get-tuple-element.119), kind=kLoop, calls=%fused_computation.1 | loop fusion | flops 13824 | bytes 36870 | tf_op jit(solution)/shard_map/add | solution.py:652
  (10 shorter events, 0.0 us)
Async XLA Ops:
  0.6 11.0 %collective-permute-start = (bf16[3,3,128,128]{3,2,1,0:T(8,128)(2,1)}, bf16[3,3,128,128]{3,2,1,0:T(8,128)(2,1)S(1)}, u32[]{:S(2)}, u32[]{:S(2)}) collective-permute-start(bf16[3,3,128,128]{3,2,1,0:T(8,128)(2,1)} %own.3), channel_id=1, source_target_pairs={{0,8},{8,16},{16,24},{24,0},{1,9},{9,17},{17,25},{25,1},{2,10},{10... | collective-permute-start | bytes 884744 | tf_op jit(solution)/shard_map/ppermute | solution.py:18
  1.9 15.9 %collective-permute-start.1 = (bf16[3,3,128,128]{3,2,1,0:T(8,128)(2,1)}, bf16[3,3,128,128]{3,2,1,0:T(8,128)(2,1)S(1)}, u32[]{:S(2)}, u32[]{:S(2)}) collective-permute-start(bf16[3,3,128,128]{3,2,1,0:T(8,128)(2,1)} %own.3), channel_id=1, source_target_pairs={{0,24},{8,0},{16,8},{24,16},{1,25},{9,1},{17,9},{25,17},{2,26},{10... | collective-permute-start | bytes 884744 | tf_op jit(solution)/shard_map/ppermute | solution.py:18
  2.2 15.7 %collective-permute-start.5 = (bf16[3,3,128,128]{3,2,1,0:T(8,128)(2,1)}, bf16[3,3,128,128]{3,2,1,0:T(8,128)(2,1)S(1)}, u32[]{:S(2)}, u32[]{:S(2)}) collective-permute-start(bf16[3,3,128,128]{3,2,1,0:T(8,128)(2,1)} %own.3), channel_id=1, source_target_pairs={{1,2},{2,1},{3,4},{4,3},{5,6},{6,5},{9,10},{10,9},{11,12},{12,11},... | collective-permute-start | bytes 884744 | tf_op jit(solution)/shard_map/ppermute | solution.py:32
  11.6 6.2 %copy-start.7 = (bf16[2,3,96,128]{3,2,1,0:T(8,128)(2,1)}, bf16[2,3,96,128]{3,2,1,0:T(8,128)(2,1)S(1)}, u32[]{:S(2)}) copy-start(bf16[2,3,96,128]{3,2,1,0:T(8,128)(2,1)S(1)} %get-tuple-element.69) | copy-start | bytes 442372
  11.6 9.5 %collective-permute-start.4 = (bf16[3,3,128,128]{3,2,1,0:T(8,128)(2,1)}, bf16[3,3,128,128]{3,2,1,0:T(8,128)(2,1)S(1)}, u32[]{:S(2)}, u32[]{:S(2)}) collective-permute-start(bf16[3,3,128,128]{3,2,1,0:T(8,128)(2,1)} %own.3), channel_id=1, source_target_pairs={{0,1},{1,0},{2,3},{3,2},{4,5},{5,4},{6,7},{7,6},{8,9},{9,8},{10,11... | collective-permute-start | bytes 884744 | tf_op jit(solution)/shard_map/ppermute | solution.py:27
  11.7 11.6 %collective-permute-start.6 = (bf16[3,3,128,128]{3,2,1,0:T(8,128)(2,1)S(1)}, bf16[3,3,128,128]{3,2,1,0:T(8,128)(2,1)S(1)}, u32[]{:S(2)}, u32[]{:S(2)}) collective-permute-start(bf16[3,3,128,128]{3,2,1,0:T(8,128)(2,1)S(1)} %collective-permute-done.low), channel_id=1, source_target_pairs={{0,1},{1,0},{2,3},{3,2},{4,5},{5,4},{6,7},{7,6},{8,9},{9,8},{10,11... | collective-permute-start | bytes 884744 | tf_op jit(solution)/shard_map/ppermute | solution.py:27
  12.2 14.2 %collective-permute-start.7 = (bf16[3,3,128,128]{3,2,1,0:T(8,128)(2,1)S(1)}, bf16[3,3,128,128]{3,2,1,0:T(8,128)(2,1)S(1)}, u32[]{:S(2)}, u32[]{:S(2)}) collective-permute-start(bf16[3,3,128,128]{3,2,1,0:T(8,128)(2,1)S(1)} %collective-permute-done.low), channel_id=1, source_target_pairs={{1,2},{2,1},{3,4},{4,3},{5,6},{6,5},{9,10},{10,9},{11,12},{12,11},... | collective-permute-start | bytes 884744 | tf_op jit(solution)/shard_map/ppermute | solution.py:32
  17.8 8.7 %collective-permute-start.8 = (bf16[3,3,128,128]{3,2,1,0:T(8,128)(2,1)S(1)}, bf16[3,3,128,128]{3,2,1,0:T(8,128)(2,1)S(1)}, u32[]{:S(2)}, u32[]{:S(2)}) collective-permute-start(bf16[3,3,128,128]{3,2,1,0:T(8,128)(2,1)S(1)} %collective-permute-done.1.high), channel_id=1, source_target_pairs={{0,1},{1,0},{2,3},{3,2},{4,5},{5,4},{6,7},{7,6},{8,9},{9,8},{10,11... | collective-permute-start | bytes 884744 | tf_op jit(solution)/shard_map/ppermute | solution.py:27
  17.8 8.6 %collective-permute-start.9 = (bf16[3,3,128,128]{3,2,1,0:T(8,128)(2,1)S(1)}, bf16[3,3,128,128]{3,2,1,0:T(8,128)(2,1)S(1)}, u32[]{:S(2)}, u32[]{:S(2)}) collective-permute-start(bf16[3,3,128,128]{3,2,1,0:T(8,128)(2,1)S(1)} %collective-permute-done.1.high), channel_id=1, source_target_pairs={{1,2},{2,1},{3,4},{4,3},{5,6},{6,5},{9,10},{10,9},{11,12},{12,11},... | collective-permute-start | bytes 884744 | tf_op jit(solution)/shard_map/ppermute | solution.py:32
  21.1 10.7 %collective-permute-start.2 = (bf16[2,3,96,128]{3,2,1,0:T(8,128)(2,1)}, bf16[2,3,96,128]{3,2,1,0:T(8,128)(2,1)S(1)}, u32[]{:S(2)}, u32[]{:S(2)}) collective-permute-start(bf16[2,3,96,128]{3,2,1,0:T(8,128)(2,1)} %copy-done.7), channel_id=1, source_target_pairs={{0,8},{8,16},{16,24},{24,0},{1,9},{9,17},{17,25},{25,1},{2,10},{10... | collective-permute-start | bytes 442376 | tf_op jit(solution)/shard_map/ppermute | solution.py:18
  23.3 8.5 %collective-permute-start.3 = (bf16[2,3,96,128]{3,2,1,0:T(8,128)(2,1)S(1)}, bf16[2,3,96,128]{3,2,1,0:T(8,128)(2,1)S(1)}, u32[]{:S(2)}, u32[]{:S(2)}) collective-permute-start(bf16[2,3,96,128]{3,2,1,0:T(8,128)(2,1)S(1)} %get-tuple-element.70), channel_id=1, source_target_pairs={{0,24},{8,0},{16,8},{24,16},{1,25},{9,1},{17,9},{25,17},{2,26},{10... | collective-permute-start | bytes 442376 | tf_op jit(solution)/shard_map/ppermute | solution.py:18
  29.4 14.0 %copy-start.4 = (bf16[288,896]{1,0:T(8,128)(2,1)S(1)}, bf16[288,896]{1,0:T(8,128)(2,1)}, u32[]{:S(2)}) copy-start(bf16[288,896]{1,0:T(8,128)(2,1)} %get-tuple-element.85.a_re) | copy-start | bytes 1548292
  29.4 14.0 %copy-start.5 = (bf16[288,896]{1,0:T(8,128)(2,1)S(1)}, bf16[288,896]{1,0:T(8,128)(2,1)}, u32[]{:S(2)}) copy-start(bf16[288,896]{1,0:T(8,128)(2,1)} %get-tuple-element.84.a_up) | copy-start | bytes 1548292
  29.4 10.0 %collective-permute-start.12 = (bf16[2,3,96,128]{3,2,1,0:T(8,128)(2,1)S(1)}, bf16[2,3,96,128]{3,2,1,0:T(8,128)(2,1)S(1)}, u32[]{:S(2)}, u32[]{:S(2)}) collective-permute-start(bf16[2,3,96,128]{3,2,1,0:T(8,128)(2,1)S(1)} %get-tuple-element.91), channel_id=1, source_target_pairs={{0,8},{8,16},{16,24},{24,0},{1,9},{9,17},{17,25},{25,1},{2,10},{10... | collective-permute-start | bytes 442376 | tf_op jit(solution)/shard_map/ppermute | solution.py:18
  31.8 7.5 %collective-permute-start.13 = (bf16[2,3,96,128]{3,2,1,0:T(8,128)(2,1)S(1)}, bf16[2,3,96,128]{3,2,1,0:T(8,128)(2,1)S(1)}, u32[]{:S(2)}, u32[]{:S(2)}) collective-permute-start(bf16[2,3,96,128]{3,2,1,0:T(8,128)(2,1)S(1)} %get-tuple-element.95), channel_id=1, source_target_pairs={{0,24},{8,0},{16,8},{24,16},{1,25},{9,1},{17,9},{25,17},{2,26},{10... | collective-permute-start | bytes 442376 | tf_op jit(solution)/shard_map/ppermute | solution.py:18
  32.4 10.9 %collective-permute-start.10 = (bf16[7,2,96,128]{3,2,1,0:T(8,128)(2,1)S(1)}, bf16[7,2,96,128]{3,2,1,0:T(8,128)(2,1)S(1)}, u32[]{:S(2)}, u32[]{:S(2)}) collective-permute-start(bf16[7,2,96,128]{3,2,1,0:T(8,128)(2,1)S(1)} %get-tuple-element.82), channel_id=1, source_target_pairs={{0,1},{1,0},{2,3},{3,2},{4,5},{5,4},{6,7},{7,6},{8,9},{9,8},{10,11... | collective-permute-start | bytes 1032200 | tf_op jit(solution)/shard_map/ppermute | solution.py:27
  32.5 10.8 %collective-permute-start.11 = (bf16[7,2,96,128]{3,2,1,0:T(8,128)(2,1)S(1)}, bf16[7,2,96,128]{3,2,1,0:T(8,128)(2,1)S(1)}, u32[]{:S(2)}, u32[]{:S(2)}) collective-permute-start(bf16[7,2,96,128]{3,2,1,0:T(8,128)(2,1)S(1)} %get-tuple-element.83), channel_id=1, source_target_pairs={{1,2},{2,1},{3,4},{4,3},{5,6},{6,5},{9,10},{10,9},{11,12},{12,11},... | collective-permute-start | bytes 1032200 | tf_op jit(solution)/shard_map/ppermute | solution.py:32
  39.9 9.2 %copy-start = (bf16[288,896]{1,0:T(8,128)(2,1)S(1)}, bf16[288,896]{1,0:T(8,128)(2,1)}, u32[]{:S(2)}) copy-start(bf16[288,896]{1,0:T(8,128)(2,1)} %get-tuple-element.98.a_up) | copy-start | bytes 1548292
  39.9 9.2 %copy-start.1 = (bf16[288,896]{1,0:T(8,128)(2,1)S(1)}, bf16[288,896]{1,0:T(8,128)(2,1)}, u32[]{:S(2)}) copy-start(bf16[288,896]{1,0:T(8,128)(2,1)} %get-tuple-element.100.a_ca_old) | copy-start | bytes 1548292
  39.9 9.2 %copy-start.2 = (bf16[288,896]{1,0:T(8,128)(2,1)S(1)}, bf16[288,896]{1,0:T(8,128)(2,1)}, u32[]{:S(2)}) copy-start(bf16[288,896]{1,0:T(8,128)(2,1)} %get-tuple-element.101.a_ca_new) | copy-start | bytes 1548292
  40.0 9.2 %copy-start.3 = (bf16[288,896]{1,0:T(8,128)(2,1)S(1)}, bf16[288,896]{1,0:T(8,128)(2,1)}, u32[]{:S(2)}) copy-start(bf16[288,896]{1,0:T(8,128)(2,1)} %get-tuple-element.99.a_re) | copy-start | bytes 1548292
  40.0 9.2 %copy-start.6 = (bf16[216,96]{1,0:T(8,128)(2,1)S(1)}, bf16[216,96]{1,0:T(8,128)(2,1)}, u32[]{:S(2)}) copy-start(bf16[216,96]{1,0:T(8,128)(2,1)} %get-tuple-element.102.head) | copy-start | bytes 124420
  40.0 7.6 %collective-permute-start.14 = (bf16[7,2,96,128]{3,2,1,0:T(8,128)(2,1)S(1)}, bf16[7,2,96,128]{3,2,1,0:T(8,128)(2,1)S(1)}, u32[]{:S(2)}, u32[]{:S(2)}) collective-permute-start(bf16[7,2,96,128]{3,2,1,0:T(8,128)(2,1)S(1)} %get-tuple-element.96), channel_id=1, source_target_pairs={{0,1},{1,0},{2,3},{3,2},{4,5},{5,4},{6,7},{7,6},{8,9},{9,8},{10,11... | collective-permute-start | bytes 1032200 | tf_op jit(solution)/shard_map/ppermute | solution.py:27
  40.5 8.7 %collective-permute-start.15 = (bf16[7,2,96,128]{3,2,1,0:T(8,128)(2,1)S(1)}, bf16[7,2,96,128]{3,2,1,0:T(8,128)(2,1)S(1)}, u32[]{:S(2)}, u32[]{:S(2)}) collective-permute-start(bf16[7,2,96,128]{3,2,1,0:T(8,128)(2,1)S(1)} %get-tuple-element.97), channel_id=1, source_target_pairs={{1,2},{2,1},{3,4},{4,3},{5,6},{6,5},{9,10},{10,9},{11,12},{12,11},... | collective-permute-start | bytes 1032200 | tf_op jit(solution)/shard_map/ppermute | solution.py:32
  54.3 4.9 %collective-permute-start.16 = (f32[1,5,8,128]{3,2,1,0:T(8,128)S(1)}, f32[1,5,8,128]{3,2,1,0:T(8,128)S(1)}, u32[]{:S(2)}, u32[]{:S(2)}) collective-permute-start(f32[1,5,8,128]{3,2,1,0:T(8,128)S(1)} %get-tuple-element.109), channel_id=1, source_target_pairs={{0,8},{8,16},{16,24},{24,0},{1,9},{9,17},{17,25},{25,1},{2,10},{10... | collective-permute-start | bytes 61448 | tf_op jit(solution)/shard_map/ppermute | solution.py:18
  56.6 3.5 %collective-permute-start.17 = (f32[1,5,8,128]{3,2,1,0:T(8,128)S(1)}, f32[1,5,8,128]{3,2,1,0:T(8,128)S(1)}, u32[]{:S(2)}, u32[]{:S(2)}) collective-permute-start(f32[1,5,8,128]{3,2,1,0:T(8,128)S(1)} %get-tuple-element.110), channel_id=1, source_target_pairs={{0,24},{8,0},{16,8},{24,16},{1,25},{9,1},{17,9},{25,17},{2,26},{10... | collective-permute-start | bytes 61448 | tf_op jit(solution)/shard_map/ppermute | solution.py:18
  60.7 5.9 %collective-permute-start.18 = (f32[3,1,8,128]{3,2,1,0:T(8,128)S(1)}, f32[3,1,8,128]{3,2,1,0:T(8,128)S(1)}, u32[]{:S(2)}, u32[]{:S(2)}) collective-permute-start(f32[3,1,8,128]{3,2,1,0:T(8,128)S(1)} %get-tuple-element.112), channel_id=1, source_target_pairs={{0,1},{1,0},{2,3},{3,2},{4,5},{5,4},{6,7},{7,6},{8,9},{9,8},{10,11... | collective-permute-start | bytes 36872 | tf_op jit(solution)/shard_map/ppermute | solution.py:27
  62.5 5.0 %collective-permute-start.19 = (f32[3,1,8,128]{3,2,1,0:T(8,128)S(1)}, f32[3,1,8,128]{3,2,1,0:T(8,128)S(1)}, u32[]{:S(2)}, u32[]{:S(2)}) collective-permute-start(f32[3,1,8,128]{3,2,1,0:T(8,128)S(1)} %get-tuple-element.113), channel_id=1, source_target_pairs={{1,2},{2,1},{3,4},{4,3},{5,6},{6,5},{9,10},{10,9},{11,12},{12,11},... | collective-permute-start | bytes 36872 | tf_op jit(solution)/shard_map/ppermute | solution.py:32

commit v3 on v2

--- a/solution.py
+++ b/solution.py
@@ -199,7 +199,7 @@
         found.update({key: (pairs, slot) for key, slot in slots_of(part, planes, rows).items()})
     turn = (3 - lax.broadcasted_iota(jnp.int32, (1, 8, LANES), 2)) & 7
     turn = jnp.concatenate([turn] * rows, axis=2)
-    results = []
+    columns = []
     for z in range(planes):
         made = []
         for pair in range(49):
@@ -211,9 +211,9 @@
         got = jnp.concatenate(made, axis=0)
         for bit in (1, 2, 4):
             got = jnp.where((turn & bit) != 0, pltpu.roll(got, bit, 1), got)
-        got = (got * scale).reshape(49 * 8, wide).astype(BF16)
-        results.append(jnp.dot(wc[...], got, preferred_element_type=F32))
-    return results
+        columns.append((got * scale).reshape(49 * 8, wide).astype(BF16))
+    sums = jnp.dot(wc[...], jnp.concatenate(columns, axis=1), preferred_element_type=F32)
+    return [sums[:, z * wide : (z + 1) * wide] for z in range(planes)]
 
 
 def put_block(tt, block, ok, row, plane):
@@ -366,46 +366,52 @@
 def fill(place, field, own, z0, z1, mate, other):
     planes, rows, width = own.shape[:3]
     odd = place[3]
+    low, high, along = place[0] == 1, place[1] == 1, place[2] == 1
 
     def store(plane, y, value):
         at = y * LANES if isinstance(y, int) else pl.multiple_of(y * LANES, LANES)
         field[plane, :, pl.ds(at, LANES)] = value
 
-    def store_if(ok, plane, y, value):
-        @pl.when(ok)
-        def _():
-            store(plane, y, value())
-
-        @pl.when(jnp.logical_not(ok))
-        def _():
-            store(plane, y, jnp.zeros((width, LANES), BF16))
-
-    for plane in range(planes + 4):
-        in_z = None
-        if plane < 2:
-            in_z = place[0]
-        elif plane >= planes + 2:
-            in_z = place[1]
+    def mates(over):
+        for plane in over:
+            for y in range(2):
+                store(plane, y + (rows + 2) * (1 - odd), mate(plane, y))
+
+    def others(over, inside=True):
+        for plane in over:
+            for y in range(2):
+                value = other(plane, y) if inside else jnp.zeros((width, LANES), BF16)
+                store(plane, y + (rows + 2) * odd, value)
+
+    def outside(over):
+        for plane in over:
+            field[plane] = jnp.zeros(field.shape[1:], BF16)
+
+    for plane in range(planes):
         for y in range(rows):
-            if plane < 2:
-                store_if(in_z == 1, plane, y + 2, lambda: z0[plane, y])
-            elif plane >= planes + 2:
-                store_if(in_z == 1, plane, y + 2, lambda: z1[plane - planes - 2, y])
-            else:
-                store(plane, y + 2, own[plane - 2, y])
-        for y in range(2):
-            mate_at, other_at = y + (rows + 2) * (1 - odd), y + (rows + 2) * odd
-            if in_z is None:
-                store(plane, mate_at, mate[plane, y])
-                store_if(place[2] == 1, plane, other_at, lambda: other[plane, y])
-            else:
-                store_if(in_z == 1, plane, mate_at, lambda: mate[plane, y])
-                store_if(in_z + place[2] == 2, plane, other_at, lambda: other[plane, y])
+            store(plane + 2, y + 2, own[plane, y])
+    middle = range(2, planes + 2)
+    mates(middle)
+    pl.when(along)(lambda: others(middle))
+    pl.when(jnp.logical_not(along))(lambda: others(middle, False))
+    for ok, block, first in ((low, z0, 0), (high, z1, planes + 2)):
+        over = range(first, first + 2)
+
+        def inner(block=block, first=first, over=over):
+            for plane in over:
+                for y in range(rows):
+                    store(plane, y + 2, block[plane - first, y])
+            mates(over)
+
+        pl.when(ok)(inner)
+        pl.when(jnp.logical_not(ok))(lambda over=over: outside(over))
+        pl.when(jnp.logical_and(ok, along))(lambda over=over: others(over))
+        pl.when(jnp.logical_and(ok, jnp.logical_not(along)))(lambda over=over: others(over, False))
 
 
 def old_body(place, hidden, small, hz0, hz1, h_mate, h_other, a_up, a_re, update_out, reset_out, near_out, field):
     planes, rows = hidden.shape[:2]
-    fill(place, field, hidden, hz0, hz1, h_mate, h_other)
+    fill(place, field, hidden, hz0, hz1, lambda plane, y: h_mate[plane, y], lambda plane, y: h_other[plane, y])
     width = hidden.shape[2]
     up_shift, re_shift = column(small[1:2, :width]), column(small[2:3, :width])
 
@@ -461,7 +467,7 @@
     part_low, part_out, part_high, field, gated, outer, state
 ):
     planes, rows = enc.shape[:2]
-    fill(place, field, enc, ez0, ez1, e_mate, e_other)
+    fill(place, field, enc, ez0, ez1, lambda plane, y: e_mate[plane, y], lambda plane, y: e_other[plane, y])
     every = range(planes + 2)
     for n, got in enumerate(conv(a_re[...], side_by_side(field, every, 0, rows + 2), (planes + 2) * (rows + 2))):
         z, y = n // (rows + 2), n % (rows + 2)

time: 68.6 us -> 68.3 us (level)
  no operation moved by 1% of the time
where the time goes in v3:
time: 68.3 us; the launch traced here: 68 us
  starting transfers between devices  30.9 us (45%)
  Pallas kernels  29.7 us (43%)
  waiting for transfers between devices  3.67 us (5%)
  between operations  2.27 us (3%)
  other arithmetic  0.77 us (1%)
    pallas_call x11, Pallas kernels, call(): pl.pallas_call(body, out_shape=jax.tree.map(lambda o: pltpu.VMEM(o.shape,...  29.7 us
    ppermute x6, starting transfers between devices, rows_of_other(): lax.ppermute(to_other, 'gy', [(i, (i + 1 ^ 1) - 1) for i in range(1, coun...  19.5 us
    ppermute x8, starting transfers between devices, around(): lax.ppermute(block, axis, [(i, (i + step) % count) for i in range(count)])  8.4 us
    ppermute x6, starting transfers between devices, rows_of_mate(): return lax.ppermute(to_mate, 'gy', [(i, i ^ 1) for i in range(count)])  3.03 us
    ppermute x6, waiting for transfers between devices, rows_of_other(): lax.ppermute(to_other, 'gy', [(i, (i + 1 ^ 1) - 1) for i in range(1, coun...  2.73 us
  transfers between devices with their start and end apart: 20, of which 3 were waited for; matrix products, arithmetic and copies ran while one was open for 1% of the time, Pallas kernels for 36%

profile of v3, /device:TPU:11, one launch (start us, length us, event | category | flops | bytes accessed | tf_op | source)
XLA Modules:
  0.0 68.0 jit_solution(9137655882505722166)
XLA Ops:
  0.6 1.3 %collective-permute-start = (bf16[3,3,128,128]{3,2,1,0:T(8,128)(2,1)}, bf16[3,3,128,128]{3,2,1,0:T(8,128)(2,1)S(1)}, u32[]{:S(2)}, u32[]{:S(2)}) collective-permute-start(bf16[3,3,128,128]{3,2,1,0:T(8,128)(2,1)} %own.3), channel_id=1, source_target_pairs={{0,8},{8,16},{16,24},{24,0},{1,9},{9,17},{17,25},{25,1},{2,10},{10... | collective-permute-start | bytes 884744 | tf_op jit(solution)/shard_map/ppermute | solution.py:18
  1.9 0.3 collective-permute-start.1
  2.2 4.3 %collective-permute-start.5 = (bf16[3,3,128,128]{3,2,1,0:T(8,128)(2,1)}, bf16[3,3,128,128]{3,2,1,0:T(8,128)(2,1)S(1)}, u32[]{:S(2)}, u32[]{:S(2)}) collective-permute-start(bf16[3,3,128,128]{3,2,1,0:T(8,128)(2,1)} %own.3), channel_id=1, source_target_pairs={{1,2},{2,1},{3,4},{4,3},{5,6},{6,5},{9,10},{10,9},{11,12},{12,11},... | collective-permute-start | bytes 884744 | tf_op jit(solution)/shard_map/ppermute | solution.py:32
  6.5 5.1 %own.2 = (f32[81,8,128]{2,1,0:T(8,128)S(1)}, bf16[96,392]{1,0:T(8,128)(2,1)S(1)}, bf16[2,3,96,128]{3,2,1,0:T(8,128)(2,1)S(1)}, bf16[2,3,96,128]{3,2,1,0:T(8,128)...) custom-call(bf16[27,18432]{1,0:T(8,128)(2,1)} %w_reset.1, ...), custom_call_target="tpu_custom_call" | custom-call | flops 1000 | bytes 1000 | tf_op jit(solution)/shard_map/own/pallas_call | solution.py:69
  11.6 0.0 copy-start.7
  11.6 0.0 collective-permute-done.low
  11.6 0.1 collective-permute-start.4
  11.7 0.5 collective-permute-start.6
  12.2 3.2 %collective-permute-start.7 = (bf16[3,3,128,128]{3,2,1,0:T(8,128)(2,1)S(1)}, bf16[3,3,128,128]{3,2,1,0:T(8,128)(2,1)S(1)}, u32[]{:S(2)}, u32[]{:S(2)}) collective-permute-start(bf16[3,3,128,128]{3,2,1,0:T(8,128)(2,1)S(1)} %collective-permute-done.low), channel_id=1, source_target_pairs={{1,2},{2,1},{3,4},{4,3},{5,6},{6,5},{9,10},{10,9},{11,12},{12,11},... | collective-permute-start | bytes 884744 | tf_op jit(solution)/shard_map/ppermute | solution.py:32
  15.4 2.4 %lay_out_update.1 = (bf16[288,896]{1,0:T(8,128)(2,1)}, bf16[288,896]{1,0:T(8,128)(2,1)}) custom-call(bf16[27,18432]{1,0:T(8,128)(2,1)S(1)} %get-tuple-element.66.weight), custom_call_target="tpu_custom_call" | custom-call | flops 1000 | bytes 1000 | tf_op jit(solution)/shard_map/lay_out_update/pallas_call | solution.py:69
  17.8 0.0 collective-permute-done.1.high
  17.8 0.0 collective-permute-start.8
  17.8 0.0 collective-permute-done.5.other
  17.8 0.0 copy-done.7
  17.8 3.3 %collective-permute-start.9 = (bf16[3,3,128,128]{3,2,1,0:T(8,128)(2,1)S(1)}, bf16[3,3,128,128]{3,2,1,0:T(8,128)(2,1)S(1)}, u32[]{:S(2)}, u32[]{:S(2)}) collective-permute-start(bf16[3,3,128,128]{3,2,1,0:T(8,128)(2,1)S(1)} %collective-permute-done.1.high), channel_id=1, source_target_pairs={{1,2},{2,1},{3,4},{4,3},{5,6},{6,5},{9,10},{10,9},{11,12},{12,11},... | collective-permute-start | bytes 884744 | tf_op jit(solution)/shard_map/ppermute | solution.py:32
  21.1 0.0 collective-permute-done.4.mate
  21.1 2.2 %collective-permute-start.2 = (bf16[2,3,96,128]{3,2,1,0:T(8,128)(2,1)}, bf16[2,3,96,128]{3,2,1,0:T(8,128)(2,1)S(1)}, u32[]{:S(2)}, u32[]{:S(2)}) collective-permute-start(bf16[2,3,96,128]{3,2,1,0:T(8,128)(2,1)} %copy-done.7), channel_id=1, source_target_pairs={{0,8},{8,16},{16,24},{24,0},{1,9},{9,17},{17,25},{25,1},{2,10},{10... | collective-permute-start | bytes 442376 | tf_op jit(solution)/shard_map/ppermute | solution.py:18
  23.3 0.0 collective-permute-done.6.low_mate
  23.3 0.0 collective-permute-start.3
  23.3 0.1 add_convert_fusion.place
  23.4 3.1 %face.1.face_pairs = f32[216,8,128]{2,1,0:T(8,128)S(1)} custom-call(s32[4]{0:T(128)S(1)} %add_convert_fusion.place, bf16[3,128,384]{2,1,0:T(8,128)(2,1)S(1)} %get-tuple-element.71.s_flat, bf16[3,3,128,128]{3,2,1,0:T(8,128)(2,1)S(1)} %collective-permute-done.low, bf16[3,3,128,128]{3,2,1,0:T(8,128)(2,1)S(1)} %collective-permute-done.1.high, ...), custom_call_target="tpu_custom_call" | custom-call | flops 1000 | bytes 1000 | tf_op jit(solution)/shard_map/face/pallas_call | solution.py:69
  26.4 0.0 collective-permute-done.7.low_other
  26.5 0.0 collective-permute-done.8.high_mate
  26.5 0.0 collective-permute-done.9.high_other
  26.5 2.8 %corner.1 = (bf16[3,3,96,128]{3,2,1,0:T(8,128)(2,1)S(1)}, bf16[2,3,96,128]{3,2,1,0:T(8,128)(2,1)S(1)}, bf16[2,3,96,128]{3,2,1,0:T(8,128)(2,1)S(1)}) custom-call(s32[4]{0:T(128)S(1)} %add_convert_fusion.place, bf16[3,128,384]{2,1,0:T(8,128)(2,1)S(1)} %get-tuple-element.71.s_flat, f32[3,3,3,128]{3,2,1,0:T(4,128)S(1)} %get-tuple-element.72.motion, ...), custom_call_target="tpu_custom_call" | custom-call | flops 1000 | bytes 1000 | tf_op jit(solution)/shard_map/corner/pallas_call | solution.py:69
  29.3 0.0 copy-start.4
  29.3 0.0 copy-start.5
  29.3 2.4 %collective-permute-start.12 = (bf16[2,3,96,128]{3,2,1,0:T(8,128)(2,1)S(1)}, bf16[2,3,96,128]{3,2,1,0:T(8,128)(2,1)S(1)}, u32[]{:S(2)}, u32[]{:S(2)}) collective-permute-start(bf16[2,3,96,128]{3,2,1,0:T(8,128)(2,1)S(1)} %get-tuple-element.91), channel_id=1, source_target_pairs={{0,8},{8,16},{16,24},{24,0},{1,9},{9,17},{17,25},{25,1},{2,10},{10... | collective-permute-start | bytes 442376 | tf_op jit(solution)/shard_map/ppermute | solution.py:18
  31.8 0.0 collective-permute-start.13
  31.8 0.0 collective-permute-done.2.low.hz0
  31.8 0.0 collective-permute-done.3.high.hz1
  31.8 0.6 pack_hidden.1
  32.4 0.1 collective-permute-start.10
  32.5 3.1 %collective-permute-start.11 = (bf16[7,2,96,128]{3,2,1,0:T(8,128)(2,1)S(1)}, bf16[7,2,96,128]{3,2,1,0:T(8,128)(2,1)S(1)}, u32[]{:S(2)}, u32[]{:S(2)}) collective-permute-start(bf16[7,2,96,128]{3,2,1,0:T(8,128)(2,1)S(1)} %get-tuple-element.83), channel_id=1, source_target_pairs={{1,2},{2,1},{3,4},{4,3},{5,6},{6,5},{9,10},{10,9},{11,12},{12,11},... | collective-permute-start | bytes 1032200 | tf_op jit(solution)/shard_map/ppermute | solution.py:32
  35.6 3.7 %lay_out_cand.1 = (bf16[288,896]{1,0:T(8,128)(2,1)}, bf16[288,896]{1,0:T(8,128)(2,1)}, bf16[216,96]{1,0:T(8,128)(2,1)}) custom-call(bf16[27,18432]{1,0:T(8,128)(2,1)} %weight.1, bf16[3,27,96]{2,1,0:T(8,128)(2,1)} %bitcast.17), custom_call_target="tpu_custom_call" | custom-call | flops 1000 | bytes 1000 | tf_op jit(solution)/shard_map/lay_out_cand/pallas_call | solution.py:69
  39.3 0.0 collective-permute-done.12.low.ez0
  39.3 0.0 collective-permute-done.13.high.ez1
  39.3 0.6 pack_encoded.1
  39.9 0.0 copy-start
  39.9 0.0 copy-start.1
  39.9 0.0 copy-start.2
  39.9 0.0 copy-start.3
  39.9 0.0 copy-start.6
  39.9 0.5 collective-permute-start.14
  40.4 2.8 %collective-permute-start.15 = (bf16[7,2,96,128]{3,2,1,0:T(8,128)(2,1)S(1)}, bf16[7,2,96,128]{3,2,1,0:T(8,128)(2,1)S(1)}, u32[]{:S(2)}, u32[]{:S(2)}) collective-permute-start(bf16[7,2,96,128]{3,2,1,0:T(8,128)(2,1)S(1)} %get-tuple-element.97), channel_id=1, source_target_pairs={{1,2},{2,1},{3,4},{4,3},{5,6},{6,5},{9,10},{10,9},{11,12},{12,11},... | collective-permute-start | bytes 1032200 | tf_op jit(solution)/shard_map/ppermute | solution.py:32
  43.3 0.0 collective-permute-done.10.h_mate
  43.3 0.0 collective-permute-done.11.h_other
  43.3 4.0 %old.1 = (f32[3,3,96,128]{3,2,1,0:T(8,128)S(1)}, f32[5,5,96,128]{3,2,1,0:T(8,128)S(1)}, bf16[5,96,640]{2,1,0:T(8,128)(2,1)S(1)}) custom-call(s32[4]{0:T(128)S(1)} %add_convert_fusion.place, bf16[3,3,96,128]{3,2,1,0:T(8,128)(2,1)S(1)} %get-tuple-element.59.own.hidden, f32[8,128]{1,0:T(8,128)S(1)} %get-tuple-element.58.small, ...), custom_call_target="tpu_custom_call" | custom-call | flops 1000 | bytes 1000 | tf_op jit(solution)/shard_map/old/pallas_call | solution.py:69
  47.3 0.0 collective-permute-done.14.e_mate
  47.3 1.8 %collective-permute-done.15.e_other = bf16[7,2,96,128]{3,2,1,0:T(8,128)(2,1)S(1)} collective-permute-done((bf16[7,2,96,128]{3,2,1,0:T(8,128)(2,1)S(1)}, bf16[7,2,96,128]{3,2,1,0:T(8,128)(2,1)S(1)}, u32[]{:S(2)}, u32[]{:S(2)}) %collective-permute-start.15) | collective-permute-done | bytes 344096 | tf_op jit(solution)/shard_map/ppermute | solution.py:32
  49.1 0.0 copy-done.1
  49.2 4.8 %gru_outer.1 = (f32[1,5,8,128]{3,2,1,0:T(8,128)S(1)}, f32[3,5,8,128]{3,2,1,0:T(8,128)S(1)}, f32[1,5,8,128]{3,2,1,0:T(8,128)S(1)}, bf16[7,96,896]{2,1,0:T(8,128)(...) custom-call(s32[4]{0:T(128)S(1)} %add_convert_fusion.place, ...), custom_call_target="tpu_custom_call" | custom-call | flops 1000 | bytes 1000 | tf_op jit(solution)/shard_map/gru_outer/pallas_call | solution.py:69
  54.0 2.3 %collective-permute-start.16 = (f32[1,5,8,128]{3,2,1,0:T(8,128)S(1)}, f32[1,5,8,128]{3,2,1,0:T(8,128)S(1)}, u32[]{:S(2)}, u32[]{:S(2)}) collective-permute-start(f32[1,5,8,128]{3,2,1,0:T(8,128)S(1)} %get-tuple-element.109), channel_id=1, source_target_pairs={{0,8},{8,16},{16,24},{24,0},{1,9},{9,17},{17,25},{25,1},{2,10},{10... | collective-permute-start | bytes 61448 | tf_op jit(solution)/shard_map/ppermute | solution.py:18
  56.3 0.0 collective-permute-start.17
  56.3 0.6 fusion.1
  56.9 2.0 %gru_inner.1 = (bf16[3,3,96,128]{3,2,1,0:T(8,128)(2,1)}, f32[3,5,8,128]{3,2,1,0:T(8,128)S(1)}) custom-call(f32[8,128]{1,0:T(8,128)S(1)} %get-tuple-element.58.small, bf16[5,96,640]{2,1,0:T(8,128)(2,1)S(1)} %get-tuple-element.86.near, f32[3,3,96,128]{3,2,1,0:T(8,128)S(1)} %get-tuple-element.87.update_old, bf16[7,96,896]{2,1,0:T(8,128)(2,1)S(1)} %get-tuple-element.103.field, ...), custom_call_target="tpu_custom_call" | custom-call | flops 1000 | bytes 1000 | tf_op jit(solution)/shard_map/gru_inner/pallas_call | solution.py:69
  58.9 0.0 collective-permute-done.16.low
  58.9 0.9 %collective-permute-done.17.high = f32[1,5,8,128]{3,2,1,0:T(8,128)S(1)} collective-permute-done((f32[1,5,8,128]{3,2,1,0:T(8,128)S(1)}, f32[1,5,8,128]{3,2,1,0:T(8,128)S(1)}, u32[]{:S(2)}, u32[]{:S(2)}) %collective-permute-start.17) | collective-permute-done | bytes 20512 | tf_op jit(solution)/shard_map/ppermute | solution.py:18
  59.8 0.6 mix.1
  60.4 1.8 %collective-permute-start.18 = (f32[3,1,8,128]{3,2,1,0:T(8,128)S(1)}, f32[3,1,8,128]{3,2,1,0:T(8,128)S(1)}, u32[]{:S(2)}, u32[]{:S(2)}) collective-permute-start(f32[3,1,8,128]{3,2,1,0:T(8,128)S(1)} %get-tuple-element.112), channel_id=1, source_target_pairs={{0,1},{1,0},{2,3},{3,2},{4,5},{5,4},{6,7},{7,6},{8,9},{9,8},{10,11... | collective-permute-start | bytes 36872 | tf_op jit(solution)/shard_map/ppermute | solution.py:27
  62.2 2.8 %collective-permute-start.19 = (f32[3,1,8,128]{3,2,1,0:T(8,128)S(1)}, f32[3,1,8,128]{3,2,1,0:T(8,128)S(1)}, u32[]{:S(2)}, u32[]{:S(2)}) collective-permute-start(f32[3,1,8,128]{3,2,1,0:T(8,128)S(1)} %get-tuple-element.113), channel_id=1, source_target_pairs={{1,2},{2,1},{3,4},{4,3},{5,6},{6,5},{9,10},{10,9},{11,12},{12,11},... | collective-permute-start | bytes 36872 | tf_op jit(solution)/shard_map/ppermute | solution.py:32
  66.3 0.0 collective-permute-done.18
  66.3 0.9 %collective-permute-done.19 = f32[3,1,8,128]{3,2,1,0:T(8,128)S(1)} collective-permute-done((f32[3,1,8,128]{3,2,1,0:T(8,128)S(1)}, f32[3,1,8,128]{3,2,1,0:T(8,128)S(1)}, u32[]{:S(2)}, u32[]{:S(2)}) %collective-permute-start.19) | collective-permute-done | bytes 12320 | tf_op jit(solution)/shard_map/ppermute | solution.py:32
  67.3 0.7 %fusion = f32[3,3,3,128]{3,2,1,0:T(4,128)} fusion(f32[3,3,8,128]{3,2,1,0:T(8,128)S(1)} %get-tuple-element.111, f32[3,3,128]{2,1,0:T(4,128)S(1)} %slice.14, f32[3,3,128]{2,1,0:T(4,128)S(1)} %slice.12, pred[3]{0:T(512)(128)(4,1)S(1)} %get-tuple-element.118, pred[3]{0:T(512)(128)(4,1)S(1)} %get-tuple-element.119), kind=kLoop, calls=%fused_computation.1 | loop fusion | flops 13824 | bytes 36870 | tf_op jit(solution)/shard_map/add | solution.py:658
  (10 shorter events, 0.0 us)
Async XLA Ops:
  0.6 11.0 %collective-permute-start = (bf16[3,3,128,128]{3,2,1,0:T(8,128)(2,1)}, bf16[3,3,128,128]{3,2,1,0:T(8,128)(2,1)S(1)}, u32[]{:S(2)}, u32[]{:S(2)}) collective-permute-start(bf16[3,3,128,128]{3,2,1,0:T(8,128)(2,1)} %own.3), channel_id=1, source_target_pairs={{0,8},{8,16},{16,24},{24,0},{1,9},{9,17},{17,25},{25,1},{2,10},{10... | collective-permute-start | bytes 884744 | tf_op jit(solution)/shard_map/ppermute | solution.py:18
  1.9 15.9 %collective-permute-start.1 = (bf16[3,3,128,128]{3,2,1,0:T(8,128)(2,1)}, bf16[3,3,128,128]{3,2,1,0:T(8,128)(2,1)S(1)}, u32[]{:S(2)}, u32[]{:S(2)}) collective-permute-start(bf16[3,3,128,128]{3,2,1,0:T(8,128)(2,1)} %own.3), channel_id=1, source_target_pairs={{0,24},{8,0},{16,8},{24,16},{1,25},{9,1},{17,9},{25,17},{2,26},{10... | collective-permute-start | bytes 884744 | tf_op jit(solution)/shard_map/ppermute | solution.py:18
  2.2 15.7 %collective-permute-start.5 = (bf16[3,3,128,128]{3,2,1,0:T(8,128)(2,1)}, bf16[3,3,128,128]{3,2,1,0:T(8,128)(2,1)S(1)}, u32[]{:S(2)}, u32[]{:S(2)}) collective-permute-start(bf16[3,3,128,128]{3,2,1,0:T(8,128)(2,1)} %own.3), channel_id=1, source_target_pairs={{1,2},{2,1},{3,4},{4,3},{5,6},{6,5},{9,10},{10,9},{11,12},{12,11},... | collective-permute-start | bytes 884744 | tf_op jit(solution)/shard_map/ppermute | solution.py:32
  11.6 6.2 %copy-start.7 = (bf16[2,3,96,128]{3,2,1,0:T(8,128)(2,1)}, bf16[2,3,96,128]{3,2,1,0:T(8,128)(2,1)S(1)}, u32[]{:S(2)}) copy-start(bf16[2,3,96,128]{3,2,1,0:T(8,128)(2,1)S(1)} %get-tuple-element.69) | copy-start | bytes 442372
  11.6 9.5 %collective-permute-start.4 = (bf16[3,3,128,128]{3,2,1,0:T(8,128)(2,1)}, bf16[3,3,128,128]{3,2,1,0:T(8,128)(2,1)S(1)}, u32[]{:S(2)}, u32[]{:S(2)}) collective-permute-start(bf16[3,3,128,128]{3,2,1,0:T(8,128)(2,1)} %own.3), channel_id=1, source_target_pairs={{0,1},{1,0},{2,3},{3,2},{4,5},{5,4},{6,7},{7,6},{8,9},{9,8},{10,11... | collective-permute-start | bytes 884744 | tf_op jit(solution)/shard_map/ppermute | solution.py:27
  11.7 11.6 %collective-permute-start.6 = (bf16[3,3,128,128]{3,2,1,0:T(8,128)(2,1)S(1)}, bf16[3,3,128,128]{3,2,1,0:T(8,128)(2,1)S(1)}, u32[]{:S(2)}, u32[]{:S(2)}) collective-permute-start(bf16[3,3,128,128]{3,2,1,0:T(8,128)(2,1)S(1)} %collective-permute-done.low), channel_id=1, source_target_pairs={{0,1},{1,0},{2,3},{3,2},{4,5},{5,4},{6,7},{7,6},{8,9},{9,8},{10,11... | collective-permute-start | bytes 884744 | tf_op jit(solution)/shard_map/ppermute | solution.py:27
  12.2 14.2 %collective-permute-start.7 = (bf16[3,3,128,128]{3,2,1,0:T(8,128)(2,1)S(1)}, bf16[3,3,128,128]{3,2,1,0:T(8,128)(2,1)S(1)}, u32[]{:S(2)}, u32[]{:S(2)}) collective-permute-start(bf16[3,3,128,128]{3,2,1,0:T(8,128)(2,1)S(1)} %collective-permute-done.low), channel_id=1, source_target_pairs={{1,2},{2,1},{3,4},{4,3},{5,6},{6,5},{9,10},{10,9},{11,12},{12,11},... | collective-permute-start | bytes 884744 | tf_op jit(solution)/shard_map/ppermute | solution.py:32
  17.8 8.7 %collective-permute-start.8 = (bf16[3,3,128,128]{3,2,1,0:T(8,128)(2,1)S(1)}, bf16[3,3,128,128]{3,2,1,0:T(8,128)(2,1)S(1)}, u32[]{:S(2)}, u32[]{:S(2)}) collective-permute-start(bf16[3,3,128,128]{3,2,1,0:T(8,128)(2,1)S(1)} %collective-permute-done.1.high), channel_id=1, source_target_pairs={{0,1},{1,0},{2,3},{3,2},{4,5},{5,4},{6,7},{7,6},{8,9},{9,8},{10,11... | collective-permute-start | bytes 884744 | tf_op jit(solution)/shard_map/ppermute | solution.py:27
  17.8 8.6 %collective-permute-start.9 = (bf16[3,3,128,128]{3,2,1,0:T(8,128)(2,1)S(1)}, bf16[3,3,128,128]{3,2,1,0:T(8,128)(2,1)S(1)}, u32[]{:S(2)}, u32[]{:S(2)}) collective-permute-start(bf16[3,3,128,128]{3,2,1,0:T(8,128)(2,1)S(1)} %collective-permute-done.1.high), channel_id=1, source_target_pairs={{1,2},{2,1},{3,4},{4,3},{5,6},{6,5},{9,10},{10,9},{11,12},{12,11},... | collective-permute-start | bytes 884744 | tf_op jit(solution)/shard_map/ppermute | solution.py:32
  21.1 10.6 %collective-permute-start.2 = (bf16[2,3,96,128]{3,2,1,0:T(8,128)(2,1)}, bf16[2,3,96,128]{3,2,1,0:T(8,128)(2,1)S(1)}, u32[]{:S(2)}, u32[]{:S(2)}) collective-permute-start(bf16[2,3,96,128]{3,2,1,0:T(8,128)(2,1)} %copy-done.7), channel_id=1, source_target_pairs={{0,8},{8,16},{16,24},{24,0},{1,9},{9,17},{17,25},{25,1},{2,10},{10... | collective-permute-start | bytes 442376 | tf_op jit(solution)/shard_map/ppermute | solution.py:18
  23.3 8.5 %collective-permute-start.3 = (bf16[2,3,96,128]{3,2,1,0:T(8,128)(2,1)S(1)}, bf16[2,3,96,128]{3,2,1,0:T(8,128)(2,1)S(1)}, u32[]{:S(2)}, u32[]{:S(2)}) collective-permute-start(bf16[2,3,96,128]{3,2,1,0:T(8,128)(2,1)S(1)} %get-tuple-element.70), channel_id=1, source_target_pairs={{0,24},{8,0},{16,8},{24,16},{1,25},{9,1},{17,9},{25,17},{2,26},{10... | collective-permute-start | bytes 442376 | tf_op jit(solution)/shard_map/ppermute | solution.py:18
  29.3 14.0 %copy-start.4 = (bf16[288,896]{1,0:T(8,128)(2,1)S(1)}, bf16[288,896]{1,0:T(8,128)(2,1)}, u32[]{:S(2)}) copy-start(bf16[288,896]{1,0:T(8,128)(2,1)} %get-tuple-element.85.a_re) | copy-start | bytes 1548292
  29.3 14.0 %copy-start.5 = (bf16[288,896]{1,0:T(8,128)(2,1)S(1)}, bf16[288,896]{1,0:T(8,128)(2,1)}, u32[]{:S(2)}) copy-start(bf16[288,896]{1,0:T(8,128)(2,1)} %get-tuple-element.84.a_up) | copy-start | bytes 1548292
  29.3 10.0 %collective-permute-start.12 = (bf16[2,3,96,128]{3,2,1,0:T(8,128)(2,1)S(1)}, bf16[2,3,96,128]{3,2,1,0:T(8,128)(2,1)S(1)}, u32[]{:S(2)}, u32[]{:S(2)}) collective-permute-start(bf16[2,3,96,128]{3,2,1,0:T(8,128)(2,1)S(1)} %get-tuple-element.91), channel_id=1, source_target_pairs={{0,8},{8,16},{16,24},{24,0},{1,9},{9,17},{17,25},{25,1},{2,10},{10... | collective-permute-start | bytes 442376 | tf_op jit(solution)/shard_map/ppermute | solution.py:18
  31.8 7.5 %collective-permute-start.13 = (bf16[2,3,96,128]{3,2,1,0:T(8,128)(2,1)S(1)}, bf16[2,3,96,128]{3,2,1,0:T(8,128)(2,1)S(1)}, u32[]{:S(2)}, u32[]{:S(2)}) collective-permute-start(bf16[2,3,96,128]{3,2,1,0:T(8,128)(2,1)S(1)} %get-tuple-element.95), channel_id=1, source_target_pairs={{0,24},{8,0},{16,8},{24,16},{1,25},{9,1},{17,9},{25,17},{2,26},{10... | collective-permute-start | bytes 442376 | tf_op jit(solution)/shard_map/ppermute | solution.py:18
  32.4 10.9 %collective-permute-start.10 = (bf16[7,2,96,128]{3,2,1,0:T(8,128)(2,1)S(1)}, bf16[7,2,96,128]{3,2,1,0:T(8,128)(2,1)S(1)}, u32[]{:S(2)}, u32[]{:S(2)}) collective-permute-start(bf16[7,2,96,128]{3,2,1,0:T(8,128)(2,1)S(1)} %get-tuple-element.82), channel_id=1, source_target_pairs={{0,1},{1,0},{2,3},{3,2},{4,5},{5,4},{6,7},{7,6},{8,9},{9,8},{10,11... | collective-permute-start | bytes 1032200 | tf_op jit(solution)/shard_map/ppermute | solution.py:27
  32.5 10.8 %collective-permute-start.11 = (bf16[7,2,96,128]{3,2,1,0:T(8,128)(2,1)S(1)}, bf16[7,2,96,128]{3,2,1,0:T(8,128)(2,1)S(1)}, u32[]{:S(2)}, u32[]{:S(2)}) collective-permute-start(bf16[7,2,96,128]{3,2,1,0:T(8,128)(2,1)S(1)} %get-tuple-element.83), channel_id=1, source_target_pairs={{1,2},{2,1},{3,4},{4,3},{5,6},{6,5},{9,10},{10,9},{11,12},{12,11},... | collective-permute-start | bytes 1032200 | tf_op jit(solution)/shard_map/ppermute | solution.py:32
  39.9 9.2 %copy-start = (bf16[288,896]{1,0:T(8,128)(2,1)S(1)}, bf16[288,896]{1,0:T(8,128)(2,1)}, u32[]{:S(2)}) copy-start(bf16[288,896]{1,0:T(8,128)(2,1)} %get-tuple-element.98.a_up) | copy-start | bytes 1548292
  39.9 9.2 %copy-start.1 = (bf16[288,896]{1,0:T(8,128)(2,1)S(1)}, bf16[288,896]{1,0:T(8,128)(2,1)}, u32[]{:S(2)}) copy-start(bf16[288,896]{1,0:T(8,128)(2,1)} %get-tuple-element.100.a_ca_old) | copy-start | bytes 1548292
  39.9 9.2 %copy-start.2 = (bf16[288,896]{1,0:T(8,128)(2,1)S(1)}, bf16[288,896]{1,0:T(8,128)(2,1)}, u32[]{:S(2)}) copy-start(bf16[288,896]{1,0:T(8,128)(2,1)} %get-tuple-element.101.a_ca_new) | copy-start | bytes 1548292
  39.9 9.2 %copy-start.3 = (bf16[288,896]{1,0:T(8,128)(2,1)S(1)}, bf16[288,896]{1,0:T(8,128)(2,1)}, u32[]{:S(2)}) copy-start(bf16[288,896]{1,0:T(8,128)(2,1)} %get-tuple-element.99.a_re) | copy-start | bytes 1548292
  39.9 9.2 %copy-start.6 = (bf16[216,96]{1,0:T(8,128)(2,1)S(1)}, bf16[216,96]{1,0:T(8,128)(2,1)}, u32[]{:S(2)}) copy-start(bf16[216,96]{1,0:T(8,128)(2,1)} %get-tuple-element.102.head) | copy-start | bytes 124420
  39.9 7.4 %collective-permute-start.14 = (bf16[7,2,96,128]{3,2,1,0:T(8,128)(2,1)S(1)}, bf16[7,2,96,128]{3,2,1,0:T(8,128)(2,1)S(1)}, u32[]{:S(2)}, u32[]{:S(2)}) collective-permute-start(bf16[7,2,96,128]{3,2,1,0:T(8,128)(2,1)S(1)} %get-tuple-element.96), channel_id=1, source_target_pairs={{0,1},{1,0},{2,3},{3,2},{4,5},{5,4},{6,7},{7,6},{8,9},{9,8},{10,11... | collective-permute-start | bytes 1032200 | tf_op jit(solution)/shard_map/ppermute | solution.py:27
  40.4 8.7 %collective-permute-start.15 = (bf16[7,2,96,128]{3,2,1,0:T(8,128)(2,1)S(1)}, bf16[7,2,96,128]{3,2,1,0:T(8,128)(2,1)S(1)}, u32[]{:S(2)}, u32[]{:S(2)}) collective-permute-start(bf16[7,2,96,128]{3,2,1,0:T(8,128)(2,1)S(1)} %get-tuple-element.97), channel_id=1, source_target_pairs={{1,2},{2,1},{3,4},{4,3},{5,6},{6,5},{9,10},{10,9},{11,12},{12,11},... | collective-permute-start | bytes 1032200 | tf_op jit(solution)/shard_map/ppermute | solution.py:32
  54.0 4.9 %collective-permute-start.16 = (f32[1,5,8,128]{3,2,1,0:T(8,128)S(1)}, f32[1,5,8,128]{3,2,1,0:T(8,128)S(1)}, u32[]{:S(2)}, u32[]{:S(2)}) collective-permute-start(f32[1,5,8,128]{3,2,1,0:T(8,128)S(1)} %get-tuple-element.109), channel_id=1, source_target_pairs={{0,8},{8,16},{16,24},{24,0},{1,9},{9,17},{17,25},{25,1},{2,10},{10... | collective-permute-start | bytes 61448 | tf_op jit(solution)/shard_map/ppermute | solution.py:18
  56.3 3.5 %collective-permute-start.17 = (f32[1,5,8,128]{3,2,1,0:T(8,128)S(1)}, f32[1,5,8,128]{3,2,1,0:T(8,128)S(1)}, u32[]{:S(2)}, u32[]{:S(2)}) collective-permute-start(f32[1,5,8,128]{3,2,1,0:T(8,128)S(1)} %get-tuple-element.110), channel_id=1, source_target_pairs={{0,24},{8,0},{16,8},{24,16},{1,25},{9,1},{17,9},{25,17},{2,26},{10... | collective-permute-start | bytes 61448 | tf_op jit(solution)/shard_map/ppermute | solution.py:18
  60.4 5.9 %collective-permute-start.18 = (f32[3,1,8,128]{3,2,1,0:T(8,128)S(1)}, f32[3,1,8,128]{3,2,1,0:T(8,128)S(1)}, u32[]{:S(2)}, u32[]{:S(2)}) collective-permute-start(f32[3,1,8,128]{3,2,1,0:T(8,128)S(1)} %get-tuple-element.112), channel_id=1, source_target_pairs={{0,1},{1,0},{2,3},{3,2},{4,5},{5,4},{6,7},{7,6},{8,9},{9,8},{10,11... | collective-permute-start | bytes 36872 | tf_op jit(solution)/shard_map/ppermute | solution.py:27
  62.2 5.0 %collective-permute-start.19 = (f32[3,1,8,128]{3,2,1,0:T(8,128)S(1)}, f32[3,1,8,128]{3,2,1,0:T(8,128)S(1)}, u32[]{:S(2)}, u32[]{:S(2)}) collective-permute-start(f32[3,1,8,128]{3,2,1,0:T(8,128)S(1)} %get-tuple-element.113), channel_id=1, source_target_pairs={{1,2},{2,1},{3,4},{4,3},{5,6},{6,5},{9,10},{10,9},{11,12},{12,11},... | collective-permute-start | bytes 36872 | tf_op jit(solution)/shard_map/ppermute | solution.py:32

commit v4 on v3

--- a/solution.py
+++ b/solution.py
@@ -127,7 +127,7 @@
 
 def lay_out_scratch(width):
     pitch = width * 2 * width // LANES + 1
-    return [pltpu.VMEM((27 * pitch, LANES), F32), pltpu.VMEM((2, 7, 3 * width, LANES), F32)]
+    return [pltpu.VMEM((32 * pitch, LANES), F32), pltpu.VMEM((2, 7, 3 * width, LANES), F32)]
 
 
 def update_body(weight, first_out, last_out, flat, wide):
@@ -560,7 +560,7 @@
         [target_rows, pltpu.VMEM(w_reset.shape, BF16)] + lay_out_scratch(width) + [pltpu.SemaphoreType.DMA((2,))],
         [w_reset, w_update, source, target, w_corr, hidden, motion, w_motion.T] + biases,
         "own",
-        14,
+        15,
         from_hbm=(pltpu.HBM,) * 2 + (pltpu.VMEM,) * 11,
     )
     t_low, to_mate, own = lax.optimization_barrier((t_low, to_mate, own))
@@ -568,7 +568,7 @@
     t_low_mate, t_low_other = rows_around(*edges(t_low, 3))
     update_here, t_low = lax.optimization_barrier((update_here, t_low))
     up_old, up_new = call(
-        update_body, (laid, laid), lay_out_scratch(width), (update_here,), "lay_out_update", 8
+        update_body, (laid, laid), lay_out_scratch(width), (update_here,), "lay_out_update", 9
     )
     t_high, up_new = lax.optimization_barrier((t_high, up_new))
     t_high_mate, t_high_other = rows_around(*edges(t_high, 3))
@@ -592,11 +592,11 @@
     taps_head, enc = lax.optimization_barrier((jnp.transpose(w_head, (1, 0, 2)), enc))
     ca_old, ca_new, head = call(
         cand_body,
-        (laid, laid, pltpu.HBM((27 * 8, width), BF16)),
-        lay_out_scratch(width) + [pltpu.VMEM((27 * 8, LANES), F32)],
+        (laid, laid, pltpu.HBM((32 * 8, width), BF16)),
+        lay_out_scratch(width) + [pltpu.VMEM((32 * 8, LANES), F32)],
         (w_cand, taps_head),
         "lay_out_cand",
-        8,
+        9,
         from_hbm=(pltpu.VMEM,) * 2,
     )
     e_low, ca_new = lax.optimization_barrier((e_low, ca_new))

time: 68.3 us -> 68.3 us (level)
  no operation moved by 1% of the time
where the time goes in v4:
time: 68.3 us; the launch traced here: 68 us
  starting transfers between devices  30.9 us (45%)
  Pallas kernels  29.8 us (44%)
  waiting for transfers between devices  3.64 us (5%)
  between operations  2.27 us (3%)
  other arithmetic  0.77 us (1%)
    pallas_call x11, Pallas kernels, call(): pl.pallas_call(body, out_shape=jax.tree.map(lambda o: pltpu.VMEM(o.shape,...  29.8 us
    ppermute x6, starting transfers between devices, rows_of_other(): lax.ppermute(to_other, 'gy', [(i, (i + 1 ^ 1) - 1) for i in range(1, coun...  19.5 us
    ppermute x8, starting transfers between devices, around(): lax.ppermute(block, axis, [(i, (i + step) % count) for i in range(count)])  8.39 us
    ppermute x6, starting transfers between devices, rows_of_mate(): return lax.ppermute(to_mate, 'gy', [(i, i ^ 1) for i in range(count)])  3.03 us
    ppermute x6, waiting for transfers between devices, rows_of_other(): lax.ppermute(to_other, 'gy', [(i, (i + 1 ^ 1) - 1) for i in range(1, coun...  2.71 us
  transfers between devices with their start and end apart: 20, of which 3 were waited for; matrix products, arithmetic and copies ran while one was open for 1% of the time, Pallas kernels for 36%

profile of v4, /device:TPU:11, one launch (start us, length us, event | category | flops | bytes accessed | tf_op | source)
XLA Modules:
  0.0 68.0 jit_solution(12838298410548391677)
XLA Ops:
  0.6 1.3 %collective-permute-start = (bf16[3,3,128,128]{3,2,1,0:T(8,128)(2,1)}, bf16[3,3,128,128]{3,2,1,0:T(8,128)(2,1)S(1)}, u32[]{:S(2)}, u32[]{:S(2)}) collective-permute-start(bf16[3,3,128,128]{3,2,1,0:T(8,128)(2,1)} %own.3), channel_id=1, source_target_pairs={{0,8},{8,16},{16,24},{24,0},{1,9},{9,17},{17,25},{25,1},{2,10},{10... | collective-permute-start | bytes 884744 | tf_op jit(solution)/shard_map/ppermute | solution.py:18
  1.9 0.3 collective-permute-start.1
  2.2 4.3 %collective-permute-start.5 = (bf16[3,3,128,128]{3,2,1,0:T(8,128)(2,1)}, bf16[3,3,128,128]{3,2,1,0:T(8,128)(2,1)S(1)}, u32[]{:S(2)}, u32[]{:S(2)}) collective-permute-start(bf16[3,3,128,128]{3,2,1,0:T(8,128)(2,1)} %own.3), channel_id=1, source_target_pairs={{1,2},{2,1},{3,4},{4,3},{5,6},{6,5},{9,10},{10,9},{11,12},{12,11},... | collective-permute-start | bytes 884744 | tf_op jit(solution)/shard_map/ppermute | solution.py:32
  6.5 5.1 %own.2 = (f32[81,8,128]{2,1,0:T(8,128)S(1)}, bf16[96,392]{1,0:T(8,128)(2,1)S(1)}, bf16[2,3,96,128]{3,2,1,0:T(8,128)(2,1)S(1)}, bf16[2,3,96,128]{3,2,1,0:T(8,128)...) custom-call(bf16[27,18432]{1,0:T(8,128)(2,1)} %w_reset.1, ...), custom_call_target="tpu_custom_call" | custom-call | flops 1000 | bytes 1000 | tf_op jit(solution)/shard_map/own/pallas_call | solution.py:69
  11.6 0.0 copy-start.7
  11.6 0.0 collective-permute-done.low
  11.6 0.1 collective-permute-start.4
  11.7 0.5 collective-permute-start.6
  12.2 3.2 %collective-permute-start.7 = (bf16[3,3,128,128]{3,2,1,0:T(8,128)(2,1)S(1)}, bf16[3,3,128,128]{3,2,1,0:T(8,128)(2,1)S(1)}, u32[]{:S(2)}, u32[]{:S(2)}) collective-permute-start(bf16[3,3,128,128]{3,2,1,0:T(8,128)(2,1)S(1)} %collective-permute-done.low), channel_id=1, source_target_pairs={{1,2},{2,1},{3,4},{4,3},{5,6},{6,5},{9,10},{10,9},{11,12},{12,11},... | collective-permute-start | bytes 884744 | tf_op jit(solution)/shard_map/ppermute | solution.py:32
  15.4 2.4 %lay_out_update.1 = (bf16[288,896]{1,0:T(8,128)(2,1)}, bf16[288,896]{1,0:T(8,128)(2,1)}) custom-call(bf16[27,18432]{1,0:T(8,128)(2,1)S(1)} %get-tuple-element.66.weight), custom_call_target="tpu_custom_call" | custom-call | flops 1000 | bytes 1000 | tf_op jit(solution)/shard_map/lay_out_update/pallas_call | solution.py:69
  17.8 0.0 collective-permute-done.1.high
  17.8 0.0 collective-permute-start.8
  17.8 0.0 collective-permute-done.5.other
  17.8 0.0 copy-done.7
  17.8 3.3 %collective-permute-start.9 = (bf16[3,3,128,128]{3,2,1,0:T(8,128)(2,1)S(1)}, bf16[3,3,128,128]{3,2,1,0:T(8,128)(2,1)S(1)}, u32[]{:S(2)}, u32[]{:S(2)}) collective-permute-start(bf16[3,3,128,128]{3,2,1,0:T(8,128)(2,1)S(1)} %collective-permute-done.1.high), channel_id=1, source_target_pairs={{1,2},{2,1},{3,4},{4,3},{5,6},{6,5},{9,10},{10,9},{11,12},{12,11},... | collective-permute-start | bytes 884744 | tf_op jit(solution)/shard_map/ppermute | solution.py:32
  21.1 0.0 collective-permute-done.4.mate
  21.1 2.2 %collective-permute-start.2 = (bf16[2,3,96,128]{3,2,1,0:T(8,128)(2,1)}, bf16[2,3,96,128]{3,2,1,0:T(8,128)(2,1)S(1)}, u32[]{:S(2)}, u32[]{:S(2)}) collective-permute-start(bf16[2,3,96,128]{3,2,1,0:T(8,128)(2,1)} %copy-done.7), channel_id=1, source_target_pairs={{0,8},{8,16},{16,24},{24,0},{1,9},{9,17},{17,25},{25,1},{2,10},{10... | collective-permute-start | bytes 442376 | tf_op jit(solution)/shard_map/ppermute | solution.py:18
  23.3 0.0 collective-permute-done.6.low_mate
  23.3 0.0 collective-permute-start.3
  23.3 0.1 add_convert_fusion.place
  23.4 3.1 %face.1.face_pairs = f32[216,8,128]{2,1,0:T(8,128)S(1)} custom-call(s32[4]{0:T(128)S(1)} %add_convert_fusion.place, bf16[3,128,384]{2,1,0:T(8,128)(2,1)S(1)} %get-tuple-element.71.s_flat, bf16[3,3,128,128]{3,2,1,0:T(8,128)(2,1)S(1)} %collective-permute-done.low, bf16[3,3,128,128]{3,2,1,0:T(8,128)(2,1)S(1)} %collective-permute-done.1.high, ...), custom_call_target="tpu_custom_call" | custom-call | flops 1000 | bytes 1000 | tf_op jit(solution)/shard_map/face/pallas_call | solution.py:69
  26.4 0.0 collective-permute-done.7.low_other
  26.5 0.0 collective-permute-done.8.high_mate
  26.5 0.0 collective-permute-done.9.high_other
  26.5 2.8 %corner.1 = (bf16[3,3,96,128]{3,2,1,0:T(8,128)(2,1)S(1)}, bf16[2,3,96,128]{3,2,1,0:T(8,128)(2,1)S(1)}, bf16[2,3,96,128]{3,2,1,0:T(8,128)(2,1)S(1)}) custom-call(s32[4]{0:T(128)S(1)} %add_convert_fusion.place, bf16[3,128,384]{2,1,0:T(8,128)(2,1)S(1)} %get-tuple-element.71.s_flat, f32[3,3,3,128]{3,2,1,0:T(4,128)S(1)} %get-tuple-element.72.motion, ...), custom_call_target="tpu_custom_call" | custom-call | flops 1000 | bytes 1000 | tf_op jit(solution)/shard_map/corner/pallas_call | solution.py:69
  29.3 0.0 copy-start.4
  29.3 0.0 copy-start.5
  29.3 2.4 %collective-permute-start.12 = (bf16[2,3,96,128]{3,2,1,0:T(8,128)(2,1)S(1)}, bf16[2,3,96,128]{3,2,1,0:T(8,128)(2,1)S(1)}, u32[]{:S(2)}, u32[]{:S(2)}) collective-permute-start(bf16[2,3,96,128]{3,2,1,0:T(8,128)(2,1)S(1)} %get-tuple-element.91), channel_id=1, source_target_pairs={{0,8},{8,16},{16,24},{24,0},{1,9},{9,17},{17,25},{25,1},{2,10},{10... | collective-permute-start | bytes 442376 | tf_op jit(solution)/shard_map/ppermute | solution.py:18
  31.8 0.0 collective-permute-start.13
  31.8 0.0 collective-permute-done.2.low.hz0
  31.8 0.0 collective-permute-done.3.high.hz1
  31.8 0.6 pack_hidden.1
  32.4 0.1 collective-permute-start.10
  32.5 3.1 %collective-permute-start.11 = (bf16[7,2,96,128]{3,2,1,0:T(8,128)(2,1)S(1)}, bf16[7,2,96,128]{3,2,1,0:T(8,128)(2,1)S(1)}, u32[]{:S(2)}, u32[]{:S(2)}) collective-permute-start(bf16[7,2,96,128]{3,2,1,0:T(8,128)(2,1)S(1)} %get-tuple-element.83), channel_id=1, source_target_pairs={{1,2},{2,1},{3,4},{4,3},{5,6},{6,5},{9,10},{10,9},{11,12},{12,11},... | collective-permute-start | bytes 1032200 | tf_op jit(solution)/shard_map/ppermute | solution.py:32
  35.6 3.7 %lay_out_cand.1 = (bf16[288,896]{1,0:T(8,128)(2,1)}, bf16[288,896]{1,0:T(8,128)(2,1)}, bf16[256,96]{1,0:T(8,128)(2,1)}) custom-call(bf16[27,18432]{1,0:T(8,128)(2,1)} %weight.1, bf16[3,27,96]{2,1,0:T(8,128)(2,1)} %bitcast.17), custom_call_target="tpu_custom_call" | custom-call | flops 1000 | bytes 1000 | tf_op jit(solution)/shard_map/lay_out_cand/pallas_call | solution.py:69
  39.3 0.0 collective-permute-done.12.low.ez0
  39.3 0.0 collective-permute-done.13.high.ez1
  39.3 0.6 pack_encoded.1
  39.9 0.0 copy-start
  39.9 0.0 copy-start.1
  39.9 0.0 copy-start.2
  39.9 0.0 copy-start.6
  39.9 0.5 collective-permute-start.14
  40.4 2.9 %collective-permute-start.15 = (bf16[7,2,96,128]{3,2,1,0:T(8,128)(2,1)S(1)}, bf16[7,2,96,128]{3,2,1,0:T(8,128)(2,1)S(1)}, u32[]{:S(2)}, u32[]{:S(2)}) collective-permute-start(bf16[7,2,96,128]{3,2,1,0:T(8,128)(2,1)S(1)} %get-tuple-element.97), channel_id=1, source_target_pairs={{1,2},{2,1},{3,4},{4,3},{5,6},{6,5},{9,10},{10,9},{11,12},{12,11},... | collective-permute-start | bytes 1032200 | tf_op jit(solution)/shard_map/ppermute | solution.py:32
  43.3 0.0 collective-permute-done.10.h_mate
  43.3 0.0 collective-permute-done.11.h_other
  43.3 4.0 %old.1 = (f32[3,3,96,128]{3,2,1,0:T(8,128)S(1)}, f32[5,5,96,128]{3,2,1,0:T(8,128)S(1)}, bf16[5,96,640]{2,1,0:T(8,128)(2,1)S(1)}) custom-call(s32[4]{0:T(128)S(1)} %add_convert_fusion.place, bf16[3,3,96,128]{3,2,1,0:T(8,128)(2,1)S(1)} %get-tuple-element.59.own.hidden, f32[8,128]{1,0:T(8,128)S(1)} %get-tuple-element.58.small, ...), custom_call_target="tpu_custom_call" | custom-call | flops 1000 | bytes 1000 | tf_op jit(solution)/shard_map/old/pallas_call | solution.py:69
  47.3 0.0 collective-permute-done.14.e_mate
  47.3 1.8 %collective-permute-done.15.e_other = bf16[7,2,96,128]{3,2,1,0:T(8,128)(2,1)S(1)} collective-permute-done((bf16[7,2,96,128]{3,2,1,0:T(8,128)(2,1)S(1)}, bf16[7,2,96,128]{3,2,1,0:T(8,128)(2,1)S(1)}, u32[]{:S(2)}, u32[]{:S(2)}) %collective-permute-start.15) | collective-permute-done | bytes 344096 | tf_op jit(solution)/shard_map/ppermute | solution.py:32
  49.1 0.0 copy-done.3
  49.1 0.0 copy-done.6
  49.1 4.9 %gru_outer.1 = (f32[1,5,8,128]{3,2,1,0:T(8,128)S(1)}, f32[3,5,8,128]{3,2,1,0:T(8,128)S(1)}, f32[1,5,8,128]{3,2,1,0:T(8,128)S(1)}, bf16[7,96,896]{2,1,0:T(8,128)(...) custom-call(s32[4]{0:T(128)S(1)} %add_convert_fusion.place, ...), custom_call_target="tpu_custom_call" | custom-call | flops 1000 | bytes 1000 | tf_op jit(solution)/shard_map/gru_outer/pallas_call | solution.py:69
  54.0 2.3 %collective-permute-start.16 = (f32[1,5,8,128]{3,2,1,0:T(8,128)S(1)}, f32[1,5,8,128]{3,2,1,0:T(8,128)S(1)}, u32[]{:S(2)}, u32[]{:S(2)}) collective-permute-start(f32[1,5,8,128]{3,2,1,0:T(8,128)S(1)} %get-tuple-element.109), channel_id=1, source_target_pairs={{0,8},{8,16},{16,24},{24,0},{1,9},{9,17},{17,25},{25,1},{2,10},{10... | collective-permute-start | bytes 61448 | tf_op jit(solution)/shard_map/ppermute | solution.py:18
  56.3 0.0 collective-permute-start.17
  56.3 0.6 fusion.1
  57.0 2.0 %gru_inner.1 = (bf16[3,3,96,128]{3,2,1,0:T(8,128)(2,1)}, f32[3,5,8,128]{3,2,1,0:T(8,128)S(1)}) custom-call(f32[8,128]{1,0:T(8,128)S(1)} %get-tuple-element.58.small, bf16[5,96,640]{2,1,0:T(8,128)(2,1)S(1)} %get-tuple-element.86.near, f32[3,3,96,128]{3,2,1,0:T(8,128)S(1)} %get-tuple-element.87.update_old, bf16[7,96,896]{2,1,0:T(8,128)(2,1)S(1)} %get-tuple-element.103.field, ...), custom_call_target="tpu_custom_call" | custom-call | flops 1000 | bytes 1000 | tf_op jit(solution)/shard_map/gru_inner/pallas_call | solution.py:69
  59.0 0.0 collective-permute-done.16.low
  59.0 0.9 %collective-permute-done.17.high = f32[1,5,8,128]{3,2,1,0:T(8,128)S(1)} collective-permute-done((f32[1,5,8,128]{3,2,1,0:T(8,128)S(1)}, f32[1,5,8,128]{3,2,1,0:T(8,128)S(1)}, u32[]{:S(2)}, u32[]{:S(2)}) %collective-permute-start.17) | collective-permute-done | bytes 20512 | tf_op jit(solution)/shard_map/ppermute | solution.py:18
  59.9 0.6 mix.1
  60.4 1.8 %collective-permute-start.18 = (f32[3,1,8,128]{3,2,1,0:T(8,128)S(1)}, f32[3,1,8,128]{3,2,1,0:T(8,128)S(1)}, u32[]{:S(2)}, u32[]{:S(2)}) collective-permute-start(f32[3,1,8,128]{3,2,1,0:T(8,128)S(1)} %get-tuple-element.112), channel_id=1, source_target_pairs={{0,1},{1,0},{2,3},{3,2},{4,5},{5,4},{6,7},{7,6},{8,9},{9,8},{10,11... | collective-permute-start | bytes 36872 | tf_op jit(solution)/shard_map/ppermute | solution.py:27
  62.3 2.8 %collective-permute-start.19 = (f32[3,1,8,128]{3,2,1,0:T(8,128)S(1)}, f32[3,1,8,128]{3,2,1,0:T(8,128)S(1)}, u32[]{:S(2)}, u32[]{:S(2)}) collective-permute-start(f32[3,1,8,128]{3,2,1,0:T(8,128)S(1)} %get-tuple-element.113), channel_id=1, source_target_pairs={{1,2},{2,1},{3,4},{4,3},{5,6},{6,5},{9,10},{10,9},{11,12},{12,11},... | collective-permute-start | bytes 36872 | tf_op jit(solution)/shard_map/ppermute | solution.py:32
  66.4 0.0 collective-permute-done.18
  66.4 0.9 %collective-permute-done.19 = f32[3,1,8,128]{3,2,1,0:T(8,128)S(1)} collective-permute-done((f32[3,1,8,128]{3,2,1,0:T(8,128)S(1)}, f32[3,1,8,128]{3,2,1,0:T(8,128)S(1)}, u32[]{:S(2)}, u32[]{:S(2)}) %collective-permute-start.19) | collective-permute-done | bytes 12320 | tf_op jit(solution)/shard_map/ppermute | solution.py:32
  67.3 0.7 %fusion = f32[3,3,3,128]{3,2,1,0:T(4,128)} fusion(f32[3,3,8,128]{3,2,1,0:T(8,128)S(1)} %get-tuple-element.111, f32[3,3,128]{2,1,0:T(4,128)S(1)} %slice.14, f32[3,3,128]{2,1,0:T(4,128)S(1)} %slice.12, pred[3]{0:T(512)(128)(4,1)S(1)} %get-tuple-element.118, pred[3]{0:T(512)(128)(4,1)S(1)} %get-tuple-element.119), kind=kLoop, calls=%fused_computation.1 | loop fusion | flops 13824 | bytes 36870 | tf_op jit(solution)/shard_map/add | solution.py:658
  (10 shorter events, 0.0 us)
Async XLA Ops:
  0.6 11.0 %collective-permute-start = (bf16[3,3,128,128]{3,2,1,0:T(8,128)(2,1)}, bf16[3,3,128,128]{3,2,1,0:T(8,128)(2,1)S(1)}, u32[]{:S(2)}, u32[]{:S(2)}) collective-permute-start(bf16[3,3,128,128]{3,2,1,0:T(8,128)(2,1)} %own.3), channel_id=1, source_target_pairs={{0,8},{8,16},{16,24},{24,0},{1,9},{9,17},{17,25},{25,1},{2,10},{10... | collective-permute-start | bytes 884744 | tf_op jit(solution)/shard_map/ppermute | solution.py:18
  1.9 15.9 %collective-permute-start.1 = (bf16[3,3,128,128]{3,2,1,0:T(8,128)(2,1)}, bf16[3,3,128,128]{3,2,1,0:T(8,128)(2,1)S(1)}, u32[]{:S(2)}, u32[]{:S(2)}) collective-permute-start(bf16[3,3,128,128]{3,2,1,0:T(8,128)(2,1)} %own.3), channel_id=1, source_target_pairs={{0,24},{8,0},{16,8},{24,16},{1,25},{9,1},{17,9},{25,17},{2,26},{10... | collective-permute-start | bytes 884744 | tf_op jit(solution)/shard_map/ppermute | solution.py:18
  2.2 15.7 %collective-permute-start.5 = (bf16[3,3,128,128]{3,2,1,0:T(8,128)(2,1)}, bf16[3,3,128,128]{3,2,1,0:T(8,128)(2,1)S(1)}, u32[]{:S(2)}, u32[]{:S(2)}) collective-permute-start(bf16[3,3,128,128]{3,2,1,0:T(8,128)(2,1)} %own.3), channel_id=1, source_target_pairs={{1,2},{2,1},{3,4},{4,3},{5,6},{6,5},{9,10},{10,9},{11,12},{12,11},... | collective-permute-start | bytes 884744 | tf_op jit(solution)/shard_map/ppermute | solution.py:32
  11.6 6.2 %copy-start.7 = (bf16[2,3,96,128]{3,2,1,0:T(8,128)(2,1)}, bf16[2,3,96,128]{3,2,1,0:T(8,128)(2,1)S(1)}, u32[]{:S(2)}) copy-start(bf16[2,3,96,128]{3,2,1,0:T(8,128)(2,1)S(1)} %get-tuple-element.69) | copy-start | bytes 442372
  11.6 9.5 %collective-permute-start.4 = (bf16[3,3,128,128]{3,2,1,0:T(8,128)(2,1)}, bf16[3,3,128,128]{3,2,1,0:T(8,128)(2,1)S(1)}, u32[]{:S(2)}, u32[]{:S(2)}) collective-permute-start(bf16[3,3,128,128]{3,2,1,0:T(8,128)(2,1)} %own.3), channel_id=1, source_target_pairs={{0,1},{1,0},{2,3},{3,2},{4,5},{5,4},{6,7},{7,6},{8,9},{9,8},{10,11... | collective-permute-start | bytes 884744 | tf_op jit(solution)/shard_map/ppermute | solution.py:27
  11.7 11.6 %collective-permute-start.6 = (bf16[3,3,128,128]{3,2,1,0:T(8,128)(2,1)S(1)}, bf16[3,3,128,128]{3,2,1,0:T(8,128)(2,1)S(1)}, u32[]{:S(2)}, u32[]{:S(2)}) collective-permute-start(bf16[3,3,128,128]{3,2,1,0:T(8,128)(2,1)S(1)} %collective-permute-done.low), channel_id=1, source_target_pairs={{0,1},{1,0},{2,3},{3,2},{4,5},{5,4},{6,7},{7,6},{8,9},{9,8},{10,11... | collective-permute-start | bytes 884744 | tf_op jit(solution)/shard_map/ppermute | solution.py:27
  12.2 14.2 %collective-permute-start.7 = (bf16[3,3,128,128]{3,2,1,0:T(8,128)(2,1)S(1)}, bf16[3,3,128,128]{3,2,1,0:T(8,128)(2,1)S(1)}, u32[]{:S(2)}, u32[]{:S(2)}) collective-permute-start(bf16[3,3,128,128]{3,2,1,0:T(8,128)(2,1)S(1)} %collective-permute-done.low), channel_id=1, source_target_pairs={{1,2},{2,1},{3,4},{4,3},{5,6},{6,5},{9,10},{10,9},{11,12},{12,11},... | collective-permute-start | bytes 884744 | tf_op jit(solution)/shard_map/ppermute | solution.py:32
  17.8 8.7 %collective-permute-start.8 = (bf16[3,3,128,128]{3,2,1,0:T(8,128)(2,1)S(1)}, bf16[3,3,128,128]{3,2,1,0:T(8,128)(2,1)S(1)}, u32[]{:S(2)}, u32[]{:S(2)}) collective-permute-start(bf16[3,3,128,128]{3,2,1,0:T(8,128)(2,1)S(1)} %collective-permute-done.1.high), channel_id=1, source_target_pairs={{0,1},{1,0},{2,3},{3,2},{4,5},{5,4},{6,7},{7,6},{8,9},{9,8},{10,11... | collective-permute-start | bytes 884744 | tf_op jit(solution)/shard_map/ppermute | solution.py:27
  17.8 8.6 %collective-permute-start.9 = (bf16[3,3,128,128]{3,2,1,0:T(8,128)(2,1)S(1)}, bf16[3,3,128,128]{3,2,1,0:T(8,128)(2,1)S(1)}, u32[]{:S(2)}, u32[]{:S(2)}) collective-permute-start(bf16[3,3,128,128]{3,2,1,0:T(8,128)(2,1)S(1)} %collective-permute-done.1.high), channel_id=1, source_target_pairs={{1,2},{2,1},{3,4},{4,3},{5,6},{6,5},{9,10},{10,9},{11,12},{12,11},... | collective-permute-start | bytes 884744 | tf_op jit(solution)/shard_map/ppermute | solution.py:32
  21.1 10.6 %collective-permute-start.2 = (bf16[2,3,96,128]{3,2,1,0:T(8,128)(2,1)}, bf16[2,3,96,128]{3,2,1,0:T(8,128)(2,1)S(1)}, u32[]{:S(2)}, u32[]{:S(2)}) collective-permute-start(bf16[2,3,96,128]{3,2,1,0:T(8,128)(2,1)} %copy-done.7), channel_id=1, source_target_pairs={{0,8},{8,16},{16,24},{24,0},{1,9},{9,17},{17,25},{25,1},{2,10},{10... | collective-permute-start | bytes 442376 | tf_op jit(solution)/shard_map/ppermute | solution.py:18
  23.3 8.5 %collective-permute-start.3 = (bf16[2,3,96,128]{3,2,1,0:T(8,128)(2,1)S(1)}, bf16[2,3,96,128]{3,2,1,0:T(8,128)(2,1)S(1)}, u32[]{:S(2)}, u32[]{:S(2)}) collective-permute-start(bf16[2,3,96,128]{3,2,1,0:T(8,128)(2,1)S(1)} %get-tuple-element.70), channel_id=1, source_target_pairs={{0,24},{8,0},{16,8},{24,16},{1,25},{9,1},{17,9},{25,17},{2,26},{10... | collective-permute-start | bytes 442376 | tf_op jit(solution)/shard_map/ppermute | solution.py:18
  29.3 14.0 %copy-start.4 = (bf16[288,896]{1,0:T(8,128)(2,1)S(1)}, bf16[288,896]{1,0:T(8,128)(2,1)}, u32[]{:S(2)}) copy-start(bf16[288,896]{1,0:T(8,128)(2,1)} %get-tuple-element.85.a_re) | copy-start | bytes 1548292
  29.3 14.0 %copy-start.5 = (bf16[288,896]{1,0:T(8,128)(2,1)S(1)}, bf16[288,896]{1,0:T(8,128)(2,1)}, u32[]{:S(2)}) copy-start(bf16[288,896]{1,0:T(8,128)(2,1)} %get-tuple-element.84.a_up) | copy-start | bytes 1548292
  29.3 9.9 %collective-permute-start.12 = (bf16[2,3,96,128]{3,2,1,0:T(8,128)(2,1)S(1)}, bf16[2,3,96,128]{3,2,1,0:T(8,128)(2,1)S(1)}, u32[]{:S(2)}, u32[]{:S(2)}) collective-permute-start(bf16[2,3,96,128]{3,2,1,0:T(8,128)(2,1)S(1)} %get-tuple-element.91), channel_id=1, source_target_pairs={{0,8},{8,16},{16,24},{24,0},{1,9},{9,17},{17,25},{25,1},{2,10},{10... | collective-permute-start | bytes 442376 | tf_op jit(solution)/shard_map/ppermute | solution.py:18
  31.8 7.5 %collective-permute-start.13 = (bf16[2,3,96,128]{3,2,1,0:T(8,128)(2,1)S(1)}, bf16[2,3,96,128]{3,2,1,0:T(8,128)(2,1)S(1)}, u32[]{:S(2)}, u32[]{:S(2)}) collective-permute-start(bf16[2,3,96,128]{3,2,1,0:T(8,128)(2,1)S(1)} %get-tuple-element.95), channel_id=1, source_target_pairs={{0,24},{8,0},{16,8},{24,16},{1,25},{9,1},{17,9},{25,17},{2,26},{10... | collective-permute-start | bytes 442376 | tf_op jit(solution)/shard_map/ppermute | solution.py:18
  32.4 10.9 %collective-permute-start.10 = (bf16[7,2,96,128]{3,2,1,0:T(8,128)(2,1)S(1)}, bf16[7,2,96,128]{3,2,1,0:T(8,128)(2,1)S(1)}, u32[]{:S(2)}, u32[]{:S(2)}) collective-permute-start(bf16[7,2,96,128]{3,2,1,0:T(8,128)(2,1)S(1)} %get-tuple-element.82), channel_id=1, source_target_pairs={{0,1},{1,0},{2,3},{3,2},{4,5},{5,4},{6,7},{7,6},{8,9},{9,8},{10,11... | collective-permute-start | bytes 1032200 | tf_op jit(solution)/shard_map/ppermute | solution.py:27
  32.5 10.8 %collective-permute-start.11 = (bf16[7,2,96,128]{3,2,1,0:T(8,128)(2,1)S(1)}, bf16[7,2,96,128]{3,2,1,0:T(8,128)(2,1)S(1)}, u32[]{:S(2)}, u32[]{:S(2)}) collective-permute-start(bf16[7,2,96,128]{3,2,1,0:T(8,128)(2,1)S(1)} %get-tuple-element.83), channel_id=1, source_target_pairs={{1,2},{2,1},{3,4},{4,3},{5,6},{6,5},{9,10},{10,9},{11,12},{12,11},... | collective-permute-start | bytes 1032200 | tf_op jit(solution)/shard_map/ppermute | solution.py:32
  39.9 9.2 %copy-start = (bf16[288,896]{1,0:T(8,128)(2,1)S(1)}, bf16[288,896]{1,0:T(8,128)(2,1)}, u32[]{:S(2)}) copy-start(bf16[288,896]{1,0:T(8,128)(2,1)} %get-tuple-element.98.a_up) | copy-start | bytes 1548292
  39.9 9.2 %copy-start.1 = (bf16[288,896]{1,0:T(8,128)(2,1)S(1)}, bf16[288,896]{1,0:T(8,128)(2,1)}, u32[]{:S(2)}) copy-start(bf16[288,896]{1,0:T(8,128)(2,1)} %get-tuple-element.100.a_ca_old) | copy-start | bytes 1548292
  39.9 9.2 %copy-start.2 = (bf16[288,896]{1,0:T(8,128)(2,1)S(1)}, bf16[288,896]{1,0:T(8,128)(2,1)}, u32[]{:S(2)}) copy-start(bf16[288,896]{1,0:T(8,128)(2,1)} %get-tuple-element.101.a_ca_new) | copy-start | bytes 1548292
  39.9 9.2 %copy-start.3 = (bf16[288,896]{1,0:T(8,128)(2,1)S(1)}, bf16[288,896]{1,0:T(8,128)(2,1)}, u32[]{:S(2)}) copy-start(bf16[288,896]{1,0:T(8,128)(2,1)} %get-tuple-element.99.a_re) | copy-start | bytes 1548292
  39.9 9.2 %copy-start.6 = (bf16[256,96]{1,0:T(8,128)(2,1)S(1)}, bf16[256,96]{1,0:T(8,128)(2,1)}, u32[]{:S(2)}) copy-start(bf16[256,96]{1,0:T(8,128)(2,1)} %get-tuple-element.102.head) | copy-start | bytes 147460
  39.9 7.4 %collective-permute-start.14 = (bf16[7,2,96,128]{3,2,1,0:T(8,128)(2,1)S(1)}, bf16[7,2,96,128]{3,2,1,0:T(8,128)(2,1)S(1)}, u32[]{:S(2)}, u32[]{:S(2)}) collective-permute-start(bf16[7,2,96,128]{3,2,1,0:T(8,128)(2,1)S(1)} %get-tuple-element.96), channel_id=1, source_target_pairs={{0,1},{1,0},{2,3},{3,2},{4,5},{5,4},{6,7},{7,6},{8,9},{9,8},{10,11... | collective-permute-start | bytes 1032200 | tf_op jit(solution)/shard_map/ppermute | solution.py:27
  40.4 8.7 %collective-permute-start.15 = (bf16[7,2,96,128]{3,2,1,0:T(8,128)(2,1)S(1)}, bf16[7,2,96,128]{3,2,1,0:T(8,128)(2,1)S(1)}, u32[]{:S(2)}, u32[]{:S(2)}) collective-permute-start(bf16[7,2,96,128]{3,2,1,0:T(8,128)(2,1)S(1)} %get-tuple-element.97), channel_id=1, source_target_pairs={{1,2},{2,1},{3,4},{4,3},{5,6},{6,5},{9,10},{10,9},{11,12},{12,11},... | collective-permute-start | bytes 1032200 | tf_op jit(solution)/shard_map/ppermute | solution.py:32
  54.0 4.9 %collective-permute-start.16 = (f32[1,5,8,128]{3,2,1,0:T(8,128)S(1)}, f32[1,5,8,128]{3,2,1,0:T(8,128)S(1)}, u32[]{:S(2)}, u32[]{:S(2)}) collective-permute-start(f32[1,5,8,128]{3,2,1,0:T(8,128)S(1)} %get-tuple-element.109), channel_id=1, source_target_pairs={{0,8},{8,16},{16,24},{24,0},{1,9},{9,17},{17,25},{25,1},{2,10},{10... | collective-permute-start | bytes 61448 | tf_op jit(solution)/shard_map/ppermute | solution.py:18
  56.3 3.5 %collective-permute-start.17 = (f32[1,5,8,128]{3,2,1,0:T(8,128)S(1)}, f32[1,5,8,128]{3,2,1,0:T(8,128)S(1)}, u32[]{:S(2)}, u32[]{:S(2)}) collective-permute-start(f32[1,5,8,128]{3,2,1,0:T(8,128)S(1)} %get-tuple-element.110), channel_id=1, source_target_pairs={{0,24},{8,0},{16,8},{24,16},{1,25},{9,1},{17,9},{25,17},{2,26},{10... | collective-permute-start | bytes 61448 | tf_op jit(solution)/shard_map/ppermute | solution.py:18
  60.4 5.9 %collective-permute-start.18 = (f32[3,1,8,128]{3,2,1,0:T(8,128)S(1)}, f32[3,1,8,128]{3,2,1,0:T(8,128)S(1)}, u32[]{:S(2)}, u32[]{:S(2)}) collective-permute-start(f32[3,1,8,128]{3,2,1,0:T(8,128)S(1)} %get-tuple-element.112), channel_id=1, source_target_pairs={{0,1},{1,0},{2,3},{3,2},{4,5},{5,4},{6,7},{7,6},{8,9},{9,8},{10,11... | collective-permute-start | bytes 36872 | tf_op jit(solution)/shard_map/ppermute | solution.py:27
  62.3 5.0 %collective-permute-start.19 = (f32[3,1,8,128]{3,2,1,0:T(8,128)S(1)}, f32[3,1,8,128]{3,2,1,0:T(8,128)S(1)}, u32[]{:S(2)}, u32[]{:S(2)}) collective-permute-start(f32[3,1,8,128]{3,2,1,0:T(8,128)S(1)} %get-tuple-element.113), channel_id=1, source_target_pairs={{1,2},{2,1},{3,4},{4,3},{5,6},{6,5},{9,10},{10,9},{11,12},{12,11},... | collective-permute-start | bytes 36872 | tf_op jit(solution)/shard_map/ppermute | solution.py:32
